TPU v7x, 512 devices: a whole 4x8x8 slice. The times are simulated.
512 devices in a mesh: bond: 16 (over x, y_lo, core), site: 32 (over y_hi, z).
Axes of the slice: x: 4, y: 8 (y_hi: 4, y_lo: 2; y = y_hi * 2 + y_lo), z: 8, core: 2. Of those that a mesh axis runs over, the one named last changes fastest.
Arguments:
- two_site: float32 [32, 4096, 2048], P('site', None, 'bond')
- keep_list: int32 [32, 1024], P('site', 'bond'), may hold values from 0 to 127, as said below
- owner_map: int32 [32, 1024, 1], P('site', 'bond'), may hold values from 0 to 31; in each aligned block of 64 rows (0 to 63, 64 to 127, ..., all dimensions but the last counted through in order) at most 4 rows name the same one
Outputs:
- arrivals: float32 [32, 16, 32, 4, 4096], P('site', 'bond')
Inputs may be any that keep to these rules, and one draw needn't show every extreme that they name: `keep_list`: the 64 entries of one block are distinct column numbers of that block. `owner_map`: among the 64 kept columns of one block at most 4 go to one owner, and some owner gets exactly 4.
All inputs are finite; a program needn't handle non-finite values.
Results may differ from a plain program's by a relative error of at most 0.00011.
Values sent between devices are 32-bit elements; how exact they have to be, the bound alone decides.
No kernel may reach another device: no remote copies, remote signals or barrier semaphores. Data moves between devices by JAX's collectives and lax.ppermute only.
A program may use at most 64 MiB of HBM per device.

v0:
```python
import jax
import jax.numpy as jnp
from jax import lax
from jax.experimental import pallas as pl
from jax.experimental.pallas import tpu as pltpu
from jax.sharding import PartitionSpec as P

NS_STEPS = 5
LANES = 128
F32 = jnp.float32
BF16 = jnp.bfloat16

NN = ((1,), (0,))
NT = ((1,), (1,))
TN = ((0,), (0,))


def split(value):
    high = value.astype(BF16)
    return high, (value - high.astype(F32)).astype(BF16)


def dot(left, right, contract):
    return lax.dot_general(left, right, (contract, ((), ())), preferred_element_type=F32)


def product(left, right, contract):
    return dot(left[0], right[0], contract) + (
        dot(left[0], right[1], contract) + dot(left[1], right[0], contract)
    )


def gram_kernel(own_ref, next_ref, top_ref, bottom_ref):
    half = own_ref.shape[1]
    pair = split(jnp.concatenate([own_ref[...], next_ref[...]], 1))
    gram = product(pair, pair, TN)

    @pl.when(pl.program_id(0) == 0)
    def _():
        top_ref[...] = gram[:half]
        bottom_ref[...] = gram[half:]

    @pl.when(pl.program_id(0) > 0)
    def _():
        top_ref[...] += gram[:half]
        bottom_ref[...] += gram[half:]


def pair_gram(own, neighbour, steps):
    rows, width = own.shape
    tile = rows // steps
    shape = jax.ShapeDtypeStruct((width, 2 * width), F32)
    rows_in = pl.BlockSpec((tile, width), lambda i: (i, 0))
    whole = pl.BlockSpec((width, 2 * width), lambda i: (0, 0))
    return pl.pallas_call(
        gram_kernel,
        grid=(steps,),
        in_specs=[rows_in, rows_in],
        out_specs=[whole, whole],
        out_shape=[shape, shape],
        name="pair_gram",
    )(own, neighbour)


def cross_kernel(place_ref, own_ref, next_ref, far_ref, next_far_ref, before_ref, out_ref):
    here = split(jnp.concatenate([own_ref[...], next_ref[...]], 1))
    there = split(jnp.concatenate([far_ref[...], next_far_ref[...]], 1))
    gram = product(here, there, TN)

    @pl.when(pl.program_id(0) == 0)
    def _():
        out_ref[...] = before_ref[...] + gram

    @pl.when(pl.program_id(0) > 0)
    def _():
        out_ref[...] += gram


def cross_gram(place, own, neighbour, far, next_far, before, start, steps):
    rows, width = far.shape
    tile = rows // steps
    half = own.shape[0] // 2
    first = start // tile
    mine = pl.BlockSpec((tile, width), lambda i, place: (place[0] * (half // tile) + first + i, 0))
    rows_in = pl.BlockSpec((tile, width), lambda i, place: (i, 0))
    whole = pl.BlockSpec((2 * width, 2 * width), lambda i, place: (0, 0))
    return pl.pallas_call(
        cross_kernel,
        grid_spec=pltpu.PrefetchScalarGridSpec(
            num_scalar_prefetch=1,
            grid=(steps,),
            in_specs=[mine, mine, rows_in, rows_in, whole],
            out_specs=whole,
        ),
        out_shape=jax.ShapeDtypeStruct((2 * width, 2 * width), F32),
        name="cross_gram",
    )(place, own, neighbour, far, next_far, before)


def rotations(grams, sign):
    width = grams[0].shape[0]
    half = width // 2
    row = lax.broadcasted_iota(jnp.int32, (width, width), 0)
    column = lax.broadcasted_iota(jnp.int32, (width, width), 1)
    diagonal = (row == column).astype(F32)
    order = jnp.where(row < column, 0.5, -0.5) * (1.0 - diagonal)
    order = jnp.where((row < half) == (column < half), order, order * sign)
    iterates = []
    for gram in grams:
        inverse_row = 1.0 / jnp.sqrt(jnp.sum(gram * diagonal, axis=0, keepdims=True))
        inverse_column = 1.0 / jnp.sqrt(jnp.sum(gram * diagonal, axis=1, keepdims=True))
        skew = gram * inverse_column * inverse_row * order
        iterates.append((diagonal + skew) / jnp.sqrt(1.0 + jnp.sum(skew * skew)))
    for step in range(NS_STEPS):
        parts = [split(iterate) for iterate in iterates]
        squares = [product(part, part, NT) for part in parts]
        rests = [0.5 * (diagonal - square) for square in squares]
        iterates = [
            iterate + product(part, split(rest), NN)
            for iterate, part, rest in zip(iterates, parts, rests)
        ]
    return iterates


def symmetric(first, cross, second):
    return jnp.concatenate(
        [jnp.concatenate([first, cross], 1), jnp.concatenate([cross.T, second], 1)], 0
    )


def turn_kernel(
    place_ref, top_ref, bottom_ref, far_top_ref, far_bottom_ref, cross_ref, far_cross_ref, route_ref, kept_ref,
    block_ref, next_ref, far_a_ref, far_b_ref, next_far_a_ref, next_far_b_ref,
    out_ref, norm_ref, rows_ref, sems,
):
    rows, width = rows_ref.shape[1:]
    part = rows // 2
    upper, right = place_ref[0], place_ref[1]
    start = pl.multiple_of(upper * rows, rows)
    copies = [
        pltpu.make_async_copy(source, target, sems.at[number])
        for number, (source, target) in enumerate(
            [
                (block_ref.at[pl.ds(start, rows)], rows_ref.at[0]),
                (next_ref.at[pl.ds(start, rows)], rows_ref.at[2]),
                (far_a_ref, rows_ref.at[1, :part]),
                (far_b_ref, rows_ref.at[1, part:]),
                (next_far_a_ref, rows_ref.at[3, :part]),
                (next_far_b_ref, rows_ref.at[3, part:]),
            ]
        )
    ]
    for copy in copies:
        copy.start()
    sign_far = jnp.where(upper == 0, 1.0, -1.0)
    sign_next = jnp.where(right == 0, 1.0, -1.0)

    cross = cross_ref[...] + far_cross_ref[...].T
    top, bottom, far_top, far_bottom = top_ref[...], bottom_ref[...], far_top_ref[...], far_bottom_ref[...]
    lo, hi = slice(0, width), slice(width, 2 * width)
    gram_01 = symmetric(top[:, lo], cross[lo, lo], far_top[:, lo])
    gram_23 = symmetric(bottom[:, hi], cross[hi, hi], far_bottom[:, lo])
    mixed = jnp.concatenate(
        [
            jnp.concatenate([top[:, hi], cross[lo, hi]], 1),
            jnp.concatenate([cross[hi, lo].T, far_top[:, hi]], 1),
        ],
        0,
    )
    turn_01, turn_23 = rotations([gram_01, gram_23], sign_far)
    s_01, s_23 = split(turn_01), split(turn_23)
    s_01t, s_23t = split(turn_01.T), split(turn_23.T)
    half_01 = split(product(split(gram_01), s_01, NN))
    half_23 = split(product(split(gram_23), s_23, NN))
    half_mixed = split(product(split(mixed), s_23, NN))

    def corner(left, right, which):
        return product(
            (left[0][which], left[1][which]), (right[0][:, which], right[1][:, which]), NN
        )

    grams = [
        symmetric(corner(s_01t, half_01, w), corner(s_01t, half_mixed, w), corner(s_23t, half_23, w))
        for w in (lo, hi)
    ]
    seconds = rotations(grams, sign_next)

    total = jnp.zeros((1, 1), F32)
    routed = [0.0, 0.0]
    for number, (gram, second, which) in enumerate(zip(grams, seconds, (lo, hi))):
        parts = split(second)
        moved = product(split(gram), parts, NN) * second
        kept = jnp.concatenate([kept_ref[number : number + 1], kept_ref[number + 2 : number + 3]], 1)
        total += jnp.sum(jnp.sum(moved, axis=0, keepdims=True) * kept, axis=1, keepdims=True)
        turned = jnp.concatenate(
            [
                product([p[:, which] for p in s_01], [p[lo, lo] for p in parts], NN),
                product([p[:, which] for p in s_23], [p[hi, lo] for p in parts], NN),
            ],
            0,
        )
        route = route_ref[number].astype(BF16)
        routed = [into + dot(piece, route, NN) for into, piece in zip(routed, split(turned))]
    norm_ref[...] = jnp.broadcast_to(total, norm_ref.shape)

    placed = [piece.T.astype(BF16) for piece in routed]
    left = [piece[:, : 2 * width] for piece in placed]
    right_side = [piece[:, 2 * width :] for piece in placed]
    for copy in copies:
        copy.wait()
    chunk = min(512, rows)
    for begin in range(0, rows, chunk):
        span = slice(begin, begin + chunk)
        near = split(jnp.concatenate([rows_ref[0, span], rows_ref[1, span]], 1))
        far = split(jnp.concatenate([rows_ref[2, span], rows_ref[3, span]], 1))
        out_ref[:, span] = product(left, near, NT) + product(right_side, far, NT)


def turn(place, grams, routes, kept, blocks):
    rows, width = blocks[0].shape
    rows = rows // 2
    vmem = pl.BlockSpec(memory_space=pltpu.VMEM)
    anywhere = pl.BlockSpec(memory_space=pl.ANY)
    return pl.pallas_call(
        turn_kernel,
        in_specs=[pl.BlockSpec(memory_space=pltpu.SMEM)] + [vmem] * 8 + [anywhere] * 6,
        out_specs=[vmem, vmem],
        out_shape=[
            jax.ShapeDtypeStruct((2 * width, rows), F32),
            jax.ShapeDtypeStruct((8, width), F32),
        ],
        scratch_shapes=[pltpu.VMEM((4, rows, width), F32), pltpu.SemaphoreType.DMA((6,))],
        compiler_params=pltpu.CompilerParams(vmem_limit_bytes=40 * 1024 * 1024),
        name="turn",
    )(place, *grams, routes, kept, *blocks)


def from_partner(value, axis, distance):
    pairs = [(source, source ^ distance) for source in range(lax.axis_size(axis))]
    return lax.ppermute(value, axis, pairs)


def route_of(listed, side, groups, width):
    keep, owners = listed[0], listed[1]
    kept = keep.shape[0]
    order = jnp.arange(kept, dtype=jnp.int32)
    same = owners[:, None] == owners[None, :]
    slot = jnp.sum((same & (order[None, :] < order[:, None])).astype(jnp.int32), axis=1)
    capacity = max(2, 2 * kept // groups)
    target = (owners * 2 + side) * capacity + slot
    places = jnp.arange(2 * groups * capacity, dtype=jnp.int32)
    columns = jnp.arange(width, dtype=jnp.int32)
    picked = (keep[:, None] == columns[None, :]).astype(BF16)
    placed = (target[:, None] == places[None, :]).astype(BF16)
    return lax.dot_general(picked, placed, (TN, ((), ())), preferred_element_type=F32)


def on_device(two_site, keep_list, owner_map):
    block = two_site[0]
    rows, width = block.shape
    half, quarter = rows // 2, rows // 4
    count, groups = lax.axis_size("bond"), lax.axis_size("site")
    far = count // 2
    position = lax.axis_index("bond")
    upper = position // far
    place = jnp.stack([upper, position & 1]).astype(jnp.int32)

    start = (1 - upper) * half
    far_a = from_partner(lax.dynamic_slice_in_dim(block, start, quarter), "bond", far)
    far_b = from_partner(lax.dynamic_slice_in_dim(block, start + quarter, quarter), "bond", far)
    neighbour = from_partner(block, "bond", 1)
    listed = jnp.stack([keep_list[0], owner_map[0, :, 0]])
    listed = jnp.concatenate([listed, from_partner(listed, "bond", far)])
    routes = jnp.stack(
        [
            route_of(listed[:2], upper, groups, width),
            route_of(listed[2:], 1 - upper, groups, width),
        ]
    )
    lists = jnp.concatenate([listed[::2], from_partner(listed[::2], "bond", 1)])
    columns = jnp.arange(width, dtype=jnp.int32)
    kept = jnp.sum((lists[:, :, None] == columns).astype(F32), axis=1)

    top, bottom = pair_gram(block, neighbour, 4)
    far_top = from_partner(top, "bond", far)
    next_far_a = from_partner(far_a, "bond", 1)
    far_bottom = from_partner(far_top, "bond", 1)
    next_far_b = from_partner(far_b, "bond", 1)
    cross = jnp.zeros((2 * width, 2 * width), F32)
    cross = cross_gram(place, block, neighbour, far_a, next_far_a, cross, 0, 2)
    cross = cross_gram(place, block, neighbour, far_b, next_far_b, cross, quarter, 2)
    far_cross = from_partner(cross, "bond", far)

    outgoing, squares = turn(
        place,
        (top, bottom, far_top, far_bottom, cross, far_cross),
        routes,
        kept,
        (block, neighbour, far_a, far_b, next_far_a, next_far_b),
    )
    for distance in [1 << bit for bit in range(1, far.bit_length() - 1)]:
        squares = squares + from_partner(squares, "bond", distance)
    keep_count = keep_list.shape[1]
    scale = jnp.sqrt(rows * count * keep_count / squares[0, 0])
    capacity = max(2, 2 * keep_count // groups)
    members = [
        [(first + far * side) * groups + site for site in range(groups) for side in range(2)]
        for first in range(far)
    ]
    outgoing = (outgoing * scale).reshape(2 * groups, capacity, half // LANES, LANES)
    arrived = lax.all_to_all(
        outgoing.transpose(0, 2, 1, 3),
        ("bond", "site"),
        split_axis=0,
        concat_axis=0,
        tiled=True,
        axis_index_groups=members,
    )
    arrived = arrived.reshape(groups, rows // LANES, capacity, LANES).transpose(0, 2, 1, 3)
    return arrived.reshape(1, 1, groups, capacity, rows)


def solution(mesh):
    return jax.shard_map(
        on_device,
        mesh=mesh,
        in_specs=(P("site", None, "bond"), P("site", "bond"), P("site", "bond", None)),
        out_specs=P("site", "bond", None, None, None),
        check_vma=False,
    )
```

profile of v0, /device:TPU:56, one launch (start us, length us, event | category | flops | bytes accessed | tf_op | source)
XLA Modules:
  0.0 177.4 jit_solution(9019873996354892231)
XLA Ops:
  0.0 2.0 %collective-permute-start = (f32[4096,128]{1,0:T(8,128)}, f32[4096,128]{1,0:T(8,128)S(1)}, u32[]{:S(2)}, u32[]{:S(2)}) collective-permute-start(f32[4096,128]{1,0:T(8,128)} %bitcast.35), channel_id=1, source_target_pairs={{0,32},{32,0},{64,96},{96,64},{128,160},{160,128},{192,224},{224,1... | collective-permute-start | bytes 6291464 | tf_op jit(solution)/shard_map/ppermute | solution.py:240
  2.1 0.7 pad_add_fusion.2
  2.7 4.9 %collective-permute-start.8 = (s32[2,64]{1,0:T(2,128)S(1)}, s32[2,64]{1,0:T(2,128)S(1)}, u32[]{:S(2)}, u32[]{:S(2)}) collective-permute-start(s32[2,64]{1,0:T(2,128)S(1)} %pad_add_fusion.2), channel_id=1, source_target_pairs={{0,256},{32,288},{64,320},{96,352},{128,384},{160,416},{192,448},{... | collective-permute-start | bytes 1544 | tf_op jit(solution)/shard_map/ppermute | solution.py:240
  7.7 2.2 %dynamic-slice_bitcast_fusion = (f32[1024,128]{1,0:T(8,128)}, f32[1024,128]{1,0:T(8,128)}) fusion(f32[1,4096,128]{2,1,0:T(8,128)} %param.3, s32[]{:T(128)S(6)} %select_n.13, s32[]{:T(128)S(6)} %select_n.12), kind=kLoop, calls=%fused_computation.3 | loop fusion | bytes 2097160 | tf_op jit(solution)/shard_map/dynamic_slice | solution.py:269
  9.9 2.4 %collective-permute-start.5 = (f32[1024,128]{1,0:T(8,128)}, f32[1024,128]{1,0:T(8,128)S(1)}, u32[]{:S(2)}, u32[]{:S(2)}) collective-permute-start(f32[1024,128]{1,0:T(8,128)} %get-tuple-element.13), channel_id=1, source_target_pairs={{0,256},{32,288},{64,320},{96,352},{128,384},{160,416},{192,448},{... | collective-permute-start | bytes 1572872 | tf_op jit(solution)/shard_map/ppermute | solution.py:240
  12.3 4.9 %collective-permute-start.3 = (f32[1024,128]{1,0:T(8,128)}, f32[1024,128]{1,0:T(8,128)S(1)}, u32[]{:S(2)}, u32[]{:S(2)}) collective-permute-start(f32[1024,128]{1,0:T(8,128)} %get-tuple-element.14), channel_id=1, source_target_pairs={{0,256},{32,288},{64,320},{96,352},{128,384},{160,416},{192,448},{... | collective-permute-start | bytes 1572872 | tf_op jit(solution)/shard_map/ppermute | solution.py:240
  17.3 0.2 convert_reduce_fusion.2
  17.5 0.9 convolution_bitcast_fusion.1
  18.4 0.7 pad_add_fusion.3.place_ref
  19.1 0.0 collective-permute-done.8
  19.1 1.9 %collective-permute-start.9 = (s32[2,64]{1,0:T(2,128)S(1)}, s32[2,64]{1,0:T(2,128)S(1)}, u32[]{:S(2)}, u32[]{:S(2)}) collective-permute-start(s32[2,64]{1,0:T(2,128)S(1)} %slice.15), channel_id=1, source_target_pairs={{0,32},{32,0},{64,96},{96,64},{128,160},{160,128},{192,224},{224,1... | collective-permute-start | bytes 1544 | tf_op jit(solution)/shard_map/ppermute | solution.py:240
  21.1 7.2 %collective-permute-done.5.far_ref.far_a_ref = f32[1024,128]{1,0:T(8,128)S(1)} collective-permute-done((f32[1024,128]{1,0:T(8,128)}, f32[1024,128]{1,0:T(8,128)S(1)}, u32[]{:S(2)}, u32[]{:S(2)}) %collective-permute-start.5) | collective-permute-done | bytes 524320 | tf_op jit(solution)/shard_map/ppermute | solution.py:240
  28.3 1.9 %collective-permute-start.6 = (f32[1024,128]{1,0:T(8,128)S(1)}, f32[1024,128]{1,0:T(8,128)}, u32[]{:S(2)}, u32[]{:S(2)}) collective-permute-start(f32[1024,128]{1,0:T(8,128)S(1)} %collective-permute-done.5.far_ref.far_a_ref), channel_id=1, source_target_pairs={{0,32},{32,0},{64,96},{96,64},{128,160},{160,128},{192,224},{224,1... | collective-permute-start | bytes 1572872 | tf_op jit(solution)/shard_map/ppermute | solution.py:240
  30.2 8.6 %collective-permute-done.3.far_ref.far_b_ref = f32[1024,128]{1,0:T(8,128)S(1)} collective-permute-done((f32[1024,128]{1,0:T(8,128)}, f32[1024,128]{1,0:T(8,128)S(1)}, u32[]{:S(2)}, u32[]{:S(2)}) %collective-permute-start.3) | collective-permute-done | bytes 524320 | tf_op jit(solution)/shard_map/ppermute | solution.py:240
  38.8 1.9 %collective-permute-start.4 = (f32[1024,128]{1,0:T(8,128)S(1)}, f32[1024,128]{1,0:T(8,128)}, u32[]{:S(2)}, u32[]{:S(2)}) collective-permute-start(f32[1024,128]{1,0:T(8,128)S(1)} %collective-permute-done.3.far_ref.far_b_ref), channel_id=1, source_target_pairs={{0,32},{32,0},{64,96},{96,64},{128,160},{160,128},{192,224},{224,1... | collective-permute-start | bytes 1572872 | tf_op jit(solution)/shard_map/ppermute | solution.py:240
  40.7 0.2 convert_reduce_fusion.1
  40.9 0.0 collective-permute-done.next_ref
  40.9 0.0 copy-start.1
  41.0 1.3 copy-done.1
  42.3 5.2 %pair_gram.1 = (f32[128,256]{1,0:T(8,128)}, f32[128,256]{1,0:T(8,128)}) custom-call(f32[4096,128]{1,0:T(8,128)} %bitcast.36, f32[4096,128]{1,0:T(8,128)} %copy-done.1), custom_call_target="tpu_custom_call" | custom-call | tf_op jit(solution)/shard_map/pair_gram/pallas_call | solution.py:55
  47.5 2.4 %collective-permute-start.1 = (f32[128,256]{1,0:T(8,128)}, f32[128,256]{1,0:T(8,128)S(1)}, u32[]{:S(2)}, u32[]{:S(2)}) collective-permute-start(f32[128,256]{1,0:T(8,128)} %get-tuple-element.9.top_ref), channel_id=1, source_target_pairs={{0,256},{32,288},{64,320},{96,352},{128,384},{160,416},{192,448},{... | collective-permute-start | bytes 393224 | tf_op jit(solution)/shard_map/ppermute | solution.py:240
  49.9 0.9 convolution_bitcast_fusion
  50.8 0.0 collective-permute-done.6.next_far_ref.next_far_a_ref
  50.8 0.7 broadcast_in_dim.2.before_ref
  51.5 3.7 %cross_gram.2.before_ref = f32[256,256]{1,0:T(8,128)} custom-call(s32[2]{0:T(128)} %pad_add_fusion.3.place_ref, f32[4096,128]{1,0:T(8,128)} %bitcast.37, f32[4096,128]{1,0:T(8,128)} %copy-done.1, f32[1024,128]{1,0:T(8,128)} %copy-done.3, f32[1024,128]{1,0:T(8,128)} %collective-permute-done.6.next_far_ref.next_far_a_ref, f32[256,256]{1,0:T(8,128)} %broadcast_in_dim.2.before_ref), custom_call_target="tpu_custom_call" | custom-call | tf_op jit(solution)/shard_map/cross_gram/pallas_call | solution.py:87
  55.2 3.8 %cross_gram.3.cross_ref = f32[256,256]{1,0:T(8,128)} custom-call(s32[2]{0:T(128)} %pad_add_fusion.3.place_ref, f32[4096,128]{1,0:T(8,128)} %bitcast.38, f32[4096,128]{1,0:T(8,128)} %copy-done.1, f32[1024,128]{1,0:T(8,128)} %copy-done.5, f32[1024,128]{1,0:T(8,128)} %collective-permute-done.4.next_far_ref.next_far_b_ref, f32[256,256]{1,0:T(8,128)} %cross_gram.2.before_ref), custom_call_target="tpu_custom_call" | custom-call | tf_op jit(solution)/shard_map/cross_gram/pallas_call | solution.py:87
  59.1 4.9 %collective-permute-start.7 = (f32[256,256]{1,0:T(8,128)}, f32[256,256]{1,0:T(8,128)S(1)}, u32[]{:S(2)}, u32[]{:S(2)}) collective-permute-start(f32[256,256]{1,0:T(8,128)} %cross_gram.3.cross_ref), channel_id=1, source_target_pairs={{0,256},{32,288},{64,320},{96,352},{128,384},{160,416},{192,448},{... | collective-permute-start | bytes 786440 | tf_op jit(solution)/shard_map/ppermute | solution.py:240
  64.0 1.0 pad_maximum_fusion.route_ref
  65.0 2.1 %collective-permute-start.2 = (f32[128,256]{1,0:T(8,128)S(1)}, f32[128,256]{1,0:T(8,128)S(1)}, u32[]{:S(2)}, u32[]{:S(2)}) collective-permute-start(f32[128,256]{1,0:T(8,128)S(1)} %collective-permute-done.1.far_top_ref), channel_id=1, source_target_pairs={{0,32},{32,0},{64,96},{96,64},{128,160},{160,128},{192,224},{224,1... | collective-permute-start | bytes 393224 | tf_op jit(solution)/shard_map/ppermute | solution.py:240
  67.1 0.0 collective-permute-done.9
  67.1 0.1 convert_reduce_fusion.kept_ref
  67.2 3.8 %collective-permute-done.7.far_cross_ref = f32[256,256]{1,0:T(8,128)S(1)} collective-permute-done((f32[256,256]{1,0:T(8,128)}, f32[256,256]{1,0:T(8,128)S(1)}, u32[]{:S(2)}, u32[]{:S(2)}) %collective-permute-start.7) | collective-permute-done | bytes 262176 | tf_op jit(solution)/shard_map/ppermute | solution.py:240
  71.1 0.0 copy-start.2
  71.1 1.6 copy-done.2
  72.7 1.0 copy-done.6
  73.8 0.9 copy-done.7
  74.7 12.9 %turn.1 = (f32[256,2048]{1,0:T(8,128)S(1)}, f32[8,128]{1,0:T(8,128)S(1)}) custom-call(s32[2]{0:T(128)S(1)} %copy-done.10, f32[128,256]{1,0:T(8,128)S(1)} %copy-done.8, f32[128,256]{1,0:T(8,128)S(1)} %copy-done.9, f32[128,256]{1,0:T(8,128)S(1)} %collective-permute-done.1.far_top_ref, f32[128,256]{1,0:T(8,128)S(1)} %collective-permute-done.2.far_bottom_ref, ...), custom_call_target="tpu_custom_call" | custom-call | tf_op jit(solution)/shard_map/turn/pallas_call | solution.py:224
  87.6 3.2 %collective-permute-start.10 = (f32[8,128]{1,0:T(8,128)S(1)}, f32[8,128]{1,0:T(8,128)S(1)}, u32[]{:S(2)}, u32[]{:S(2)}) collective-permute-start(f32[8,128]{1,0:T(8,128)S(1)} %get-tuple-element.12), channel_id=1, source_target_pairs={{0,64},{32,96},{64,0},{96,32},{128,192},{160,224},{192,128},{224,1... | collective-permute-start | bytes 12296 | tf_op jit(solution)/shard_map/ppermute | solution.py:240
  90.9 2.2 %collective-permute-done.10 = f32[8,128]{1,0:T(8,128)S(1)} collective-permute-done((f32[8,128]{1,0:T(8,128)S(1)}, f32[8,128]{1,0:T(8,128)S(1)}, u32[]{:S(2)}, u32[]{:S(2)}) %collective-permute-start.10) | collective-permute-done | bytes 4128 | tf_op jit(solution)/shard_map/ppermute | solution.py:240
  93.1 3.4 %collective-permute-start.11 = (f32[8,128]{1,0:T(8,128)S(1)}, f32[8,128]{1,0:T(8,128)S(1)}, u32[]{:S(2)}, u32[]{:S(2)}) collective-permute-start(f32[8,128]{1,0:T(8,128)S(1)} %add.61), channel_id=1, source_target_pairs={{0,128},{32,160},{64,192},{96,224},{128,0},{160,32},{192,64},{224,... | collective-permute-start | bytes 12296 | tf_op jit(solution)/shard_map/ppermute | solution.py:240
  96.5 2.1 %collective-permute-done.11 = f32[8,128]{1,0:T(8,128)S(1)} collective-permute-done((f32[8,128]{1,0:T(8,128)S(1)}, f32[8,128]{1,0:T(8,128)S(1)}, u32[]{:S(2)}, u32[]{:S(2)}) %collective-permute-start.11) | collective-permute-done | bytes 4128 | tf_op jit(solution)/shard_map/ppermute | solution.py:240
  98.6 0.5 slice.16
  99.9 0.1 multiply_bitcast_fusion
  100.0 0.4 copy.10
  100.4 71.0 %all_to_all.5 = f32[64,16,4,128]{3,1,2,0:T(8,128)S(1)} all-to-all(f32[64,16,4,128]{3,1,2,0:T(8,128)S(1)} %bitcast.40), channel_id=1, replica_groups={{0,256,1,257,2,258,3,259,4,260,5,261,6,262,7,263,8,264,9,265,10,266,11,..., dimensions={0} | all-to-all | bytes 4194304 | tf_op jit(solution)/shard_map/all_to_all | solution.py:311
  171.4 0.2 copy.8
  171.5 1.5 reshape.42
  173.1 4.3 %copy.9 = f32[1,1,32,4,4096]{4,3,2,1,0:T(4,128)} copy(f32[1,1,32,4,4096]{4,2,3,1,0:T(8,128)} %reshape.42) | data formatting | bytes 4194304 | tf_op jit(solution)/shard_map/reshape | solution.py:320
  (31 shorter events, 0.1 us)
Async XLA Ops:
  0.0 17.5 %copy-start.11 = (s32[1,64]{1,0:T(1,128)S(1)}, s32[1,64]{1,0:T(1,128)}, u32[]{:S(2)}) copy-start(s32[1,64]{1,0:T(1,128)} %param.4) | copy-start | bytes 772
  0.0 17.3 %copy-start.12 = (s32[1,64,1]{1,2,0:T(1,128)S(1)}, s32[1,64,1]{1,2,0:T(1,128)}, u32[]{:S(2)}) copy-start(s32[1,64,1]{1,2,0:T(1,128)} %param.5) | copy-start | bytes 772
  0.0 40.9 %collective-permute-start = (f32[4096,128]{1,0:T(8,128)}, f32[4096,128]{1,0:T(8,128)S(1)}, u32[]{:S(2)}, u32[]{:S(2)}) collective-permute-start(f32[4096,128]{1,0:T(8,128)} %bitcast.35), channel_id=1, source_target_pairs={{0,32},{32,0},{64,96},{96,64},{128,160},{160,128},{192,224},{224,1... | collective-permute-start | bytes 6291464 | tf_op jit(solution)/shard_map/ppermute | solution.py:240
  2.7 16.4 %collective-permute-start.8 = (s32[2,64]{1,0:T(2,128)S(1)}, s32[2,64]{1,0:T(2,128)S(1)}, u32[]{:S(2)}, u32[]{:S(2)}) collective-permute-start(s32[2,64]{1,0:T(2,128)S(1)} %pad_add_fusion.2), channel_id=1, source_target_pairs={{0,256},{32,288},{64,320},{96,352},{128,384},{160,416},{192,448},{... | collective-permute-start | bytes 1544 | tf_op jit(solution)/shard_map/ppermute | solution.py:240
  9.9 18.4 %collective-permute-start.5 = (f32[1024,128]{1,0:T(8,128)}, f32[1024,128]{1,0:T(8,128)S(1)}, u32[]{:S(2)}, u32[]{:S(2)}) collective-permute-start(f32[1024,128]{1,0:T(8,128)} %get-tuple-element.13), channel_id=1, source_target_pairs={{0,256},{32,288},{64,320},{96,352},{128,384},{160,416},{192,448},{... | collective-permute-start | bytes 1572872 | tf_op jit(solution)/shard_map/ppermute | solution.py:240
  12.3 26.5 %collective-permute-start.3 = (f32[1024,128]{1,0:T(8,128)}, f32[1024,128]{1,0:T(8,128)S(1)}, u32[]{:S(2)}, u32[]{:S(2)}) collective-permute-start(f32[1024,128]{1,0:T(8,128)} %get-tuple-element.14), channel_id=1, source_target_pairs={{0,256},{32,288},{64,320},{96,352},{128,384},{160,416},{192,448},{... | collective-permute-start | bytes 1572872 | tf_op jit(solution)/shard_map/ppermute | solution.py:240
  19.1 48.0 %collective-permute-start.9 = (s32[2,64]{1,0:T(2,128)S(1)}, s32[2,64]{1,0:T(2,128)S(1)}, u32[]{:S(2)}, u32[]{:S(2)}) collective-permute-start(s32[2,64]{1,0:T(2,128)S(1)} %slice.15), channel_id=1, source_target_pairs={{0,32},{32,0},{64,96},{96,64},{128,160},{160,128},{192,224},{224,1... | collective-permute-start | bytes 1544 | tf_op jit(solution)/shard_map/ppermute | solution.py:240
  28.3 23.2 %copy-start.3 = (f32[1024,128]{1,0:T(8,128)}, f32[1024,128]{1,0:T(8,128)S(1)}, u32[]{:S(2)}) copy-start(f32[1024,128]{1,0:T(8,128)S(1)} %collective-permute-done.5.far_ref.far_a_ref) | copy-start | bytes 1572868
  28.3 22.5 %collective-permute-start.6 = (f32[1024,128]{1,0:T(8,128)S(1)}, f32[1024,128]{1,0:T(8,128)}, u32[]{:S(2)}, u32[]{:S(2)}) collective-permute-start(f32[1024,128]{1,0:T(8,128)S(1)} %collective-permute-done.5.far_ref.far_a_ref), channel_id=1, source_target_pairs={{0,32},{32,0},{64,96},{96,64},{128,160},{160,128},{192,224},{224,1... | collective-permute-start | bytes 1572872 | tf_op jit(solution)/shard_map/ppermute | solution.py:240
  38.8 16.4 %copy-start.5 = (f32[1024,128]{1,0:T(8,128)}, f32[1024,128]{1,0:T(8,128)S(1)}, u32[]{:S(2)}) copy-start(f32[1024,128]{1,0:T(8,128)S(1)} %collective-permute-done.3.far_ref.far_b_ref) | copy-start | bytes 1572868
  38.8 16.4 %collective-permute-start.4 = (f32[1024,128]{1,0:T(8,128)S(1)}, f32[1024,128]{1,0:T(8,128)}, u32[]{:S(2)}, u32[]{:S(2)}) collective-permute-start(f32[1024,128]{1,0:T(8,128)S(1)} %collective-permute-done.3.far_ref.far_b_ref), channel_id=1, source_target_pairs={{0,32},{32,0},{64,96},{96,64},{128,160},{160,128},{192,224},{224,1... | collective-permute-start | bytes 1572872 | tf_op jit(solution)/shard_map/ppermute | solution.py:240
  40.9 1.3 copy-start.1
  47.5 17.5 %collective-permute-start.1 = (f32[128,256]{1,0:T(8,128)}, f32[128,256]{1,0:T(8,128)S(1)}, u32[]{:S(2)}, u32[]{:S(2)}) collective-permute-start(f32[128,256]{1,0:T(8,128)} %get-tuple-element.9.top_ref), channel_id=1, source_target_pairs={{0,256},{32,288},{64,320},{96,352},{128,384},{160,416},{192,448},{... | collective-permute-start | bytes 393224 | tf_op jit(solution)/shard_map/ppermute | solution.py:240
  55.2 15.9 %copy-start = (f32[1,4096,128]{2,1,0:T(8,128)S(1)}, f32[1,4096,128]{2,1,0:T(8,128)}, u32[]{:S(2)}) copy-start(f32[1,4096,128]{2,1,0:T(8,128)} %param.3) | copy-start | bytes 6291460
  55.2 15.9 %copy-start.4 = (f32[1024,128]{1,0:T(8,128)S(1)}, f32[1024,128]{1,0:T(8,128)}, u32[]{:S(2)}) copy-start(f32[1024,128]{1,0:T(8,128)} %copy-done.3) | copy-start | bytes 1572868
  55.2 15.9 %copy-start.8 = (f32[128,256]{1,0:T(8,128)S(1)}, f32[128,256]{1,0:T(8,128)}, u32[]{:S(2)}) copy-start(f32[128,256]{1,0:T(8,128)} %get-tuple-element.9.top_ref) | copy-start | bytes 393220
  55.2 15.9 %copy-start.9 = (f32[128,256]{1,0:T(8,128)S(1)}, f32[128,256]{1,0:T(8,128)}, u32[]{:S(2)}) copy-start(f32[128,256]{1,0:T(8,128)} %get-tuple-element.10.bottom_ref) | copy-start | bytes 393220
  55.2 15.9 %copy-start.10 = (s32[2]{0:T(128)S(1)}, s32[2]{0:T(128)}, u32[]{:S(2)}) copy-start(s32[2]{0:T(128)} %pad_add_fusion.3.place_ref) | copy-start | bytes 28
  59.1 12.0 %collective-permute-start.7 = (f32[256,256]{1,0:T(8,128)}, f32[256,256]{1,0:T(8,128)S(1)}, u32[]{:S(2)}, u32[]{:S(2)}) collective-permute-start(f32[256,256]{1,0:T(8,128)} %cross_gram.3.cross_ref), channel_id=1, source_target_pairs={{0,256},{32,288},{64,320},{96,352},{128,384},{160,416},{192,448},{... | collective-permute-start | bytes 786440 | tf_op jit(solution)/shard_map/ppermute | solution.py:240
  65.0 6.1 %collective-permute-start.2 = (f32[128,256]{1,0:T(8,128)S(1)}, f32[128,256]{1,0:T(8,128)S(1)}, u32[]{:S(2)}, u32[]{:S(2)}) collective-permute-start(f32[128,256]{1,0:T(8,128)S(1)} %collective-permute-done.1.far_top_ref), channel_id=1, source_target_pairs={{0,32},{32,0},{64,96},{96,64},{128,160},{160,128},{192,224},{224,1... | collective-permute-start | bytes 393224 | tf_op jit(solution)/shard_map/ppermute | solution.py:240
  71.1 1.6 copy-start.2
  72.7 1.0 copy-start.6
  73.8 0.9 copy-start.7
  87.6 5.5 %collective-permute-start.10 = (f32[8,128]{1,0:T(8,128)S(1)}, f32[8,128]{1,0:T(8,128)S(1)}, u32[]{:S(2)}, u32[]{:S(2)}) collective-permute-start(f32[8,128]{1,0:T(8,128)S(1)} %get-tuple-element.12), channel_id=1, source_target_pairs={{0,64},{32,96},{64,0},{96,32},{128,192},{160,224},{192,128},{224,1... | collective-permute-start | bytes 12296 | tf_op jit(solution)/shard_map/ppermute | solution.py:240
  93.1 5.5 %collective-permute-start.11 = (f32[8,128]{1,0:T(8,128)S(1)}, f32[8,128]{1,0:T(8,128)S(1)}, u32[]{:S(2)}, u32[]{:S(2)}) collective-permute-start(f32[8,128]{1,0:T(8,128)S(1)} %add.61), channel_id=1, source_target_pairs={{0,128},{32,160},{64,192},{96,224},{128,0},{160,32},{192,64},{224,... | collective-permute-start | bytes 12296 | tf_op jit(solution)/shard_map/ppermute | solution.py:240
where the time goes:
time: 179 us; the launch traced here: 177 us
  blocking collectives  71 us (40%)
  starting transfers between devices  36.1 us (20%)
  Pallas kernels  25.6 us (14%)
  waiting for transfers between devices  24.1 us (13%)
  local copies, waits for them, and re-layouts  14.8 us (8%)
  other arithmetic  2.98 us (2%)
  matrix products  1.88 us (1%)
    all_to_all x1, blocking collectives, on_device(): lax.all_to_all(outgoing.transpose(0, 2, 1, 3), ('bond', 'site'), split_ax...  71 us
    ppermute x12, starting transfers between devices, from_partner(): return lax.ppermute(value, axis, pairs)  36.1 us
    ppermute x12, waiting for transfers between devices, from_partner(): return lax.ppermute(value, axis, pairs)  24.1 us
    pallas_call x1, Pallas kernels, turn(): pl.pallas_call(turn_kernel, in_specs=[pl.BlockSpec(memory_space=pltpu.SME...  12.9 us
    pallas_call x2, Pallas kernels, cross_gram(): pl.pallas_call(cross_kernel, grid_spec=pltpu.PrefetchScalarGridSpec(num_s...  7.49 us
    reshape x2, local copies, waits for them, and re-layouts, on_device(): return arrived.reshape(1, 1, groups, capacity, rows)  5.81 us
    unnamed x27, local copies, waits for them, and re-layouts  5.31 us
    pallas_call x1, Pallas kernels, pair_gram(): pl.pallas_call(gram_kernel, grid=(steps,), in_specs=[rows_in, rows_in], o...  5.19 us
  transfers between devices with their start and end apart: 12, of which 5 were waited for; matrix products, arithmetic and copies ran while one was open for 4% of the time, Pallas kernels for 7%

commit v1 on v0

v1 whole, which is shorter than its diff:
```python
import functools

import jax
import jax.numpy as jnp
from jax import lax
from jax.experimental import pallas as pl
from jax.experimental.pallas import tpu as pltpu
from jax.sharding import PartitionSpec as P

NS_STEPS = 5
LANES = 128
F32 = jnp.float32
BF16 = jnp.bfloat16

NN = ((1,), (0,))
NT = ((1,), (1,))
TN = ((0,), (0,))


def piece_sizes(rows):
    return (rows // 2, rows // 2)


def split(value):
    high = value.astype(BF16)
    return high, (value - high.astype(F32)).astype(BF16)


def dot(left, right, contract):
    return lax.dot_general(left, right, (contract, ((), ())), preferred_element_type=F32)


def product(left, right, contract):
    return dot(left[0], right[0], contract) + (
        dot(left[0], right[1], contract) + dot(left[1], right[0], contract)
    )


VMEM = pl.BlockSpec(memory_space=pltpu.VMEM)
SMEM = pl.BlockSpec(memory_space=pltpu.SMEM)
ANY = pl.BlockSpec(memory_space=pl.ANY)


def array(*shape):
    return jax.ShapeDtypeStruct(shape, F32)


BRIEF = pl.CostEstimate(flops=1, bytes_accessed=1, transcendentals=0)


def params(mebibytes):
    return pltpu.CompilerParams(vmem_limit_bytes=mebibytes * 1024 * 1024)


def after_kernel(first_ref, value_ref, out_ref):
    out_ref[...] = value_ref[...]


def after(first, value):
    return pl.pallas_call(
        after_kernel,
        in_specs=[ANY, VMEM],
        out_specs=VMEM,
        out_shape=jax.ShapeDtypeStruct(value.shape, value.dtype),
        compiler_params=params(8),
        cost_estimate=BRIEF,
        name="after",
    )(first, value)


def gram_kernel(own_ref, next_ref, top_ref, bottom_ref):
    rows, half = own_ref.shape
    chunk = min(1024, rows)
    high = low = jnp.zeros((2 * half, 2 * half), F32)
    for begin in range(0, rows, chunk):
        span = slice(begin, begin + chunk)
        pair = split(jnp.concatenate([own_ref[span], next_ref[span]], 1))
        high += dot(pair[0], pair[0], TN)
        low += dot(pair[0], pair[1], TN)
    gram = high + (low + low.T)
    top_ref[...] = gram[:half]
    bottom_ref[...] = gram[half:]


def pair_gram(own, neighbour):
    width = own.shape[1]
    return pl.pallas_call(
        gram_kernel,
        in_specs=[VMEM, VMEM],
        out_specs=[VMEM, VMEM],
        out_shape=[array(width, 2 * width)] * 2,
        compiler_params=params(12),
        cost_estimate=BRIEF,
        name="pair_gram",
    )(own, neighbour)


def half_rows(place_ref, ref, start, size):
    half = ref.shape[0] // 2
    return ref[pl.ds(pl.multiple_of(place_ref[0] * half, half) + start, size)]


def cross_kernel(start, pieces, adds, place_ref, own_ref, next_ref, *rest):
    out_ref = rest[-1]
    total = rest[2 * pieces][...] if adds else jnp.zeros(out_ref.shape, F32)
    for far_ref, next_far_ref in zip(rest[:pieces], rest[pieces : 2 * pieces]):
        size = min(512, far_ref.shape[0])
        for begin in range(0, far_ref.shape[0], size):
            span = slice(begin, begin + size)
            here = [half_rows(place_ref, ref, start, size) for ref in (own_ref, next_ref)]
            here = split(jnp.concatenate(here, 1))
            there = split(jnp.concatenate([far_ref[span], next_far_ref[span]], 1))
            total += product(here, there, TN)
            start += size
    out_ref[...] = total


def cross_gram(place, own, neighbour, far, next_far, start, before=(), first=()):
    width = own.shape[1]
    return pl.pallas_call(
        functools.partial(cross_kernel, start, len(far), len(before)),
        in_specs=[SMEM] + [VMEM] * (2 + 2 * len(far) + len(before)) + [ANY] * len(first),
        out_specs=VMEM,
        out_shape=array(2 * width, 2 * width),
        compiler_params=params(12),
        cost_estimate=BRIEF,
        name="cross_gram",
    )(place, own, neighbour, *far, *next_far, *before, *first)


def rotations(grams, sign):
    width = grams[0].shape[0]
    half = width // 2
    row = lax.broadcasted_iota(jnp.int32, (width, width), 0)
    column = lax.broadcasted_iota(jnp.int32, (width, width), 1)
    diagonal = (row == column).astype(F32)
    order = jnp.where(row < column, 0.5, -0.5) * (1.0 - diagonal)
    order = jnp.where((row < half) == (column < half), order, order * sign)
    iterates = []
    for gram in grams:
        inverse_row = 1.0 / jnp.sqrt(jnp.sum(gram * diagonal, axis=0, keepdims=True))
        inverse_column = 1.0 / jnp.sqrt(jnp.sum(gram * diagonal, axis=1, keepdims=True))
        skew = gram * inverse_column * inverse_row * order
        iterates.append((diagonal + skew) / jnp.sqrt(1.0 + jnp.sum(skew * skew)))
    for step in range(NS_STEPS):
        parts = [split(iterate) for iterate in iterates]
        squares = [product(part, part, NT) for part in parts]
        rests = [0.5 * (diagonal - square) for square in squares]
        iterates = [
            iterate + product(part, split(rest), NN)
            for iterate, part, rest in zip(iterates, parts, rests)
        ]
    return iterates


def symmetric(first, cross, second):
    return jnp.concatenate(
        [jnp.concatenate([first, cross], 1), jnp.concatenate([cross.T, second], 1)], 0
    )


def turn_kernel(
    place_ref, top_ref, bottom_ref, far_top_ref, far_bottom_ref, cross_ref, far_cross_ref, kept_ref,
    turned_ref, norm_ref,
):
    width = top_ref.shape[0]
    sign_far = jnp.where(place_ref[0] == 0, 1.0, -1.0)
    sign_next = jnp.where(place_ref[1] == 0, 1.0, -1.0)
    cross = cross_ref[...] + far_cross_ref[...].T
    top, bottom, far_top, far_bottom = top_ref[...], bottom_ref[...], far_top_ref[...], far_bottom_ref[...]
    lo, hi = slice(0, width), slice(width, 2 * width)
    gram_01 = symmetric(top[:, lo], cross[lo, lo], far_top[:, lo])
    gram_23 = symmetric(bottom[:, hi], cross[hi, hi], far_bottom[:, lo])
    mixed = jnp.concatenate(
        [
            jnp.concatenate([top[:, hi], cross[lo, hi]], 1),
            jnp.concatenate([cross[hi, lo].T, far_top[:, hi]], 1),
        ],
        0,
    )
    turn_01, turn_23 = rotations([gram_01, gram_23], sign_far)
    s_01, s_23 = split(turn_01), split(turn_23)
    s_01t, s_23t = split(turn_01.T), split(turn_23.T)
    half_01 = split(product(split(gram_01), s_01, NN))
    half_23 = split(product(split(gram_23), s_23, NN))
    half_mixed = split(product(split(mixed), s_23, NN))

    def corner(left, right, which):
        return product([p[which] for p in left], [p[:, which] for p in right], NN)

    grams = [
        symmetric(corner(s_01t, half_01, w), corner(s_01t, half_mixed, w), corner(s_23t, half_23, w))
        for w in (lo, hi)
    ]
    seconds = rotations(grams, sign_next)

    total = jnp.zeros((1, 1), F32)
    for number, (gram, second, which) in enumerate(zip(grams, seconds, (lo, hi))):
        parts = split(second)
        moved = product(split(gram), parts, NN) * second
        kept = jnp.concatenate([kept_ref[number : number + 1], kept_ref[number + 2 : number + 3]], 1)
        total += jnp.sum(jnp.sum(moved, axis=0, keepdims=True) * kept, axis=1, keepdims=True)
        turned_ref[number] = jnp.concatenate(
            [
                product([p[:, which] for p in s_01], [p[lo, lo] for p in parts], NN),
                product([p[:, which] for p in s_23], [p[hi, lo] for p in parts], NN),
            ],
            0,
        )
    norm_ref[...] = jnp.broadcast_to(total, norm_ref.shape)


def turn(place, grams, kept):
    width = grams[0].shape[0]
    return pl.pallas_call(
        turn_kernel,
        in_specs=[SMEM] + [VMEM] * 7,
        out_specs=[VMEM, VMEM],
        out_shape=[array(2, 4 * width, width), array(8, width)],
        compiler_params=params(24),
        name="turn",
    )(place, *grams, kept)


def place_kernel(place_ref, turned_ref, route_ref, block_ref, next_ref, *rest):
    far_refs, out_ref = rest[:-1], rest[-1]
    width = block_ref.shape[1]
    placed = []
    for piece in zip(*[split(turned_ref[number]) for number in range(2)]):
        moved = sum(dot(piece[number], route_ref[number].astype(BF16), NN) for number in range(2))
        placed.append(moved.T.astype(BF16))
    left = [piece[:, : 2 * width] for piece in placed]
    right = [piece[:, 2 * width :] for piece in placed]
    pieces = len(far_refs) // 2
    done = 0
    for far_ref, next_far_ref in zip(far_refs[:pieces], far_refs[pieces:]):
        size = min(512, far_ref.shape[0])
        for begin in range(0, far_ref.shape[0], size):
            span = slice(begin, begin + size)
            here = [half_rows(place_ref, ref, done, size) for ref in (block_ref, next_ref)]
            near = split(jnp.concatenate([here[0], far_ref[span]], 1))
            away = split(jnp.concatenate([here[1], next_far_ref[span]], 1))
            out_ref[:, done : done + size] = product(left, near, NT) + product(right, away, NT)
            done += size


def placed(place, turned, routes, own, neighbour, far, next_far):
    width = own.shape[1]
    rows = sum(piece.shape[0] for piece in far)
    return pl.pallas_call(
        place_kernel,
        in_specs=[SMEM] + [VMEM] * (4 + 2 * len(far)),
        out_specs=VMEM,
        out_shape=array(routes.shape[2], rows),
        compiler_params=params(16),
        cost_estimate=pl.CostEstimate(
            flops=48 * rows * width * width, bytes_accessed=16 * rows * width, transcendentals=0
        ),
        name="placed",
    )(place, turned, routes, own, neighbour, *far, *next_far)


def spread_kernel(total, kept_ref, norm_ref, out_ref):
    scale = jnp.sqrt(total / norm_ref[0:1, 0:1])
    for tile in range(out_ref.shape[1]):
        value = kept_ref[:, tile * LANES : (tile + 1) * LANES] * scale
        out_ref[:, tile] = value.reshape(out_ref.shape[0], out_ref.shape[2], LANES)


def spread(kept, norm, total, capacity):
    shape = (kept.shape[0] // capacity, kept.shape[1] // LANES, capacity, LANES)
    return pl.pallas_call(
        functools.partial(spread_kernel, total),
        in_specs=[VMEM, VMEM],
        out_specs=VMEM,
        out_shape=array(*shape),
        compiler_params=params(8),
        name="spread",
    )(kept, norm)


def join_kernel(tiles_ref, out_ref):
    for tile in range(tiles_ref.shape[1]):
        out_ref[:, :, tile * LANES : (tile + 1) * LANES] = tiles_ref[:, tile]


def join(tiles):
    groups, count, capacity, _ = tiles.shape
    return pl.pallas_call(
        join_kernel,
        in_specs=[VMEM],
        out_specs=VMEM,
        out_shape=array(groups, capacity, count * LANES),
        compiler_params=params(8),
        name="join",
    )(tiles)


def from_partner(value, axis, distance):
    pairs = [(source, source ^ distance) for source in range(lax.axis_size(axis))]
    return lax.ppermute(value, axis, pairs)


def route_of(listed, side, groups, width):
    keep, owners = listed[0], listed[1]
    kept = keep.shape[0]
    order = jnp.arange(kept, dtype=jnp.int32)
    same = owners[:, None] == owners[None, :]
    slot = jnp.sum((same & (order[None, :] < order[:, None])).astype(jnp.int32), axis=1)
    capacity = max(2, 2 * kept // groups)
    target = (owners * 2 + side) * capacity + slot
    places = jnp.arange(2 * groups * capacity, dtype=jnp.int32)
    columns = jnp.arange(width, dtype=jnp.int32)
    picked = (keep[:, None] == columns[None, :]).astype(BF16)
    placed = (target[:, None] == places[None, :]).astype(BF16)
    return lax.dot_general(picked, placed, (TN, ((), ())), preferred_element_type=F32)


def on_device(two_site, keep_list, owner_map):
    block = two_site[0]
    rows, width = block.shape
    half = rows // 2
    count, groups = lax.axis_size("bond"), lax.axis_size("site")
    far = count // 2
    position = lax.axis_index("bond")
    upper = position // far
    place = jnp.stack([upper, position & 1]).astype(jnp.int32)

    sizes = piece_sizes(half)
    starts = [(1 - upper) * half + sum(sizes[:number]) for number in range(len(sizes))]
    sent = [
        lax.dynamic_slice_in_dim(block, start, size) for start, size in zip(starts, sizes)
    ]
    neighbour = from_partner(block, "bond", 1)
    far_rows = [from_partner(piece, "bond", far) for piece in sent]
    listed = jnp.stack([keep_list[0], owner_map[0, :, 0]])
    top, bottom = pair_gram(block, neighbour)
    next_rows = [from_partner(piece, "bond", 1) for piece in far_rows]
    far_top = from_partner(top, "bond", far)
    far_bottom = from_partner(far_top, "bond", 1)
    listed = after(far_rows[0], listed)
    listed = jnp.concatenate([listed, from_partner(listed, "bond", far)])
    routes = jnp.stack(
        [
            route_of(listed[:2], upper, groups, width),
            route_of(listed[2:], 1 - upper, groups, width),
        ]
    )
    lists = jnp.concatenate([listed[::2], from_partner(listed[::2], "bond", 1)])
    columns = jnp.arange(width, dtype=jnp.int32)
    kept = jnp.sum((lists[:, :, None] == columns).astype(F32), axis=1)

    last = half - sent[-1].shape[0]
    cross = cross_gram(place, block, neighbour, far_rows[:-1], next_rows[:-1], 0)
    cross = cross_gram(place, block, neighbour, far_rows[-1:], next_rows[-1:], last, (cross,))
    far_cross = from_partner(cross, "bond", far)

    turned, squares = turn(place, (top, bottom, far_top, far_bottom, cross, far_cross), kept)
    outgoing = placed(place, turned, routes, block, neighbour, far_rows, next_rows)
    for distance in [1 << bit for bit in range(1, far.bit_length() - 1)]:
        squares = squares + from_partner(squares, "bond", distance)
    keep_count = keep_list.shape[1]
    capacity = max(2, 2 * keep_count // groups)
    members = [
        [(first + far * side) * groups + site for site in range(groups) for side in range(2)]
        for first in range(far)
    ]
    arrived = lax.all_to_all(
        spread(outgoing, squares, float(rows * count * keep_count), capacity),
        ("bond", "site"),
        split_axis=0,
        concat_axis=0,
        tiled=True,
        axis_index_groups=members,
    )
    joined = join(arrived.reshape(groups, rows // LANES, capacity, LANES))
    return joined.reshape(1, 1, groups, capacity, rows)


def solution(mesh):
    return jax.shard_map(
        on_device,
        mesh=mesh,
        in_specs=(P("site", None, "bond"), P("site", "bond"), P("site", "bond", None)),
        out_specs=P("site", "bond", None, None, None),
        check_vma=False,
    )
```

time: 179 us -> 158 us (0.88)
  local copies, waits for them, and re-layouts: 14.8 us -> 2.29 us
  other arithmetic: 2.98 us -> 0.61 us
  Pallas kernels: 25.6 us -> 23.3 us
    reshape x2 -> x0, local copies, waits for them, and re-layouts: 5.81 us -> none  [on_device(): return arrived.reshape(1, 1, groups, capacity, rows)]
    unnamed x27 -> x6, local copies, waits for them, and re-layouts: 5.31 us -> 0.01 us
    pallas_call x4 -> x8, Pallas kernels: 25.6 us -> 23.3 us  [the longest x1 9.57 us: turn(): pl.pallas_call(turn_kernel, in_specs=[SMEM] + [VMEM] * 7, out_specs=[VMEM...]
  transfers between devices with their start and end apart: 12 -> 12, of which waited for: 5 -> 4; matrix products, arithmetic and copies ran while one was open for 4% -> 2% of each run, Pallas kernels for 7% -> 7%
where the time goes in v1:
time: 158 us
  blocking collectives  71.7 us (45%)
  starting transfers between devices  35.7 us (23%)
  Pallas kernels  23.3 us (15%)
  waiting for transfers between devices  23.2 us (15%)
  local copies, waits for them, and re-layouts  2.29 us (1%)
    all_to_all x1, blocking collectives, on_device(): lax.all_to_all(spread(outgoing, squares, float(rows * count * keep_count)...  71.7 us
    ppermute x12, starting transfers between devices, from_partner(): return lax.ppermute(value, axis, pairs)  35.7 us
    ppermute x12, waiting for transfers between devices, from_partner(): return lax.ppermute(value, axis, pairs)  23.2 us
    pallas_call x1, Pallas kernels, turn(): pl.pallas_call(turn_kernel, in_specs=[SMEM] + [VMEM] * 7, out_specs=[VMEM...  9.57 us
    pallas_call x2, Pallas kernels, cross_gram(): pl.pallas_call(functools.partial(cross_kernel, start, len(far), len(befor...  4.61 us
    pallas_call x1, Pallas kernels, placed(): pl.pallas_call(place_kernel, in_specs=[SMEM] + [VMEM] * (4 + 2 * len(far)...  4.01 us
  transfers between devices with their start and end apart: 12, of which 4 were waited for; matrix products, arithmetic and copies ran while one was open for 2% of the time, Pallas kernels for 7%

profile of v1, /device:TPU:56, one launch (start us, length us, event | category | flops | bytes accessed | tf_op | source)
XLA Modules:
  0.0 157.6 jit_solution(3840147065509643484)
XLA Ops:
  0.0 0.0 copy-start
  0.0 0.0 copy-start.1
  0.0 0.0 copy-start.2
  0.0 2.1 %collective-permute-start = (f32[4096,128]{1,0:T(8,128)}, f32[4096,128]{1,0:T(8,128)}, u32[]{:S(2)}, u32[]{:S(2)}) collective-permute-start(f32[4096,128]{1,0:T(8,128)} %bitcast.26), channel_id=1, source_target_pairs={{0,32},{32,0},{64,96},{96,64},{128,160},{160,128},{192,224},{224,1... | collective-permute-start | bytes 6291464 | tf_op jit(solution)/shard_map/ppermute | solution.py:301
  2.1 2.2 %dynamic-slice_bitcast_fusion = (f32[1024,128]{1,0:T(8,128)}, f32[1024,128]{1,0:T(8,128)}) fusion(f32[1,4096,128]{2,1,0:T(8,128)} %param.3, s32[]{:T(128)S(6)} %select_n.13, s32[]{:T(128)S(6)} %select_n.12), kind=kLoop, calls=%fused_computation.2 | loop fusion | bytes 2097160 | tf_op jit(solution)/shard_map/dynamic_slice | solution.py:332
  4.3 4.9 %collective-permute-start.5 = (f32[1024,128]{1,0:T(8,128)}, f32[1024,128]{1,0:T(8,128)S(1)}, u32[]{:S(2)}, u32[]{:S(2)}) collective-permute-start(f32[1024,128]{1,0:T(8,128)} %get-tuple-element.13), channel_id=1, source_target_pairs={{0,256},{32,288},{64,320},{96,352},{128,384},{160,416},{192,448},{... | collective-permute-start | bytes 1572872 | tf_op jit(solution)/shard_map/ppermute | solution.py:301
  9.3 2.4 %collective-permute-start.3 = (f32[1024,128]{1,0:T(8,128)}, f32[1024,128]{1,0:T(8,128)S(1)}, u32[]{:S(2)}, u32[]{:S(2)}) collective-permute-start(f32[1024,128]{1,0:T(8,128)} %get-tuple-element.14), channel_id=1, source_target_pairs={{0,256},{32,288},{64,320},{96,352},{128,384},{160,416},{192,448},{... | collective-permute-start | bytes 1572872 | tf_op jit(solution)/shard_map/ppermute | solution.py:301
  11.7 0.1 pad_add_fusion.3.place_ref
  11.8 0.0 copy-done.1
  11.8 0.0 copy-done.2
  11.8 10.9 %collective-permute-done.5.rest_0_.first_ref = f32[1024,128]{1,0:T(8,128)S(1)} collective-permute-done((f32[1024,128]{1,0:T(8,128)}, f32[1024,128]{1,0:T(8,128)S(1)}, u32[]{:S(2)}, u32[]{:S(2)}) %collective-permute-start.5) | collective-permute-done | bytes 524320 | tf_op jit(solution)/shard_map/ppermute | solution.py:301
  22.7 4.9 %collective-permute-start.8 = (s32[2,64]{1,0:T(2,128)S(1)}, s32[2,64]{1,0:T(2,128)S(1)}, u32[]{:S(2)}, u32[]{:S(2)}) collective-permute-start(s32[2,64]{1,0:T(2,128)S(1)} %after.1), channel_id=1, source_target_pairs={{0,256},{32,288},{64,320},{96,352},{128,384},{160,416},{192,448},{... | collective-permute-start | bytes 1544 | tf_op jit(solution)/shard_map/ppermute | solution.py:301
  27.6 0.2 convert_reduce_fusion.2
  27.8 0.3 convolution_bitcast_fusion.1
  28.1 1.9 %collective-permute-start.6 = (f32[1024,128]{1,0:T(8,128)S(1)}, f32[1024,128]{1,0:T(8,128)}, u32[]{:S(2)}, u32[]{:S(2)}) collective-permute-start(f32[1024,128]{1,0:T(8,128)S(1)} %collective-permute-done.5.rest_0_.first_ref), channel_id=1, source_target_pairs={{0,32},{32,0},{64,96},{96,64},{128,160},{160,128},{192,224},{224,1... | collective-permute-start | bytes 1572872 | tf_op jit(solution)/shard_map/ppermute | solution.py:301
  30.0 3.5 %collective-permute-done.3.rest_0_.rest_1_ = f32[1024,128]{1,0:T(8,128)S(1)} collective-permute-done((f32[1024,128]{1,0:T(8,128)}, f32[1024,128]{1,0:T(8,128)S(1)}, u32[]{:S(2)}, u32[]{:S(2)}) %collective-permute-start.3) | collective-permute-done | bytes 524320 | tf_op jit(solution)/shard_map/ppermute | solution.py:301
  33.5 1.9 %collective-permute-start.4 = (f32[1024,128]{1,0:T(8,128)S(1)}, f32[1024,128]{1,0:T(8,128)}, u32[]{:S(2)}, u32[]{:S(2)}) collective-permute-start(f32[1024,128]{1,0:T(8,128)S(1)} %collective-permute-done.3.rest_0_.rest_1_), channel_id=1, source_target_pairs={{0,32},{32,0},{64,96},{96,64},{128,160},{160,128},{192,224},{224,1... | collective-permute-start | bytes 1572872 | tf_op jit(solution)/shard_map/ppermute | solution.py:301
  35.4 0.0 collective-permute-done.8
  35.5 2.4 %collective-permute-start.9 = (s32[2,64]{1,0:T(2,128)S(1)}, s32[2,64]{1,0:T(2,128)S(1)}, u32[]{:S(2)}, u32[]{:S(2)}) collective-permute-start(s32[2,64]{1,0:T(2,128)S(1)} %slice.16), channel_id=1, source_target_pairs={{0,32},{32,0},{64,96},{96,64},{128,160},{160,128},{192,224},{224,1... | collective-permute-start | bytes 1544 | tf_op jit(solution)/shard_map/ppermute | solution.py:301
  37.9 0.2 convert_reduce_fusion.1
  38.1 0.0 collective-permute-done.next_ref
  38.1 0.0 copy-done
  38.1 2.9 %pair_gram.1 = (f32[128,256]{1,0:T(8,128)S(1)}, f32[128,256]{1,0:T(8,128)S(1)}) custom-call(f32[4096,128]{1,0:T(8,128)S(1)} %bitcast.27, f32[4096,128]{1,0:T(8,128)} %collective-permute-done.next_ref), custom_call_target="tpu_custom_call" | custom-call | flops 1 | bytes 1 | tf_op jit(solution)/shard_map/pair_gram/pallas_call | solution.py:87
  41.0 4.9 %collective-permute-start.1 = (f32[128,256]{1,0:T(8,128)S(1)}, f32[128,256]{1,0:T(8,128)S(1)}, u32[]{:S(2)}, u32[]{:S(2)}) collective-permute-start(f32[128,256]{1,0:T(8,128)S(1)} %get-tuple-element.9.top_ref), channel_id=1, source_target_pairs={{0,256},{32,288},{64,320},{96,352},{128,384},{160,416},{192,448},{... | collective-permute-start | bytes 393224 | tf_op jit(solution)/shard_map/ppermute | solution.py:301
  46.0 0.0 collective-permute-done.6.rest_1_.rest_2_
  46.0 2.3 %cross_gram.2.rest_2_ = f32[256,256]{1,0:T(8,128)S(1)} custom-call(s32[2]{0:T(128)S(1)} %pad_add_fusion.3.place_ref, f32[4096,128]{1,0:T(8,128)S(1)} %bitcast.28, f32[4096,128]{1,0:T(8,128)} %collective-permute-done.next_ref, f32[1024,128]{1,0:T(8,128)S(1)} %collective-permute-done.5.rest_0_.first_ref, f32[1024,128]{1,0:T(8,128)} %collective-permute-done.6.rest_1_.rest_2_), custom_call_target="tpu_custom_call" | custom-call | flops 1 | bytes 1 | tf_op jit(solution)/shard_map/cross_gram/pallas_call | solution.py:120
  48.3 0.0 collective-permute-done.4.rest_1_.rest_3_
  48.3 2.3 %cross_gram.3.cross_ref = f32[256,256]{1,0:T(8,128)S(1)} custom-call(s32[2]{0:T(128)S(1)} %pad_add_fusion.3.place_ref, f32[4096,128]{1,0:T(8,128)S(1)} %bitcast.29, f32[4096,128]{1,0:T(8,128)} %collective-permute-done.next_ref, f32[1024,128]{1,0:T(8,128)S(1)} %collective-permute-done.3.rest_0_.rest_1_, f32[1024,128]{1,0:T(8,128)} %collective-permute-done.4.rest_1_.rest_3_, ...), custom_call_target="tpu_custom_call" | custom-call | flops 1 | bytes 1 | tf_op jit(solution)/shard_map/cross_gram/pallas_call | solution.py:120
  50.6 2.4 %collective-permute-start.7 = (f32[256,256]{1,0:T(8,128)S(1)}, f32[256,256]{1,0:T(8,128)S(1)}, u32[]{:S(2)}, u32[]{:S(2)}) collective-permute-start(f32[256,256]{1,0:T(8,128)S(1)} %cross_gram.3.cross_ref), channel_id=1, source_target_pairs={{0,256},{32,288},{64,320},{96,352},{128,384},{160,416},{192,448},{... | collective-permute-start | bytes 786440 | tf_op jit(solution)/shard_map/ppermute | solution.py:301
  53.1 0.3 convolution_bitcast_fusion
  53.3 0.0 collective-permute-done.1.far_top_ref
  53.4 1.9 %collective-permute-start.2 = (f32[128,256]{1,0:T(8,128)S(1)}, f32[128,256]{1,0:T(8,128)S(1)}, u32[]{:S(2)}, u32[]{:S(2)}) collective-permute-start(f32[128,256]{1,0:T(8,128)S(1)} %collective-permute-done.1.far_top_ref), channel_id=1, source_target_pairs={{0,32},{32,0},{64,96},{96,64},{128,160},{160,128},{192,224},{224,1... | collective-permute-start | bytes 393224 | tf_op jit(solution)/shard_map/ppermute | solution.py:301
  55.3 0.0 collective-permute-done.9
  55.3 0.1 convert_reduce_fusion.kept_ref
  55.4 6.6 %collective-permute-done.7.far_cross_ref = f32[256,256]{1,0:T(8,128)S(1)} collective-permute-done((f32[256,256]{1,0:T(8,128)S(1)}, f32[256,256]{1,0:T(8,128)S(1)}, u32[]{:S(2)}, u32[]{:S(2)}) %collective-permute-start.7) | collective-permute-done | bytes 262176 | tf_op jit(solution)/shard_map/ppermute | solution.py:301
  62.0 0.0 collective-permute-done.2.far_bottom_ref
  62.0 9.6 %turn.1 = (f32[2,512,128]{2,1,0:T(8,128)S(1)}, f32[8,128]{1,0:T(8,128)S(1)}) custom-call(s32[2]{0:T(128)S(1)} %pad_add_fusion.3.place_ref, f32[128,256]{1,0:T(8,128)S(1)} %get-tuple-element.9.top_ref, f32[128,256]{1,0:T(8,128)S(1)} %get-tuple-element.10.bottom_ref, f32[128,256]{1,0:T(8,128)S(1)} %collective-permute-done.1.far_top_ref, ...), custom_call_target="tpu_custom_call" | custom-call | tf_op jit(solution)/shard_map/turn/pallas_call | solution.py:215
  71.6 3.3 %collective-permute-start.10 = (f32[8,128]{1,0:T(8,128)S(1)}, f32[8,128]{1,0:T(8,128)S(1)}, u32[]{:S(2)}, u32[]{:S(2)}) collective-permute-start(f32[8,128]{1,0:T(8,128)S(1)} %get-tuple-element.12), channel_id=1, source_target_pairs={{0,64},{32,96},{64,0},{96,32},{128,192},{160,224},{192,128},{224,1... | collective-permute-start | bytes 12296 | tf_op jit(solution)/shard_map/ppermute | solution.py:301
  74.9 2.2 %collective-permute-done.10 = f32[8,128]{1,0:T(8,128)S(1)} collective-permute-done((f32[8,128]{1,0:T(8,128)S(1)}, f32[8,128]{1,0:T(8,128)S(1)}, u32[]{:S(2)}, u32[]{:S(2)}) %collective-permute-start.10) | collective-permute-done | bytes 4128 | tf_op jit(solution)/shard_map/ppermute | solution.py:301
  77.1 2.7 %collective-permute-start.11 = (f32[8,128]{1,0:T(8,128)S(1)}, f32[8,128]{1,0:T(8,128)S(1)}, u32[]{:S(2)}, u32[]{:S(2)}) collective-permute-start(f32[8,128]{1,0:T(8,128)S(1)} %add.61), channel_id=1, source_target_pairs={{0,128},{32,160},{64,192},{96,224},{128,0},{160,32},{192,64},{224,... | collective-permute-start | bytes 12296 | tf_op jit(solution)/shard_map/ppermute | solution.py:301
  79.8 4.0 %placed.1.kept_ref = f32[256,2048]{1,0:T(8,128)S(1)} custom-call(s32[2]{0:T(128)S(1)} %pad_add_fusion.3.place_ref, f32[2,512,128]{2,1,0:T(8,128)S(1)} %get-tuple-element.11.turned_ref, f32[2,128,256]{2,1,0:T(8,128)S(1)} %pad_maximum_fusion.route_ref, f32[4096,128]{1,0:T(8,128)S(1)} %bitcast.30, f32[4096,128]{1,0:T(8,128)} %collective-permute-done.next_ref, ...), custom_call_target="tpu_custom_call" | custom-call | flops 1610612736 | bytes 4194304 | tf_op jit(solution)/shard_map/placed/pallas_call | solution.py:250
  83.8 0.0 collective-permute-done.11
  83.8 0.6 spread.1
  84.4 71.7 %all_to_all.5 = f32[64,16,4,128]{3,2,1,0:T(4,128)S(1)} all-to-all(f32[64,16,4,128]{3,2,1,0:T(4,128)S(1)} %spread.1), channel_id=1, replica_groups={{0,256,1,257,2,258,3,259,4,260,5,261,6,262,7,263,8,264,9,265,10,266,11,..., dimensions={0} | all-to-all | bytes 4194304 | tf_op jit(solution)/shard_map/all_to_all | solution.py:368
  156.0 1.5 join.1
  (12 shorter events, 0.1 us)
Async XLA Ops:
  0.0 38.1 %copy-start = (f32[1,4096,128]{2,1,0:T(8,128)S(1)}, f32[1,4096,128]{2,1,0:T(8,128)}, u32[]{:S(2)}) copy-start(f32[1,4096,128]{2,1,0:T(8,128)} %param.3) | copy-start | bytes 6291460
  0.0 11.8 %copy-start.1 = (s32[1,64,1]{1,2,0:T(1,128)S(1)}, s32[1,64,1]{1,2,0:T(1,128)}, u32[]{:S(2)}) copy-start(s32[1,64,1]{1,2,0:T(1,128)} %param.5) | copy-start | bytes 772
  0.0 11.8 %copy-start.2 = (s32[1,64]{1,0:T(1,128)S(1)}, s32[1,64]{1,0:T(1,128)}, u32[]{:S(2)}) copy-start(s32[1,64]{1,0:T(1,128)} %param.4) | copy-start | bytes 772
  0.0 38.1 %collective-permute-start = (f32[4096,128]{1,0:T(8,128)}, f32[4096,128]{1,0:T(8,128)}, u32[]{:S(2)}, u32[]{:S(2)}) collective-permute-start(f32[4096,128]{1,0:T(8,128)} %bitcast.26), channel_id=1, source_target_pairs={{0,32},{32,0},{64,96},{96,64},{128,160},{160,128},{192,224},{224,1... | collective-permute-start | bytes 6291464 | tf_op jit(solution)/shard_map/ppermute | solution.py:301
  4.3 18.3 %collective-permute-start.5 = (f32[1024,128]{1,0:T(8,128)}, f32[1024,128]{1,0:T(8,128)S(1)}, u32[]{:S(2)}, u32[]{:S(2)}) collective-permute-start(f32[1024,128]{1,0:T(8,128)} %get-tuple-element.13), channel_id=1, source_target_pairs={{0,256},{32,288},{64,320},{96,352},{128,384},{160,416},{192,448},{... | collective-permute-start | bytes 1572872 | tf_op jit(solution)/shard_map/ppermute | solution.py:301
  9.3 24.2 %collective-permute-start.3 = (f32[1024,128]{1,0:T(8,128)}, f32[1024,128]{1,0:T(8,128)S(1)}, u32[]{:S(2)}, u32[]{:S(2)}) collective-permute-start(f32[1024,128]{1,0:T(8,128)} %get-tuple-element.14), channel_id=1, source_target_pairs={{0,256},{32,288},{64,320},{96,352},{128,384},{160,416},{192,448},{... | collective-permute-start | bytes 1572872 | tf_op jit(solution)/shard_map/ppermute | solution.py:301
  22.7 12.8 %collective-permute-start.8 = (s32[2,64]{1,0:T(2,128)S(1)}, s32[2,64]{1,0:T(2,128)S(1)}, u32[]{:S(2)}, u32[]{:S(2)}) collective-permute-start(s32[2,64]{1,0:T(2,128)S(1)} %after.1), channel_id=1, source_target_pairs={{0,256},{32,288},{64,320},{96,352},{128,384},{160,416},{192,448},{... | collective-permute-start | bytes 1544 | tf_op jit(solution)/shard_map/ppermute | solution.py:301
  28.1 17.9 %collective-permute-start.6 = (f32[1024,128]{1,0:T(8,128)S(1)}, f32[1024,128]{1,0:T(8,128)}, u32[]{:S(2)}, u32[]{:S(2)}) collective-permute-start(f32[1024,128]{1,0:T(8,128)S(1)} %collective-permute-done.5.rest_0_.first_ref), channel_id=1, source_target_pairs={{0,32},{32,0},{64,96},{96,64},{128,160},{160,128},{192,224},{224,1... | collective-permute-start | bytes 1572872 | tf_op jit(solution)/shard_map/ppermute | solution.py:301
  33.5 14.8 %collective-permute-start.4 = (f32[1024,128]{1,0:T(8,128)S(1)}, f32[1024,128]{1,0:T(8,128)}, u32[]{:S(2)}, u32[]{:S(2)}) collective-permute-start(f32[1024,128]{1,0:T(8,128)S(1)} %collective-permute-done.3.rest_0_.rest_1_), channel_id=1, source_target_pairs={{0,32},{32,0},{64,96},{96,64},{128,160},{160,128},{192,224},{224,1... | collective-permute-start | bytes 1572872 | tf_op jit(solution)/shard_map/ppermute | solution.py:301
  35.5 19.8 %collective-permute-start.9 = (s32[2,64]{1,0:T(2,128)S(1)}, s32[2,64]{1,0:T(2,128)S(1)}, u32[]{:S(2)}, u32[]{:S(2)}) collective-permute-start(s32[2,64]{1,0:T(2,128)S(1)} %slice.16), channel_id=1, source_target_pairs={{0,32},{32,0},{64,96},{96,64},{128,160},{160,128},{192,224},{224,1... | collective-permute-start | bytes 1544 | tf_op jit(solution)/shard_map/ppermute | solution.py:301
  41.0 12.3 %collective-permute-start.1 = (f32[128,256]{1,0:T(8,128)S(1)}, f32[128,256]{1,0:T(8,128)S(1)}, u32[]{:S(2)}, u32[]{:S(2)}) collective-permute-start(f32[128,256]{1,0:T(8,128)S(1)} %get-tuple-element.9.top_ref), channel_id=1, source_target_pairs={{0,256},{32,288},{64,320},{96,352},{128,384},{160,416},{192,448},{... | collective-permute-start | bytes 393224 | tf_op jit(solution)/shard_map/ppermute | solution.py:301
  50.6 11.3 %collective-permute-start.7 = (f32[256,256]{1,0:T(8,128)S(1)}, f32[256,256]{1,0:T(8,128)S(1)}, u32[]{:S(2)}, u32[]{:S(2)}) collective-permute-start(f32[256,256]{1,0:T(8,128)S(1)} %cross_gram.3.cross_ref), channel_id=1, source_target_pairs={{0,256},{32,288},{64,320},{96,352},{128,384},{160,416},{192,448},{... | collective-permute-start | bytes 786440 | tf_op jit(solution)/shard_map/ppermute | solution.py:301
  53.4 8.6 %collective-permute-start.2 = (f32[128,256]{1,0:T(8,128)S(1)}, f32[128,256]{1,0:T(8,128)S(1)}, u32[]{:S(2)}, u32[]{:S(2)}) collective-permute-start(f32[128,256]{1,0:T(8,128)S(1)} %collective-permute-done.1.far_top_ref), channel_id=1, source_target_pairs={{0,32},{32,0},{64,96},{96,64},{128,160},{160,128},{192,224},{224,1... | collective-permute-start | bytes 393224 | tf_op jit(solution)/shard_map/ppermute | solution.py:301
  71.6 5.5 %collective-permute-start.10 = (f32[8,128]{1,0:T(8,128)S(1)}, f32[8,128]{1,0:T(8,128)S(1)}, u32[]{:S(2)}, u32[]{:S(2)}) collective-permute-start(f32[8,128]{1,0:T(8,128)S(1)} %get-tuple-element.12), channel_id=1, source_target_pairs={{0,64},{32,96},{64,0},{96,32},{128,192},{160,224},{192,128},{224,1... | collective-permute-start | bytes 12296 | tf_op jit(solution)/shard_map/ppermute | solution.py:301
  77.1 6.7 %collective-permute-start.11 = (f32[8,128]{1,0:T(8,128)S(1)}, f32[8,128]{1,0:T(8,128)S(1)}, u32[]{:S(2)}, u32[]{:S(2)}) collective-permute-start(f32[8,128]{1,0:T(8,128)S(1)} %add.61), channel_id=1, source_target_pairs={{0,128},{32,160},{64,192},{96,224},{128,0},{160,32},{192,64},{224,... | collective-permute-start | bytes 12296 | tf_op jit(solution)/shard_map/ppermute | solution.py:301

commit v2 on v1

--- a/solution.py
+++ b/solution.py
@@ -18,7 +18,14 @@
 
 
 def piece_sizes(rows):
-    return (rows // 2, rows // 2)
+    first = rows * 7 // 16
+    return (first, rows - first)
+
+
+def tiles(rows):
+    count = max(1, round(rows / 512))
+    bounds = [LANES * (number * (rows // LANES) // count) for number in range(count)] + [rows]
+    return [slice(begin, end) for begin, end in zip(bounds[:-1], bounds[1:])]
 
 
 def split(value):
@@ -52,80 +59,82 @@
     return pltpu.CompilerParams(vmem_limit_bytes=mebibytes * 1024 * 1024)
 
 
-def after_kernel(first_ref, value_ref, out_ref):
-    out_ref[...] = value_ref[...]
-
-
-def after(first, value):
-    return pl.pallas_call(
-        after_kernel,
-        in_specs=[ANY, VMEM],
+def held_kernel(first_ref, value_ref, listed_ref, out_ref):
+    rows = value_ref.shape[0]
+    out_ref[:rows] = value_ref[...]
+    out_ref[rows:] = listed_ref[...]
+
+
+def held(first, value, listed):
+    return pl.pallas_call(
+        held_kernel,
+        in_specs=[ANY, VMEM, VMEM],
         out_specs=VMEM,
-        out_shape=jax.ShapeDtypeStruct(value.shape, value.dtype),
+        out_shape=array(value.shape[0] + listed.shape[0], value.shape[1]),
         compiler_params=params(8),
         cost_estimate=BRIEF,
-        name="after",
-    )(first, value)
-
-
-def gram_kernel(own_ref, next_ref, top_ref, bottom_ref):
-    rows, half = own_ref.shape
+        name="held",
+    )(first, value, listed)
+
+
+def half_rows(place_ref, ref, start, size):
+    half = ref.shape[0] // 2
+    return ref[pl.ds(pl.multiple_of(place_ref[0] * half, half) + start, size)]
+
+
+def cross_products(place_ref, own_ref, next_ref, far_ref, next_far_ref, start, count):
+    width = own_ref.shape[1]
+    total = jnp.zeros((2 * width, 2 * width), F32)
+    for span in tiles(count):
+        first, size = start + span.start, span.stop - span.start
+        here = [half_rows(place_ref, ref, first, size) for ref in (own_ref, next_ref)]
+        here = split(jnp.concatenate(here, 1))
+        there = split(jnp.concatenate([far_ref[span], next_far_ref[span]], 1))
+        total += product(here, there, TN)
+    lo, hi = slice(0, width), slice(width, 2 * width)
+    return [total[lo, lo], total[lo, hi], total[hi, lo], total[hi, hi]]
+
+
+def first_kernel(place_ref, own_ref, next_ref, far_ref, next_far_ref, out_ref):
+    rows, width = own_ref.shape
     chunk = min(1024, rows)
-    high = low = jnp.zeros((2 * half, 2 * half), F32)
+    high = low = jnp.zeros((2 * width, 2 * width), F32)
     for begin in range(0, rows, chunk):
         span = slice(begin, begin + chunk)
         pair = split(jnp.concatenate([own_ref[span], next_ref[span]], 1))
         high += dot(pair[0], pair[0], TN)
         low += dot(pair[0], pair[1], TN)
     gram = high + (low + low.T)
-    top_ref[...] = gram[:half]
-    bottom_ref[...] = gram[half:]
-
-
-def pair_gram(own, neighbour):
-    width = own.shape[1]
-    return pl.pallas_call(
-        gram_kernel,
-        in_specs=[VMEM, VMEM],
-        out_specs=[VMEM, VMEM],
-        out_shape=[array(width, 2 * width)] * 2,
+    parts = cross_products(place_ref, own_ref, next_ref, far_ref, next_far_ref, 0, far_ref.shape[0])
+    parts += [gram[:width, :width], gram[:width, width:], gram[width:, width:]]
+    for number, part in enumerate(parts):
+        out_ref[number * width : (number + 1) * width] = part
+    out_ref[7 * width :] = jnp.zeros((16, width), F32)
+
+
+def last_kernel(start, place_ref, own_ref, next_ref, far_ref, next_far_ref, before_ref, out_ref):
+    width = own_ref.shape[1]
+    count = far_ref.shape[0] - 8
+    parts = cross_products(place_ref, own_ref, next_ref, far_ref, next_far_ref, start, count)
+    for number, part in enumerate(parts):
+        span = slice(number * width, (number + 1) * width)
+        out_ref[span] = before_ref[span] + part
+    out_ref[4 * width : 7 * width] = before_ref[4 * width : 7 * width]
+    out_ref[7 * width : 7 * width + 8] = far_ref[count:]
+    out_ref[7 * width + 8 :] = next_far_ref[count:]
+
+
+def gram_call(kernel, name, place, *values):
+    width = values[0].shape[1]
+    return pl.pallas_call(
+        kernel,
+        in_specs=[SMEM] + [VMEM] * len(values),
+        out_specs=VMEM,
+        out_shape=array(7 * width + 16, width),
         compiler_params=params(12),
         cost_estimate=BRIEF,
-        name="pair_gram",
-    )(own, neighbour)
-
-
-def half_rows(place_ref, ref, start, size):
-    half = ref.shape[0] // 2
-    return ref[pl.ds(pl.multiple_of(place_ref[0] * half, half) + start, size)]
-
-
-def cross_kernel(start, pieces, adds, place_ref, own_ref, next_ref, *rest):
-    out_ref = rest[-1]
-    total = rest[2 * pieces][...] if adds else jnp.zeros(out_ref.shape, F32)
-    for far_ref, next_far_ref in zip(rest[:pieces], rest[pieces : 2 * pieces]):
-        size = min(512, far_ref.shape[0])
-        for begin in range(0, far_ref.shape[0], size):
-            span = slice(begin, begin + size)
-            here = [half_rows(place_ref, ref, start, size) for ref in (own_ref, next_ref)]
-            here = split(jnp.concatenate(here, 1))
-            there = split(jnp.concatenate([far_ref[span], next_far_ref[span]], 1))
-            total += product(here, there, TN)
-            start += size
-    out_ref[...] = total
-
-
-def cross_gram(place, own, neighbour, far, next_far, start, before=(), first=()):
-    width = own.shape[1]
-    return pl.pallas_call(
-        functools.partial(cross_kernel, start, len(far), len(before)),
-        in_specs=[SMEM] + [VMEM] * (2 + 2 * len(far) + len(before)) + [ANY] * len(first),
-        out_specs=VMEM,
-        out_shape=array(2 * width, 2 * width),
-        compiler_params=params(12),
-        cost_estimate=BRIEF,
-        name="cross_gram",
-    )(place, own, neighbour, *far, *next_far, *before, *first)
+        name=name,
+    )(place, *values)
 
 
 def rotations(grams, sign):
@@ -159,24 +168,31 @@
     )
 
 
-def turn_kernel(
-    place_ref, top_ref, bottom_ref, far_top_ref, far_bottom_ref, cross_ref, far_cross_ref, kept_ref,
-    turned_ref, norm_ref,
-):
-    width = top_ref.shape[0]
+def kept_row(listed):
+    width = listed.shape[1]
+    row = lax.broadcasted_iota(jnp.int32, (width // 2, width), 0)
+    column = lax.broadcasted_iota(jnp.int32, (width // 2, width), 1)
+    numbers = jnp.sum(jnp.where(row == column, listed, 0.0), axis=1, keepdims=True)
+    return jnp.sum((numbers == column.astype(F32)).astype(F32), axis=0, keepdims=True)
+
+
+def turn_kernel(place_ref, mine_ref, theirs_ref, turned_ref, norm_ref):
+    width = mine_ref.shape[1]
     sign_far = jnp.where(place_ref[0] == 0, 1.0, -1.0)
     sign_next = jnp.where(place_ref[1] == 0, 1.0, -1.0)
-    cross = cross_ref[...] + far_cross_ref[...].T
-    top, bottom, far_top, far_bottom = top_ref[...], bottom_ref[...], far_top_ref[...], far_bottom_ref[...]
+    mine, theirs = [
+        [ref[number * width : (number + 1) * width] for number in range(7)]
+        for ref in (mine_ref, theirs_ref)
+    ]
+    lists = [ref[begin : begin + 1] for begin in (7 * width, 7 * width + 8) for ref in (mine_ref, theirs_ref)]
+    kept_rows = [kept_row(listed) for listed in lists]
     lo, hi = slice(0, width), slice(width, 2 * width)
-    gram_01 = symmetric(top[:, lo], cross[lo, lo], far_top[:, lo])
-    gram_23 = symmetric(bottom[:, hi], cross[hi, hi], far_bottom[:, lo])
+    gram_01 = symmetric(mine[4], mine[0] + theirs[0].T, theirs[4])
+    gram_23 = symmetric(mine[6], mine[3] + theirs[3].T, theirs[6])
+    gram_03 = mine[1] + theirs[2].T
+    gram_12 = mine[2].T + theirs[1]
     mixed = jnp.concatenate(
-        [
-            jnp.concatenate([top[:, hi], cross[lo, hi]], 1),
-            jnp.concatenate([cross[hi, lo].T, far_top[:, hi]], 1),
-        ],
-        0,
+        [jnp.concatenate([mine[5], gram_03], 1), jnp.concatenate([gram_12, theirs[5]], 1)], 0
     )
     turn_01, turn_23 = rotations([gram_01, gram_23], sign_far)
     s_01, s_23 = split(turn_01), split(turn_23)
@@ -198,7 +214,7 @@
     for number, (gram, second, which) in enumerate(zip(grams, seconds, (lo, hi))):
         parts = split(second)
         moved = product(split(gram), parts, NN) * second
-        kept = jnp.concatenate([kept_ref[number : number + 1], kept_ref[number + 2 : number + 3]], 1)
+        kept = jnp.concatenate([kept_rows[number], kept_rows[number + 2]], 1)
         total += jnp.sum(jnp.sum(moved, axis=0, keepdims=True) * kept, axis=1, keepdims=True)
         turned_ref[number] = jnp.concatenate(
             [
@@ -210,19 +226,19 @@
     norm_ref[...] = jnp.broadcast_to(total, norm_ref.shape)
 
 
-def turn(place, grams, kept):
-    width = grams[0].shape[0]
+def turn(place, *values):
+    width = values[0].shape[1]
     return pl.pallas_call(
         turn_kernel,
-        in_specs=[SMEM] + [VMEM] * 7,
+        in_specs=[SMEM] + [VMEM] * len(values),
         out_specs=[VMEM, VMEM],
         out_shape=[array(2, 4 * width, width), array(8, width)],
         compiler_params=params(24),
         name="turn",
-    )(place, *grams, kept)
-
-
-def place_kernel(place_ref, turned_ref, route_ref, block_ref, next_ref, *rest):
+    )(place, *values)
+
+
+def place_kernel(sizes, place_ref, turned_ref, route_ref, block_ref, next_ref, *rest):
     far_refs, out_ref = rest[:-1], rest[-1]
     width = block_ref.shape[1]
     placed = []
@@ -233,10 +249,9 @@
     right = [piece[:, 2 * width :] for piece in placed]
     pieces = len(far_refs) // 2
     done = 0
-    for far_ref, next_far_ref in zip(far_refs[:pieces], far_refs[pieces:]):
-        size = min(512, far_ref.shape[0])
-        for begin in range(0, far_ref.shape[0], size):
-            span = slice(begin, begin + size)
+    for far_ref, next_far_ref, rows in zip(far_refs[:pieces], far_refs[pieces:], sizes):
+        for span in tiles(rows):
+            size = span.stop - span.start
             here = [half_rows(place_ref, ref, done, size) for ref in (block_ref, next_ref)]
             near = split(jnp.concatenate([here[0], far_ref[span]], 1))
             away = split(jnp.concatenate([here[1], next_far_ref[span]], 1))
@@ -244,11 +259,11 @@
             done += size
 
 
-def placed(place, turned, routes, own, neighbour, far, next_far):
+def placed(place, turned, routes, own, neighbour, far, next_far, sizes):
     width = own.shape[1]
-    rows = sum(piece.shape[0] for piece in far)
-    return pl.pallas_call(
-        place_kernel,
+    rows = sum(sizes)
+    return pl.pallas_call(
+        functools.partial(place_kernel, sizes),
         in_specs=[SMEM] + [VMEM] * (4 + 2 * len(far)),
         out_specs=VMEM,
         out_shape=array(routes.shape[2], rows),
@@ -301,9 +316,10 @@
     return lax.ppermute(value, axis, pairs)
 
 
-def route_of(listed, side, groups, width):
-    keep, owners = listed[0], listed[1]
-    kept = keep.shape[0]
+def route_of(listed, side, groups):
+    width = listed.shape[0]
+    kept = width // 2
+    keep, owners = listed.astype(jnp.int32).reshape(2, kept)
     order = jnp.arange(kept, dtype=jnp.int32)
     same = owners[:, None] == owners[None, :]
     slot = jnp.sum((same & (order[None, :] < order[:, None])).astype(jnp.int32), axis=1)
@@ -328,35 +344,35 @@
 
     sizes = piece_sizes(half)
     starts = [(1 - upper) * half + sum(sizes[:number]) for number in range(len(sizes))]
+    listed = jnp.concatenate([keep_list[0], owner_map[0, :, 0]]).astype(F32)
+    listed = jnp.broadcast_to(listed, (8, width))
+    sources = (block, lax.optimization_barrier(block))
     sent = [
-        lax.dynamic_slice_in_dim(block, start, size) for start, size in zip(starts, sizes)
+        lax.dynamic_slice_in_dim(source, start, size)
+        for source, start, size in zip(sources, starts, sizes)
     ]
     neighbour = from_partner(block, "bond", 1)
-    far_rows = [from_partner(piece, "bond", far) for piece in sent]
-    listed = jnp.stack([keep_list[0], owner_map[0, :, 0]])
-    top, bottom = pair_gram(block, neighbour)
-    next_rows = [from_partner(piece, "bond", 1) for piece in far_rows]
-    far_top = from_partner(top, "bond", far)
-    far_bottom = from_partner(far_top, "bond", 1)
-    listed = after(far_rows[0], listed)
-    listed = jnp.concatenate([listed, from_partner(listed, "bond", far)])
+    far_a, far_b = [from_partner(piece, "bond", far) for piece in sent]
+    next_far_a = from_partner(far_a, "bond", 1)
+    grams = gram_call(first_kernel, "first_gram", place, block, neighbour, far_a, next_far_a)
+    far_b = held(grams, far_b, listed)
+    next_far_b = from_partner(far_b, "bond", 1)
+    grams = gram_call(
+        functools.partial(last_kernel, sizes[0]),
+        "last_gram", place, block, neighbour, far_b, next_far_b, grams,
+    )
+    far_grams = from_partner(grams, "bond", far)
     routes = jnp.stack(
         [
-            route_of(listed[:2], upper, groups, width),
-            route_of(listed[2:], 1 - upper, groups, width),
+            route_of(listed[0], upper, groups),
+            route_of(far_grams[7 * width], 1 - upper, groups),
         ]
     )
-    lists = jnp.concatenate([listed[::2], from_partner(listed[::2], "bond", 1)])
-    columns = jnp.arange(width, dtype=jnp.int32)
-    kept = jnp.sum((lists[:, :, None] == columns).astype(F32), axis=1)
-
-    last = half - sent[-1].shape[0]
-    cross = cross_gram(place, block, neighbour, far_rows[:-1], next_rows[:-1], 0)
-    cross = cross_gram(place, block, neighbour, far_rows[-1:], next_rows[-1:], last, (cross,))
-    far_cross = from_partner(cross, "bond", far)
-
-    turned, squares = turn(place, (top, bottom, far_top, far_bottom, cross, far_cross), kept)
-    outgoing = placed(place, turned, routes, block, neighbour, far_rows, next_rows)
+
+    turned, squares = turn(place, grams, far_grams)
+    outgoing = placed(
+        place, turned, routes, block, neighbour, (far_a, far_b), (next_far_a, next_far_b), sizes
+    )
     for distance in [1 << bit for bit in range(1, far.bit_length() - 1)]:
         squares = squares + from_partner(squares, "bond", distance)
     keep_count = keep_list.shape[1]

time: 158 us -> 152 us (0.962)
  starting transfers between devices: 35.7 us -> 25 us
  waiting for transfers between devices: 23.2 us -> 28.8 us
    ppermute x12 -> x8, starting transfers between devices: 35.7 us -> 25 us  [from_partner(): return lax.ppermute(value, axis, pairs)]
    ppermute x12 -> x8, waiting for transfers between devices: 23.2 us -> 28.8 us  [from_partner(): return lax.ppermute(value, axis, pairs)]
    pallas_call x6 -> x5, Pallas kernels: 21.1 us -> 20.7 us  [the longest x1 9.51 us: turn(): pl.pallas_call(turn_kernel, in_specs=[SMEM] + [VMEM] * len(values), out_s...]
  transfers between devices with their start and end apart: 12 -> 8, of which waited for: 4 -> 6; matrix products, arithmetic and copies ran while one was open for 2% -> 3% of each run, Pallas kernels for 7% -> 5%
where the time goes in v2:
time: 152 us; the launch traced here: 151 us
  blocking collectives  70.3 us (46%)
  waiting for transfers between devices  28.8 us (19%)
  starting transfers between devices  25 us (16%)
  Pallas kernels  22.8 us (15%)
  local copies, waits for them, and re-layouts  3.13 us (2%)
    all_to_all x1, blocking collectives, on_device(): lax.all_to_all(spread(outgoing, squares, float(rows * count * keep_count)...  70.3 us
    ppermute x8, waiting for transfers between devices, from_partner(): return lax.ppermute(value, axis, pairs)  28.8 us
    ppermute x8, starting transfers between devices, from_partner(): return lax.ppermute(value, axis, pairs)  25 us
    pallas_call x1, Pallas kernels, turn(): pl.pallas_call(turn_kernel, in_specs=[SMEM] + [VMEM] * len(values), out_s...  9.51 us
    pallas_call x2, Pallas kernels, gram_call(): pl.pallas_call(kernel, in_specs=[SMEM] + [VMEM] * len(values), out_specs=...  5.72 us
    pallas_call x1, Pallas kernels, placed(): pl.pallas_call(functools.partial(place_kernel, sizes), in_specs=[SMEM] +...  4.38 us
  transfers between devices with their start and end apart: 8, of which 6 were waited for; matrix products, arithmetic and copies ran while one was open for 3% of the time, Pallas kernels for 5%

profile of v2, /device:TPU:56, one launch (start us, length us, event | category | flops | bytes accessed | tf_op | source)
XLA Modules:
  0.0 151.5 jit_solution(15659099278358022340)
XLA Ops:
  0.0 0.0 copy-start
  0.0 0.0 copy-start.1
  0.0 0.0 copy-start.2
  0.0 2.1 %collective-permute-start = (f32[4096,128]{1,0:T(8,128)}, f32[4096,128]{1,0:T(8,128)}, u32[]{:S(2)}, u32[]{:S(2)}) collective-permute-start(f32[4096,128]{1,0:T(8,128)} %bitcast.19), channel_id=1, source_target_pairs={{0,32},{32,0},{64,96},{96,64},{128,160},{160,128},{192,224},{224,1... | collective-permute-start | bytes 6291464 | tf_op jit(solution)/shard_map/ppermute | solution.py:316
  2.1 1.1 dynamic-slice_bitcast_fusion
  3.2 4.9 %collective-permute-start.1 = (f32[896,128]{1,0:T(8,128)S(1)}, f32[896,128]{1,0:T(8,128)S(1)}, u32[]{:S(2)}, u32[]{:S(2)}) collective-permute-start(f32[896,128]{1,0:T(8,128)S(1)} %dynamic-slice_bitcast_fusion), channel_id=1, source_target_pairs={{0,256},{32,288},{64,320},{96,352},{128,384},{160,416},{192,448},{... | collective-permute-start | bytes 1376264 | tf_op jit(solution)/shard_map/ppermute | solution.py:316
  8.1 1.9 %constant_dynamic-slice_fusion = f32[1152,128]{1,0:T(8,128)} fusion(f32[4096,128]{1,0:T(8,128)} %bitcast.20, s32[]{:T(128)S(6)} %select_n.13), kind=kLoop, calls=%fused_computation.24 | loop fusion | bytes 1179652 | tf_op jit(solution)/shard_map/dynamic_slice | solution.py:351
  10.0 2.4 %collective-permute-start.3 = (f32[1152,128]{1,0:T(8,128)}, f32[1152,128]{1,0:T(8,128)}, u32[]{:S(2)}, u32[]{:S(2)}) collective-permute-start(f32[1152,128]{1,0:T(8,128)} %constant_dynamic-slice_fusion), channel_id=1, source_target_pairs={{0,256},{32,288},{64,320},{96,352},{128,384},{160,416},{192,448},{... | collective-permute-start | bytes 1769480 | tf_op jit(solution)/shard_map/ppermute | solution.py:316
  12.4 7.4 %collective-permute-done.1.far_ref.rest_0_ = f32[896,128]{1,0:T(8,128)S(1)} collective-permute-done((f32[896,128]{1,0:T(8,128)S(1)}, f32[896,128]{1,0:T(8,128)S(1)}, u32[]{:S(2)}, u32[]{:S(2)}) %collective-permute-start.1) | collective-permute-done | bytes 458784 | tf_op jit(solution)/shard_map/ppermute | solution.py:316
  19.9 1.9 %collective-permute-start.2 = (f32[896,128]{1,0:T(8,128)S(1)}, f32[896,128]{1,0:T(8,128)S(1)}, u32[]{:S(2)}, u32[]{:S(2)}) collective-permute-start(f32[896,128]{1,0:T(8,128)S(1)} %collective-permute-done.1.far_ref.rest_0_), channel_id=1, source_target_pairs={{0,32},{32,0},{64,96},{96,64},{128,160},{160,128},{192,224},{224,1... | collective-permute-start | bytes 1376264 | tf_op jit(solution)/shard_map/ppermute | solution.py:316
  21.8 0.1 pad_add_fusion.place_ref
  21.9 0.0 copy-done.1
  21.9 0.0 copy-done.2
  21.9 0.1 fusion.6
  21.9 1.6 %collective-permute-done.2.next_far_ref.rest_2_ = f32[896,128]{1,0:T(8,128)S(1)} collective-permute-done((f32[896,128]{1,0:T(8,128)S(1)}, f32[896,128]{1,0:T(8,128)S(1)}, u32[]{:S(2)}, u32[]{:S(2)}) %collective-permute-start.2) | collective-permute-done | bytes 458784 | tf_op jit(solution)/shard_map/ppermute | solution.py:316
  23.6 0.0 collective-permute-done.next_ref
  23.6 0.0 copy-done
  23.6 3.3 %first_gram.1.first_ref.before_ref = f32[912,128]{1,0:T(8,128)S(1)} custom-call(s32[2]{0:T(128)S(1)} %pad_add_fusion.place_ref, f32[4096,128]{1,0:T(8,128)S(1)} %bitcast.21, f32[4096,128]{1,0:T(8,128)} %collective-permute-done.next_ref, f32[896,128]{1,0:T(8,128)S(1)} %collective-permute-done.1.far_ref.rest_0_, ...), custom_call_target="tpu_custom_call" | custom-call | flops 1 | bytes 1 | tf_op jit(solution)/shard_map/first_gram/pallas_call | solution.py:129
  26.9 5.3 %collective-permute-done.3.value_ref = f32[1152,128]{1,0:T(8,128)} collective-permute-done((f32[1152,128]{1,0:T(8,128)}, f32[1152,128]{1,0:T(8,128)}, u32[]{:S(2)}, u32[]{:S(2)}) %collective-permute-start.3) | collective-permute-done | bytes 589856 | tf_op jit(solution)/shard_map/ppermute | solution.py:316
  32.2 1.1 held.1.far_ref.rest_1_
  33.3 1.9 %collective-permute-start.4 = (f32[1160,128]{1,0:T(8,128)S(1)}, f32[1160,128]{1,0:T(8,128)S(1)}, u32[]{:S(2)}, u32[]{:S(2)}) collective-permute-start(f32[1160,128]{1,0:T(8,128)S(1)} %held.1.far_ref.rest_1_), channel_id=1, source_target_pairs={{0,32},{32,0},{64,96},{96,64},{128,160},{160,128},{192,224},{224,1... | collective-permute-start | bytes 1781768 | tf_op jit(solution)/shard_map/ppermute | solution.py:316
  35.3 2.0 %collective-permute-done.4.next_far_ref.rest_3_ = f32[1160,128]{1,0:T(8,128)S(1)} collective-permute-done((f32[1160,128]{1,0:T(8,128)S(1)}, f32[1160,128]{1,0:T(8,128)S(1)}, u32[]{:S(2)}, u32[]{:S(2)}) %collective-permute-start.4) | collective-permute-done | bytes 593952 | tf_op jit(solution)/shard_map/ppermute | solution.py:316
  37.2 2.4 %last_gram.1.mine_ref = f32[912,128]{1,0:T(8,128)S(1)} custom-call(s32[2]{0:T(128)S(1)} %pad_add_fusion.place_ref, f32[4096,128]{1,0:T(8,128)S(1)} %bitcast.22, f32[4096,128]{1,0:T(8,128)} %collective-permute-done.next_ref, f32[1160,128]{1,0:T(8,128)S(1)} %held.1.far_ref.rest_1_, f32[1160,128]{1,0:T(8,128)S(1)} %collective-permute-done.4.next_far_ref.rest_3_, ...), custom_call_target="tpu_custom_call" | custom-call | flops 1 | bytes 1 | tf_op jit(solution)/shard_map/last_gram/pallas_call | solution.py:129
  39.6 4.9 %collective-permute-start.5 = (f32[912,128]{1,0:T(8,128)S(1)}, f32[912,128]{1,0:T(8,128)S(1)}, u32[]{:S(2)}, u32[]{:S(2)}) collective-permute-start(f32[912,128]{1,0:T(8,128)S(1)} %last_gram.1.mine_ref), channel_id=1, source_target_pairs={{0,256},{32,288},{64,320},{96,352},{128,384},{160,416},{192,448},{... | collective-permute-start | bytes 1400840 | tf_op jit(solution)/shard_map/ppermute | solution.py:316
  44.5 0.1 unstack.19
  44.6 0.2 convert_reduce_fusion.1
  44.8 0.1 fusion.7
  44.9 0.3 convolution_bitcast_fusion.1
  45.2 10.6 %collective-permute-done.5.theirs_ref = f32[912,128]{1,0:T(8,128)S(1)} collective-permute-done((f32[912,128]{1,0:T(8,128)S(1)}, f32[912,128]{1,0:T(8,128)S(1)}, u32[]{:S(2)}, u32[]{:S(2)}) %collective-permute-start.5) | collective-permute-done | bytes 466976 | tf_op jit(solution)/shard_map/ppermute | solution.py:316
  55.7 0.1 slice_bitcast_fusion.1
  55.8 0.2 convert_reduce_fusion
  56.0 0.1 multiply_add_fusion
  56.1 9.5 %turn.1 = (f32[2,512,128]{2,1,0:T(8,128)S(1)}, f32[8,128]{1,0:T(8,128)S(1)}) custom-call(s32[2]{0:T(128)S(1)} %pad_add_fusion.place_ref, f32[912,128]{1,0:T(8,128)S(1)} %last_gram.1.mine_ref, f32[912,128]{1,0:T(8,128)S(1)} %collective-permute-done.5.theirs_ref), custom_call_target="tpu_custom_call" | custom-call | tf_op jit(solution)/shard_map/turn/pallas_call | solution.py:231
  65.6 3.3 %collective-permute-start.6 = (f32[8,128]{1,0:T(8,128)S(1)}, f32[8,128]{1,0:T(8,128)S(1)}, u32[]{:S(2)}, u32[]{:S(2)}) collective-permute-start(f32[8,128]{1,0:T(8,128)S(1)} %get-tuple-element.8), channel_id=1, source_target_pairs={{0,64},{32,96},{64,0},{96,32},{128,192},{160,224},{192,128},{224,1... | collective-permute-start | bytes 12296 | tf_op jit(solution)/shard_map/ppermute | solution.py:316
  68.9 0.3 convolution_bitcast_fusion
  69.2 1.9 %collective-permute-done.6 = f32[8,128]{1,0:T(8,128)S(1)} collective-permute-done((f32[8,128]{1,0:T(8,128)S(1)}, f32[8,128]{1,0:T(8,128)S(1)}, u32[]{:S(2)}, u32[]{:S(2)}) %collective-permute-start.6) | collective-permute-done | bytes 4128 | tf_op jit(solution)/shard_map/ppermute | solution.py:316
  71.1 3.6 %collective-permute-start.7 = (f32[8,128]{1,0:T(8,128)S(1)}, f32[8,128]{1,0:T(8,128)S(1)}, u32[]{:S(2)}, u32[]{:S(2)}) collective-permute-start(f32[8,128]{1,0:T(8,128)S(1)} %add.53), channel_id=1, source_target_pairs={{0,128},{32,160},{64,192},{96,224},{128,0},{160,32},{192,64},{224,... | collective-permute-start | bytes 12296 | tf_op jit(solution)/shard_map/ppermute | solution.py:316
  74.7 4.4 %placed.1.kept_ref = f32[256,2048]{1,0:T(8,128)S(1)} custom-call(s32[2]{0:T(128)S(1)} %pad_add_fusion.place_ref, f32[2,512,128]{2,1,0:T(8,128)S(1)} %get-tuple-element.7.turned_ref, f32[2,128,256]{2,1,0:T(8,128)S(1)} %pad_maximum_fusion.route_ref, f32[4096,128]{1,0:T(8,128)S(1)} %bitcast.23, f32[4096,128]{1,0:T(8,128)} %collective-permute-done.next_ref, ...), custom_call_target="tpu_custom_call" | custom-call | flops 1610612736 | bytes 4194304 | tf_op jit(solution)/shard_map/placed/pallas_call | solution.py:265
  79.1 0.0 collective-permute-done.7
  79.1 0.6 spread.1
  79.7 70.3 %all_to_all.5 = f32[64,16,4,128]{3,2,1,0:T(4,128)S(1)} all-to-all(f32[64,16,4,128]{3,2,1,0:T(4,128)S(1)} %spread.1), channel_id=1, replica_groups={{0,256,1,257,2,258,3,259,4,260,5,261,6,262,7,263,8,264,9,265,10,266,11,..., dimensions={0} | all-to-all | bytes 4194304 | tf_op jit(solution)/shard_map/all_to_all | solution.py:384
  149.9 1.5 %join.1 = f32[32,4,4096]{2,1,0:T(4,128)} custom-call(f32[32,32,4,128]{3,2,1,0:T(4,128)S(1)} %bitcast.24), custom_call_target="tpu_custom_call" | custom-call | tf_op jit(solution)/shard_map/join/pallas_call | solution.py:304
  (5 shorter events, 0.0 us)
Async XLA Ops:
  0.0 23.6 %copy-start = (f32[1,4096,128]{2,1,0:T(8,128)S(1)}, f32[1,4096,128]{2,1,0:T(8,128)}, u32[]{:S(2)}) copy-start(f32[1,4096,128]{2,1,0:T(8,128)} %param.3) | copy-start | bytes 6291460
  0.0 21.9 %copy-start.1 = (s32[1,64,1]{1,2,0:T(1,128)S(1)}, s32[1,64,1]{1,2,0:T(1,128)}, u32[]{:S(2)}) copy-start(s32[1,64,1]{1,2,0:T(1,128)} %param.5) | copy-start | bytes 772
  0.0 21.9 %copy-start.2 = (s32[1,64]{1,0:T(1,128)S(1)}, s32[1,64]{1,0:T(1,128)}, u32[]{:S(2)}) copy-start(s32[1,64]{1,0:T(1,128)} %param.4) | copy-start | bytes 772
  0.0 23.6 %collective-permute-start = (f32[4096,128]{1,0:T(8,128)}, f32[4096,128]{1,0:T(8,128)}, u32[]{:S(2)}, u32[]{:S(2)}) collective-permute-start(f32[4096,128]{1,0:T(8,128)} %bitcast.19), channel_id=1, source_target_pairs={{0,32},{32,0},{64,96},{96,64},{128,160},{160,128},{192,224},{224,1... | collective-permute-start | bytes 6291464 | tf_op jit(solution)/shard_map/ppermute | solution.py:316
  3.2 16.7 %collective-permute-start.1 = (f32[896,128]{1,0:T(8,128)S(1)}, f32[896,128]{1,0:T(8,128)S(1)}, u32[]{:S(2)}, u32[]{:S(2)}) collective-permute-start(f32[896,128]{1,0:T(8,128)S(1)} %dynamic-slice_bitcast_fusion), channel_id=1, source_target_pairs={{0,256},{32,288},{64,320},{96,352},{128,384},{160,416},{192,448},{... | collective-permute-start | bytes 1376264 | tf_op jit(solution)/shard_map/ppermute | solution.py:316
  10.0 22.2 %collective-permute-start.3 = (f32[1152,128]{1,0:T(8,128)}, f32[1152,128]{1,0:T(8,128)}, u32[]{:S(2)}, u32[]{:S(2)}) collective-permute-start(f32[1152,128]{1,0:T(8,128)} %constant_dynamic-slice_fusion), channel_id=1, source_target_pairs={{0,256},{32,288},{64,320},{96,352},{128,384},{160,416},{192,448},{... | collective-permute-start | bytes 1769480 | tf_op jit(solution)/shard_map/ppermute | solution.py:316
  19.9 3.7 %collective-permute-start.2 = (f32[896,128]{1,0:T(8,128)S(1)}, f32[896,128]{1,0:T(8,128)S(1)}, u32[]{:S(2)}, u32[]{:S(2)}) collective-permute-start(f32[896,128]{1,0:T(8,128)S(1)} %collective-permute-done.1.far_ref.rest_0_), channel_id=1, source_target_pairs={{0,32},{32,0},{64,96},{96,64},{128,160},{160,128},{192,224},{224,1... | collective-permute-start | bytes 1376264 | tf_op jit(solution)/shard_map/ppermute | solution.py:316
  33.3 3.9 %collective-permute-start.4 = (f32[1160,128]{1,0:T(8,128)S(1)}, f32[1160,128]{1,0:T(8,128)S(1)}, u32[]{:S(2)}, u32[]{:S(2)}) collective-permute-start(f32[1160,128]{1,0:T(8,128)S(1)} %held.1.far_ref.rest_1_), channel_id=1, source_target_pairs={{0,32},{32,0},{64,96},{96,64},{128,160},{160,128},{192,224},{224,1... | collective-permute-start | bytes 1781768 | tf_op jit(solution)/shard_map/ppermute | solution.py:316
  39.6 16.1 %collective-permute-start.5 = (f32[912,128]{1,0:T(8,128)S(1)}, f32[912,128]{1,0:T(8,128)S(1)}, u32[]{:S(2)}, u32[]{:S(2)}) collective-permute-start(f32[912,128]{1,0:T(8,128)S(1)} %last_gram.1.mine_ref), channel_id=1, source_target_pairs={{0,256},{32,288},{64,320},{96,352},{128,384},{160,416},{192,448},{... | collective-permute-start | bytes 1400840 | tf_op jit(solution)/shard_map/ppermute | solution.py:316
  65.6 5.5 %collective-permute-start.6 = (f32[8,128]{1,0:T(8,128)S(1)}, f32[8,128]{1,0:T(8,128)S(1)}, u32[]{:S(2)}, u32[]{:S(2)}) collective-permute-start(f32[8,128]{1,0:T(8,128)S(1)} %get-tuple-element.8), channel_id=1, source_target_pairs={{0,64},{32,96},{64,0},{96,32},{128,192},{160,224},{192,128},{224,1... | collective-permute-start | bytes 12296 | tf_op jit(solution)/shard_map/ppermute | solution.py:316
  71.1 8.0 %collective-permute-start.7 = (f32[8,128]{1,0:T(8,128)S(1)}, f32[8,128]{1,0:T(8,128)S(1)}, u32[]{:S(2)}, u32[]{:S(2)}) collective-permute-start(f32[8,128]{1,0:T(8,128)S(1)} %add.53), channel_id=1, source_target_pairs={{0,128},{32,160},{64,192},{96,224},{128,0},{160,32},{192,64},{224,... | collective-permute-start | bytes 12296 | tf_op jit(solution)/shard_map/ppermute | solution.py:316

commit v3 on v2

--- a/solution.py
+++ b/solution.py
@@ -18,7 +18,7 @@
 
 
 def piece_sizes(rows):
-    first = rows * 7 // 16
+    first = rows * 3 // 4
     return (first, rows - first)
 
 
@@ -59,69 +59,43 @@
     return pltpu.CompilerParams(vmem_limit_bytes=mebibytes * 1024 * 1024)
 
 
-def held_kernel(first_ref, value_ref, listed_ref, out_ref):
-    rows = value_ref.shape[0]
-    out_ref[:rows] = value_ref[...]
-    out_ref[rows:] = listed_ref[...]
-
-
-def held(first, value, listed):
-    return pl.pallas_call(
-        held_kernel,
-        in_specs=[ANY, VMEM, VMEM],
-        out_specs=VMEM,
-        out_shape=array(value.shape[0] + listed.shape[0], value.shape[1]),
-        compiler_params=params(8),
-        cost_estimate=BRIEF,
-        name="held",
-    )(first, value, listed)
-
-
 def half_rows(place_ref, ref, start, size):
     half = ref.shape[0] // 2
     return ref[pl.ds(pl.multiple_of(place_ref[0] * half, half) + start, size)]
 
 
-def cross_products(place_ref, own_ref, next_ref, far_ref, next_far_ref, start, count):
-    width = own_ref.shape[1]
-    total = jnp.zeros((2 * width, 2 * width), F32)
-    for span in tiles(count):
+def cross_products(place_ref, own_ref, next_ref, far_ref, start):
+    rows, width = far_ref.shape
+    total = jnp.zeros((width, 2 * width), F32)
+    for span in tiles(rows):
         first, size = start + span.start, span.stop - span.start
         here = [half_rows(place_ref, ref, first, size) for ref in (own_ref, next_ref)]
-        here = split(jnp.concatenate(here, 1))
-        there = split(jnp.concatenate([far_ref[span], next_far_ref[span]], 1))
-        total += product(here, there, TN)
-    lo, hi = slice(0, width), slice(width, 2 * width)
-    return [total[lo, lo], total[lo, hi], total[hi, lo], total[hi, hi]]
-
-
-def first_kernel(place_ref, own_ref, next_ref, far_ref, next_far_ref, out_ref):
+        total += product(split(far_ref[span]), split(jnp.concatenate(here, 1)), TN)
+    return total
+
+
+def first_kernel(place_ref, own_ref, next_ref, far_ref, listed_ref, out_ref):
     rows, width = own_ref.shape
     chunk = min(1024, rows)
-    high = low = jnp.zeros((2 * width, 2 * width), F32)
+    total = jnp.zeros((width, 2 * width), F32)
     for begin in range(0, rows, chunk):
         span = slice(begin, begin + chunk)
-        pair = split(jnp.concatenate([own_ref[span], next_ref[span]], 1))
-        high += dot(pair[0], pair[0], TN)
-        low += dot(pair[0], pair[1], TN)
-    gram = high + (low + low.T)
-    parts = cross_products(place_ref, own_ref, next_ref, far_ref, next_far_ref, 0, far_ref.shape[0])
-    parts += [gram[:width, :width], gram[:width, width:], gram[width:, width:]]
-    for number, part in enumerate(parts):
-        out_ref[number * width : (number + 1) * width] = part
-    out_ref[7 * width :] = jnp.zeros((16, width), F32)
-
-
-def last_kernel(start, place_ref, own_ref, next_ref, far_ref, next_far_ref, before_ref, out_ref):
+        own, neighbour = split(own_ref[span]), split(next_ref[span])
+        pair = [jnp.concatenate([a, b], 1) for a, b in zip(own, neighbour)]
+        total += product(own, pair, TN)
+    cross = cross_products(place_ref, own_ref, next_ref, far_ref, 0)
+    for number, part in enumerate([cross, total]):
+        out_ref[2 * number * width : (2 * number + 1) * width] = part[:, :width]
+        out_ref[(2 * number + 1) * width : (2 * number + 2) * width] = part[:, width:]
+    out_ref[4 * width :] = listed_ref[...]
+
+
+def last_kernel(start, place_ref, own_ref, next_ref, far_ref, before_ref, out_ref):
     width = own_ref.shape[1]
-    count = far_ref.shape[0] - 8
-    parts = cross_products(place_ref, own_ref, next_ref, far_ref, next_far_ref, start, count)
-    for number, part in enumerate(parts):
-        span = slice(number * width, (number + 1) * width)
-        out_ref[span] = before_ref[span] + part
-    out_ref[4 * width : 7 * width] = before_ref[4 * width : 7 * width]
-    out_ref[7 * width : 7 * width + 8] = far_ref[count:]
-    out_ref[7 * width + 8 :] = next_far_ref[count:]
+    cross = cross_products(place_ref, own_ref, next_ref, far_ref, start)
+    out_ref[:width] = before_ref[:width] + cross[:, :width]
+    out_ref[width : 2 * width] = before_ref[width : 2 * width] + cross[:, width:]
+    out_ref[2 * width :] = before_ref[2 * width :]
 
 
 def gram_call(kernel, name, place, *values):
@@ -130,7 +104,7 @@
         kernel,
         in_specs=[SMEM] + [VMEM] * len(values),
         out_specs=VMEM,
-        out_shape=array(7 * width + 16, width),
+        out_shape=array(4 * width + 8, width),
         compiler_params=params(12),
         cost_estimate=BRIEF,
         name=name,
@@ -176,23 +150,22 @@
     return jnp.sum((numbers == column.astype(F32)).astype(F32), axis=0, keepdims=True)
 
 
-def turn_kernel(place_ref, mine_ref, theirs_ref, turned_ref, norm_ref):
+def turn_kernel(place_ref, mine_ref, far_ref, next_ref, next_far_ref, turned_ref, norm_ref):
     width = mine_ref.shape[1]
     sign_far = jnp.where(place_ref[0] == 0, 1.0, -1.0)
     sign_next = jnp.where(place_ref[1] == 0, 1.0, -1.0)
-    mine, theirs = [
-        [ref[number * width : (number + 1) * width] for number in range(7)]
-        for ref in (mine_ref, theirs_ref)
+    refs = (mine_ref, far_ref, next_ref, next_far_ref)
+    mine, far, neighbour, next_far = [
+        [ref[number * width : (number + 1) * width] for number in range(4)] for ref in refs
     ]
-    lists = [ref[begin : begin + 1] for begin in (7 * width, 7 * width + 8) for ref in (mine_ref, theirs_ref)]
-    kept_rows = [kept_row(listed) for listed in lists]
+    kept_rows = [kept_row(ref[4 * width : 4 * width + 1]) for ref in refs]
     lo, hi = slice(0, width), slice(width, 2 * width)
-    gram_01 = symmetric(mine[4], mine[0] + theirs[0].T, theirs[4])
-    gram_23 = symmetric(mine[6], mine[3] + theirs[3].T, theirs[6])
-    gram_03 = mine[1] + theirs[2].T
-    gram_12 = mine[2].T + theirs[1]
+    gram_01 = symmetric(mine[2], mine[0].T + far[0], far[2])
+    gram_23 = symmetric(neighbour[2], neighbour[0].T + next_far[0], next_far[2])
+    gram_03 = far[1] + neighbour[1].T
+    gram_12 = mine[1] + next_far[1].T
     mixed = jnp.concatenate(
-        [jnp.concatenate([mine[5], gram_03], 1), jnp.concatenate([gram_12, theirs[5]], 1)], 0
+        [jnp.concatenate([mine[3], gram_03], 1), jnp.concatenate([gram_12, far[3]], 1)], 0
     )
     turn_01, turn_23 = rotations([gram_01, gram_23], sign_far)
     s_01, s_23 = split(turn_01), split(turn_23)
@@ -241,12 +214,12 @@
 def place_kernel(sizes, place_ref, turned_ref, route_ref, block_ref, next_ref, *rest):
     far_refs, out_ref = rest[:-1], rest[-1]
     width = block_ref.shape[1]
-    placed = []
+    moved = []
     for piece in zip(*[split(turned_ref[number]) for number in range(2)]):
-        moved = sum(dot(piece[number], route_ref[number].astype(BF16), NN) for number in range(2))
-        placed.append(moved.T.astype(BF16))
-    left = [piece[:, : 2 * width] for piece in placed]
-    right = [piece[:, 2 * width :] for piece in placed]
+        total = sum(dot(piece[number], route_ref[number].astype(BF16), NN) for number in range(2))
+        moved.append(total.astype(BF16))
+    top = [piece[: 2 * width] for piece in moved]
+    bottom = [piece[2 * width :] for piece in moved]
     pieces = len(far_refs) // 2
     done = 0
     for far_ref, next_far_ref, rows in zip(far_refs[:pieces], far_refs[pieces:], sizes):
@@ -255,7 +228,7 @@
             here = [half_rows(place_ref, ref, done, size) for ref in (block_ref, next_ref)]
             near = split(jnp.concatenate([here[0], far_ref[span]], 1))
             away = split(jnp.concatenate([here[1], next_far_ref[span]], 1))
-            out_ref[:, done : done + size] = product(left, near, NT) + product(right, away, NT)
+            out_ref[:, done : done + size] = (product(near, top, NN) + product(away, bottom, NN)).T
             done += size
 
 
@@ -353,23 +326,22 @@
     ]
     neighbour = from_partner(block, "bond", 1)
     far_a, far_b = [from_partner(piece, "bond", far) for piece in sent]
-    next_far_a = from_partner(far_a, "bond", 1)
-    grams = gram_call(first_kernel, "first_gram", place, block, neighbour, far_a, next_far_a)
-    far_b = held(grams, far_b, listed)
-    next_far_b = from_partner(far_b, "bond", 1)
+    grams = gram_call(first_kernel, "first_gram", place, block, neighbour, far_a, listed)
     grams = gram_call(
         functools.partial(last_kernel, sizes[0]),
-        "last_gram", place, block, neighbour, far_b, next_far_b, grams,
+        "last_gram", place, block, neighbour, far_b, grams,
     )
     far_grams = from_partner(grams, "bond", far)
+    next_grams = [from_partner(value, "bond", 1) for value in (grams, far_grams)]
+    next_far_a, next_far_b = [from_partner(value, "bond", 1) for value in (far_a, far_b)]
     routes = jnp.stack(
         [
             route_of(listed[0], upper, groups),
-            route_of(far_grams[7 * width], 1 - upper, groups),
+            route_of(far_grams[4 * width], 1 - upper, groups),
         ]
     )
 
-    turned, squares = turn(place, grams, far_grams)
+    turned, squares = turn(place, grams, far_grams, *next_grams)
     outgoing = placed(
         place, turned, routes, block, neighbour, (far_a, far_b), (next_far_a, next_far_b), sizes
     )

time: 152 us -> 149 us (0.980)
  waiting for transfers between devices: 28.8 us -> 20.2 us
  starting transfers between devices: 25 us -> 29.5 us
  blocking collectives: 70.3 us -> 72.8 us
  Pallas kernels: 22.8 us -> 20.5 us
    ppermute x8 -> x10, waiting for transfers between devices: 28.8 us -> 20.2 us  [from_partner(): return lax.ppermute(value, axis, pairs)]
    ppermute x8 -> x10, starting transfers between devices: 25 us -> 29.5 us  [from_partner(): return lax.ppermute(value, axis, pairs)]
    all_to_all x1, blocking collectives: 70.3 us -> 72.8 us  [on_device(): lax.all_to_all(spread(outgoing, squares, float(rows * count * keep_count)...]
  transfers between devices with their start and end apart: 8 -> 10, of which waited for: 6 -> 4; matrix products, arithmetic and copies ran while one was open for 3% -> 3% of each run, Pallas kernels for 5% -> 11%
where the time goes in v3:
time: 149 us; the launch traced here: 148 us
  blocking collectives  72.8 us (49%)
  starting transfers between devices  29.5 us (20%)
  Pallas kernels  20.5 us (14%)
  waiting for transfers between devices  20.2 us (14%)
  local copies, waits for them, and re-layouts  3.2 us (2%)
    all_to_all x1, blocking collectives, on_device(): lax.all_to_all(spread(outgoing, squares, float(rows * count * keep_count)...  72.8 us
    ppermute x10, starting transfers between devices, from_partner(): return lax.ppermute(value, axis, pairs)  29.5 us
    ppermute x10, waiting for transfers between devices, from_partner(): return lax.ppermute(value, axis, pairs)  20.2 us
    pallas_call x1, Pallas kernels, turn(): pl.pallas_call(turn_kernel, in_specs=[SMEM] + [VMEM] * len(values), out_s...  9.52 us
    pallas_call x2, Pallas kernels, gram_call(): pl.pallas_call(kernel, in_specs=[SMEM] + [VMEM] * len(values), out_specs=...  4.86 us
    pallas_call x1, Pallas kernels, placed(): pl.pallas_call(functools.partial(place_kernel, sizes), in_specs=[SMEM] +...  3.96 us
    dynamic_slice x2, local copies, waits for them, and re-layouts, on_device(): lax.dynamic_slice_in_dim(source, start, size)  3.04 us
  transfers between devices with their start and end apart: 10, of which 4 were waited for; matrix products, arithmetic and copies ran while one was open for 3% of the time, Pallas kernels for 11%

profile of v3, /device:TPU:56, one launch (start us, length us, event | category | flops | bytes accessed | tf_op | source)
XLA Modules:
  0.0 147.7 jit_solution(14448851036067540974)
XLA Ops:
  0.0 0.0 copy-start
  0.0 0.0 copy-start.1
  0.0 0.0 copy-start.2
  0.0 2.1 %collective-permute-start = (f32[4096,128]{1,0:T(8,128)}, f32[4096,128]{1,0:T(8,128)}, u32[]{:S(2)}, u32[]{:S(2)}) collective-permute-start(f32[4096,128]{1,0:T(8,128)} %bitcast.19), channel_id=1, source_target_pairs={{0,32},{32,0},{64,96},{96,64},{128,160},{160,128},{192,224},{224,1... | collective-permute-start | bytes 6291464 | tf_op jit(solution)/shard_map/ppermute | solution.py:289
  2.1 2.1 %dynamic-slice_bitcast_fusion = f32[1536,128]{1,0:T(8,128)} fusion(f32[1,4096,128]{2,1,0:T(8,128)} %param.3, s32[]{:T(128)S(6)} %select_n.13), kind=kLoop, calls=%fused_computation.2 | loop fusion | bytes 1572868 | tf_op jit(solution)/shard_map/dynamic_slice | solution.py:324
  4.2 4.9 %collective-permute-start.2 = (f32[1536,128]{1,0:T(8,128)}, f32[1536,128]{1,0:T(8,128)S(1)}, u32[]{:S(2)}, u32[]{:S(2)}) collective-permute-start(f32[1536,128]{1,0:T(8,128)} %dynamic-slice_bitcast_fusion), channel_id=1, source_target_pairs={{0,256},{32,288},{64,320},{96,352},{128,384},{160,416},{192,448},{... | collective-permute-start | bytes 2359304 | tf_op jit(solution)/shard_map/ppermute | solution.py:289
  9.1 1.0 constant_dynamic-slice_fusion
  10.1 2.4 %collective-permute-start.1 = (f32[512,128]{1,0:T(8,128)S(1)}, f32[512,128]{1,0:T(8,128)S(1)}, u32[]{:S(2)}, u32[]{:S(2)}) collective-permute-start(f32[512,128]{1,0:T(8,128)S(1)} %constant_dynamic-slice_fusion), channel_id=1, source_target_pairs={{0,256},{32,288},{64,320},{96,352},{128,384},{160,416},{192,448},{... | collective-permute-start | bytes 786440 | tf_op jit(solution)/shard_map/ppermute | solution.py:289
  12.5 0.0 copy-done.1
  12.5 0.0 copy-done.2
  12.5 0.1 fusion.6
  12.6 0.1 unstack.19
  12.7 0.1 pad_add_fusion.place_ref
  12.7 0.2 convert_reduce_fusion.1
  12.9 15.2 %collective-permute-done.2.far_ref.rest_0_ = f32[1536,128]{1,0:T(8,128)S(1)} collective-permute-done((f32[1536,128]{1,0:T(8,128)}, f32[1536,128]{1,0:T(8,128)S(1)}, u32[]{:S(2)}, u32[]{:S(2)}) %collective-permute-start.2) | collective-permute-done | bytes 786464 | tf_op jit(solution)/shard_map/ppermute | solution.py:289
  28.1 0.0 collective-permute-done.next_ref
  28.1 0.0 copy-done
  28.1 2.9 %first_gram.1.before_ref = f32[520,128]{1,0:T(8,128)S(1)} custom-call(s32[2]{0:T(128)S(1)} %pad_add_fusion.place_ref, f32[4096,128]{1,0:T(8,128)S(1)} %bitcast.21, f32[4096,128]{1,0:T(8,128)} %collective-permute-done.next_ref, f32[1536,128]{1,0:T(8,128)S(1)} %collective-permute-done.2.far_ref.rest_0_, f32[8,128]{1,0:T(8,128)S(1)} %broadcast_in_dim.2.listed_ref), custom_call_target="tpu_custom_call" | custom-call | flops 1 | bytes 1 | tf_op jit(solution)/shard_map/first_gram/pallas_call | solution.py:103
  31.1 2.3 %collective-permute-done.1.far_ref.rest_1_ = f32[512,128]{1,0:T(8,128)S(1)} collective-permute-done((f32[512,128]{1,0:T(8,128)S(1)}, f32[512,128]{1,0:T(8,128)S(1)}, u32[]{:S(2)}, u32[]{:S(2)}) %collective-permute-start.1) | collective-permute-done | bytes 262176 | tf_op jit(solution)/shard_map/ppermute | solution.py:289
  33.3 1.9 %last_gram.1.mine_ref = f32[520,128]{1,0:T(8,128)S(1)} custom-call(s32[2]{0:T(128)S(1)} %pad_add_fusion.place_ref, f32[4096,128]{1,0:T(8,128)S(1)} %bitcast.22, f32[4096,128]{1,0:T(8,128)} %collective-permute-done.next_ref, f32[512,128]{1,0:T(8,128)S(1)} %collective-permute-done.1.far_ref.rest_1_, f32[520,128]{1,0:T(8,128)S(1)} %first_gram.1.before_ref), custom_call_target="tpu_custom_call" | custom-call | flops 1 | bytes 1 | tf_op jit(solution)/shard_map/last_gram/pallas_call | solution.py:103
  35.2 4.9 %collective-permute-start.3 = (f32[520,128]{1,0:T(8,128)S(1)}, f32[520,128]{1,0:T(8,128)S(1)}, u32[]{:S(2)}, u32[]{:S(2)}) collective-permute-start(f32[520,128]{1,0:T(8,128)S(1)} %last_gram.1.mine_ref), channel_id=1, source_target_pairs={{0,256},{32,288},{64,320},{96,352},{128,384},{160,416},{192,448},{... | collective-permute-start | bytes 798728 | tf_op jit(solution)/shard_map/ppermute | solution.py:289
  40.2 0.1 fusion.7
  40.3 0.3 convolution_bitcast_fusion.1
  40.6 1.9 %collective-permute-start.7 = (f32[512,128]{1,0:T(8,128)S(1)}, f32[512,128]{1,0:T(8,128)S(1)}, u32[]{:S(2)}, u32[]{:S(2)}) collective-permute-start(f32[512,128]{1,0:T(8,128)S(1)} %collective-permute-done.1.far_ref.rest_1_), channel_id=1, source_target_pairs={{0,32},{32,0},{64,96},{96,64},{128,160},{160,128},{192,224},{224,1... | collective-permute-start | bytes 786440 | tf_op jit(solution)/shard_map/ppermute | solution.py:289
  42.5 2.4 %collective-permute-start.6 = (f32[1536,128]{1,0:T(8,128)S(1)}, f32[1536,128]{1,0:T(8,128)S(1)}, u32[]{:S(2)}, u32[]{:S(2)}) collective-permute-start(f32[1536,128]{1,0:T(8,128)S(1)} %collective-permute-done.2.far_ref.rest_0_), channel_id=1, source_target_pairs={{0,32},{32,0},{64,96},{96,64},{128,160},{160,128},{192,224},{224,1... | collective-permute-start | bytes 2359304 | tf_op jit(solution)/shard_map/ppermute | solution.py:289
  44.9 1.9 %collective-permute-start.4 = (f32[520,128]{1,0:T(8,128)S(1)}, f32[520,128]{1,0:T(8,128)S(1)}, u32[]{:S(2)}, u32[]{:S(2)}) collective-permute-start(f32[520,128]{1,0:T(8,128)S(1)} %last_gram.1.mine_ref), channel_id=1, source_target_pairs={{0,32},{32,0},{64,96},{96,64},{128,160},{160,128},{192,224},{224,1... | collective-permute-start | bytes 798728 | tf_op jit(solution)/shard_map/ppermute | solution.py:289
  46.8 0.0 collective-permute-done.3.far_ref
  46.8 2.4 %collective-permute-start.5 = (f32[520,128]{1,0:T(8,128)S(1)}, f32[520,128]{1,0:T(8,128)S(1)}, u32[]{:S(2)}, u32[]{:S(2)}) collective-permute-start(f32[520,128]{1,0:T(8,128)S(1)} %collective-permute-done.3.far_ref), channel_id=1, source_target_pairs={{0,32},{32,0},{64,96},{96,64},{128,160},{160,128},{192,224},{224,1... | collective-permute-start | bytes 798728 | tf_op jit(solution)/shard_map/ppermute | solution.py:289
  49.3 0.1 slice_bitcast_fusion.1
  49.3 0.2 convert_reduce_fusion
  49.5 0.1 multiply_add_fusion
  49.6 0.3 convolution_bitcast_fusion
  49.9 0.0 collective-permute-done.4.next_ref
  49.9 0.5 collective-permute-done.5.next_far_ref
  50.4 9.5 %turn.1 = (f32[2,512,128]{2,1,0:T(8,128)S(1)}, f32[8,128]{1,0:T(8,128)S(1)}) custom-call(s32[2]{0:T(128)S(1)} %pad_add_fusion.place_ref, f32[520,128]{1,0:T(8,128)S(1)} %last_gram.1.mine_ref, f32[520,128]{1,0:T(8,128)S(1)} %collective-permute-done.3.far_ref, f32[520,128]{1,0:T(8,128)S(1)} %collective-permute-done.4.next_ref, ...), custom_call_target="tpu_custom_call" | custom-call | tf_op jit(solution)/shard_map/turn/pallas_call | solution.py:204
  59.9 3.3 %collective-permute-start.8 = (f32[8,128]{1,0:T(8,128)S(1)}, f32[8,128]{1,0:T(8,128)S(1)}, u32[]{:S(2)}, u32[]{:S(2)}) collective-permute-start(f32[8,128]{1,0:T(8,128)S(1)} %get-tuple-element.8), channel_id=1, source_target_pairs={{0,64},{32,96},{64,0},{96,32},{128,192},{160,224},{192,128},{224,1... | collective-permute-start | bytes 12296 | tf_op jit(solution)/shard_map/ppermute | solution.py:289
  63.2 2.2 %collective-permute-done.8 = f32[8,128]{1,0:T(8,128)S(1)} collective-permute-done((f32[8,128]{1,0:T(8,128)S(1)}, f32[8,128]{1,0:T(8,128)S(1)}, u32[]{:S(2)}, u32[]{:S(2)}) %collective-permute-start.8) | collective-permute-done | bytes 4128 | tf_op jit(solution)/shard_map/ppermute | solution.py:289
  65.4 3.2 %collective-permute-start.9 = (f32[8,128]{1,0:T(8,128)S(1)}, f32[8,128]{1,0:T(8,128)S(1)}, u32[]{:S(2)}, u32[]{:S(2)}) collective-permute-start(f32[8,128]{1,0:T(8,128)S(1)} %add.53), channel_id=1, source_target_pairs={{0,128},{32,160},{64,192},{96,224},{128,0},{160,32},{192,64},{224,... | collective-permute-start | bytes 12296 | tf_op jit(solution)/shard_map/ppermute | solution.py:289
  68.7 0.0 collective-permute-done.7.rest_3_
  68.7 0.0 collective-permute-done.6.rest_2_
  68.7 4.0 %placed.1.kept_ref = f32[256,2048]{1,0:T(8,128)S(1)} custom-call(s32[2]{0:T(128)S(1)} %pad_add_fusion.place_ref, f32[2,512,128]{2,1,0:T(8,128)S(1)} %get-tuple-element.7.turned_ref, f32[2,128,256]{2,1,0:T(8,128)S(1)} %pad_maximum_fusion.route_ref, f32[4096,128]{1,0:T(8,128)S(1)} %bitcast.23, f32[4096,128]{1,0:T(8,128)} %collective-permute-done.next_ref, ...), custom_call_target="tpu_custom_call" | custom-call | flops 1610612736 | bytes 4194304 | tf_op jit(solution)/shard_map/placed/pallas_call | solution.py:238
  72.7 0.0 collective-permute-done.9
  72.7 0.6 spread.1
  73.3 72.8 %all_to_all.5 = f32[64,16,4,128]{3,2,1,0:T(4,128)S(1)} all-to-all(f32[64,16,4,128]{3,2,1,0:T(4,128)S(1)} %spread.1), channel_id=1, replica_groups={{0,256,1,257,2,258,3,259,4,260,5,261,6,262,7,263,8,264,9,265,10,266,11,..., dimensions={0} | all-to-all | bytes 4194304 | tf_op jit(solution)/shard_map/all_to_all | solution.py:356
  146.1 1.5 %join.1 = f32[32,4,4096]{2,1,0:T(4,128)} custom-call(f32[32,32,4,128]{3,2,1,0:T(4,128)S(1)} %bitcast.24), custom_call_target="tpu_custom_call" | custom-call | tf_op jit(solution)/shard_map/join/pallas_call | solution.py:277
  (5 shorter events, 0.0 us)
Async XLA Ops:
  0.0 28.1 %copy-start = (f32[1,4096,128]{2,1,0:T(8,128)S(1)}, f32[1,4096,128]{2,1,0:T(8,128)}, u32[]{:S(2)}) copy-start(f32[1,4096,128]{2,1,0:T(8,128)} %param.3) | copy-start | bytes 6291460
  0.0 12.5 %copy-start.1 = (s32[1,64,1]{1,2,0:T(1,128)S(1)}, s32[1,64,1]{1,2,0:T(1,128)}, u32[]{:S(2)}) copy-start(s32[1,64,1]{1,2,0:T(1,128)} %param.5) | copy-start | bytes 772
  0.0 12.5 %copy-start.2 = (s32[1,64]{1,0:T(1,128)S(1)}, s32[1,64]{1,0:T(1,128)}, u32[]{:S(2)}) copy-start(s32[1,64]{1,0:T(1,128)} %param.4) | copy-start | bytes 772
  0.0 28.1 %collective-permute-start = (f32[4096,128]{1,0:T(8,128)}, f32[4096,128]{1,0:T(8,128)}, u32[]{:S(2)}, u32[]{:S(2)}) collective-permute-start(f32[4096,128]{1,0:T(8,128)} %bitcast.19), channel_id=1, source_target_pairs={{0,32},{32,0},{64,96},{96,64},{128,160},{160,128},{192,224},{224,1... | collective-permute-start | bytes 6291464 | tf_op jit(solution)/shard_map/ppermute | solution.py:289
  4.2 23.9 %collective-permute-start.2 = (f32[1536,128]{1,0:T(8,128)}, f32[1536,128]{1,0:T(8,128)S(1)}, u32[]{:S(2)}, u32[]{:S(2)}) collective-permute-start(f32[1536,128]{1,0:T(8,128)} %dynamic-slice_bitcast_fusion), channel_id=1, source_target_pairs={{0,256},{32,288},{64,320},{96,352},{128,384},{160,416},{192,448},{... | collective-permute-start | bytes 2359304 | tf_op jit(solution)/shard_map/ppermute | solution.py:289
  10.1 23.2 %collective-permute-start.1 = (f32[512,128]{1,0:T(8,128)S(1)}, f32[512,128]{1,0:T(8,128)S(1)}, u32[]{:S(2)}, u32[]{:S(2)}) collective-permute-start(f32[512,128]{1,0:T(8,128)S(1)} %constant_dynamic-slice_fusion), channel_id=1, source_target_pairs={{0,256},{32,288},{64,320},{96,352},{128,384},{160,416},{192,448},{... | collective-permute-start | bytes 786440 | tf_op jit(solution)/shard_map/ppermute | solution.py:289
  35.2 11.6 %collective-permute-start.3 = (f32[520,128]{1,0:T(8,128)S(1)}, f32[520,128]{1,0:T(8,128)S(1)}, u32[]{:S(2)}, u32[]{:S(2)}) collective-permute-start(f32[520,128]{1,0:T(8,128)S(1)} %last_gram.1.mine_ref), channel_id=1, source_target_pairs={{0,256},{32,288},{64,320},{96,352},{128,384},{160,416},{192,448},{... | collective-permute-start | bytes 798728 | tf_op jit(solution)/shard_map/ppermute | solution.py:289
  40.6 28.1 %collective-permute-start.7 = (f32[512,128]{1,0:T(8,128)S(1)}, f32[512,128]{1,0:T(8,128)S(1)}, u32[]{:S(2)}, u32[]{:S(2)}) collective-permute-start(f32[512,128]{1,0:T(8,128)S(1)} %collective-permute-done.1.far_ref.rest_1_), channel_id=1, source_target_pairs={{0,32},{32,0},{64,96},{96,64},{128,160},{160,128},{192,224},{224,1... | collective-permute-start | bytes 786440 | tf_op jit(solution)/shard_map/ppermute | solution.py:289
  42.5 26.2 %collective-permute-start.6 = (f32[1536,128]{1,0:T(8,128)S(1)}, f32[1536,128]{1,0:T(8,128)S(1)}, u32[]{:S(2)}, u32[]{:S(2)}) collective-permute-start(f32[1536,128]{1,0:T(8,128)S(1)} %collective-permute-done.2.far_ref.rest_0_), channel_id=1, source_target_pairs={{0,32},{32,0},{64,96},{96,64},{128,160},{160,128},{192,224},{224,1... | collective-permute-start | bytes 2359304 | tf_op jit(solution)/shard_map/ppermute | solution.py:289
  44.9 5.0 %collective-permute-start.4 = (f32[520,128]{1,0:T(8,128)S(1)}, f32[520,128]{1,0:T(8,128)S(1)}, u32[]{:S(2)}, u32[]{:S(2)}) collective-permute-start(f32[520,128]{1,0:T(8,128)S(1)} %last_gram.1.mine_ref), channel_id=1, source_target_pairs={{0,32},{32,0},{64,96},{96,64},{128,160},{160,128},{192,224},{224,1... | collective-permute-start | bytes 798728 | tf_op jit(solution)/shard_map/ppermute | solution.py:289
  46.8 3.6 %collective-permute-start.5 = (f32[520,128]{1,0:T(8,128)S(1)}, f32[520,128]{1,0:T(8,128)S(1)}, u32[]{:S(2)}, u32[]{:S(2)}) collective-permute-start(f32[520,128]{1,0:T(8,128)S(1)} %collective-permute-done.3.far_ref), channel_id=1, source_target_pairs={{0,32},{32,0},{64,96},{96,64},{128,160},{160,128},{192,224},{224,1... | collective-permute-start | bytes 798728 | tf_op jit(solution)/shard_map/ppermute | solution.py:289
  59.9 5.5 %collective-permute-start.8 = (f32[8,128]{1,0:T(8,128)S(1)}, f32[8,128]{1,0:T(8,128)S(1)}, u32[]{:S(2)}, u32[]{:S(2)}) collective-permute-start(f32[8,128]{1,0:T(8,128)S(1)} %get-tuple-element.8), channel_id=1, source_target_pairs={{0,64},{32,96},{64,0},{96,32},{128,192},{160,224},{192,128},{224,1... | collective-permute-start | bytes 12296 | tf_op jit(solution)/shard_map/ppermute | solution.py:289
  65.4 7.2 %collective-permute-start.9 = (f32[8,128]{1,0:T(8,128)S(1)}, f32[8,128]{1,0:T(8,128)S(1)}, u32[]{:S(2)}, u32[]{:S(2)}) collective-permute-start(f32[8,128]{1,0:T(8,128)S(1)} %add.53), channel_id=1, source_target_pairs={{0,128},{32,160},{64,192},{96,224},{128,0},{160,32},{192,64},{224,... | collective-permute-start | bytes 12296 | tf_op jit(solution)/shard_map/ppermute | solution.py:289

commit v4 on v3

--- a/solution.py
+++ b/solution.py
@@ -64,35 +64,48 @@
     return ref[pl.ds(pl.multiple_of(place_ref[0] * half, half) + start, size)]
 
 
-def cross_products(place_ref, own_ref, next_ref, far_ref, start):
+def half_rows_of(place_ref, refs, start, size):
+    rows = refs[0].shape[0]
+    side = len(refs) // 2
+    piece, first = start // rows, start % rows
+    span = slice(first, first + size)
+    return jnp.where(place_ref[0] == 0, refs[piece][span], refs[side + piece][span])
+
+
+def cross_products(place_ref, own_ref, next_refs, far_ref, start):
     rows, width = far_ref.shape
     total = jnp.zeros((width, 2 * width), F32)
     for span in tiles(rows):
         first, size = start + span.start, span.stop - span.start
-        here = [half_rows(place_ref, ref, first, size) for ref in (own_ref, next_ref)]
+        here = [
+            half_rows(place_ref, own_ref, first, size),
+            half_rows_of(place_ref, next_refs, first, size),
+        ]
         total += product(split(far_ref[span]), split(jnp.concatenate(here, 1)), TN)
     return total
 
 
-def first_kernel(place_ref, own_ref, next_ref, far_ref, listed_ref, out_ref):
+def first_kernel(place_ref, own_ref, far_ref, listed_ref, *rest):
+    next_refs, out_ref = rest[:-1], rest[-1]
     rows, width = own_ref.shape
-    chunk = min(1024, rows)
+    chunk = rows // len(next_refs)
     total = jnp.zeros((width, 2 * width), F32)
-    for begin in range(0, rows, chunk):
-        span = slice(begin, begin + chunk)
-        own, neighbour = split(own_ref[span]), split(next_ref[span])
+    for number, next_ref in enumerate(next_refs):
+        span = slice(number * chunk, (number + 1) * chunk)
+        own, neighbour = split(own_ref[span]), split(next_ref[...])
         pair = [jnp.concatenate([a, b], 1) for a, b in zip(own, neighbour)]
         total += product(own, pair, TN)
-    cross = cross_products(place_ref, own_ref, next_ref, far_ref, 0)
+    cross = cross_products(place_ref, own_ref, next_refs, far_ref, 0)
     for number, part in enumerate([cross, total]):
         out_ref[2 * number * width : (2 * number + 1) * width] = part[:, :width]
         out_ref[(2 * number + 1) * width : (2 * number + 2) * width] = part[:, width:]
     out_ref[4 * width :] = listed_ref[...]
 
 
-def last_kernel(start, place_ref, own_ref, next_ref, far_ref, before_ref, out_ref):
+def last_kernel(start, place_ref, own_ref, far_ref, before_ref, *rest):
+    next_refs, out_ref = rest[:-1], rest[-1]
     width = own_ref.shape[1]
-    cross = cross_products(place_ref, own_ref, next_ref, far_ref, start)
+    cross = cross_products(place_ref, own_ref, next_refs, far_ref, start)
     out_ref[:width] = before_ref[:width] + cross[:, :width]
     out_ref[width : 2 * width] = before_ref[width : 2 * width] + cross[:, width:]
     out_ref[2 * width :] = before_ref[2 * width :]
@@ -211,8 +224,9 @@
     )(place, *values)
 
 
-def place_kernel(sizes, place_ref, turned_ref, route_ref, block_ref, next_ref, *rest):
-    far_refs, out_ref = rest[:-1], rest[-1]
+def place_kernel(spans, count, place_ref, turned_ref, route_ref, block_ref, *rest):
+    next_refs, rest = rest[:count], rest[count:]
+    far_refs, next_far_refs, out_ref = rest[: len(spans)], rest[len(spans) : 2 * len(spans)], rest[-1]
     width = block_ref.shape[1]
     moved = []
     for piece in zip(*[split(turned_ref[number]) for number in range(2)]):
@@ -220,24 +234,27 @@
         moved.append(total.astype(BF16))
     top = [piece[: 2 * width] for piece in moved]
     bottom = [piece[2 * width :] for piece in moved]
-    pieces = len(far_refs) // 2
     done = 0
-    for far_ref, next_far_ref, rows in zip(far_refs[:pieces], far_refs[pieces:], sizes):
-        for span in tiles(rows):
-            size = span.stop - span.start
-            here = [half_rows(place_ref, ref, done, size) for ref in (block_ref, next_ref)]
-            near = split(jnp.concatenate([here[0], far_ref[span]], 1))
-            away = split(jnp.concatenate([here[1], next_far_ref[span]], 1))
+    for far_ref, next_far_ref, (start, span) in zip(far_refs, next_far_refs, spans):
+        for tile in tiles(span.stop - span.start):
+            size = tile.stop - tile.start
+            there = slice(span.start + tile.start, span.start + tile.stop)
+            here = [
+                half_rows(place_ref, block_ref, start + tile.start, size),
+                half_rows_of(place_ref, next_refs, start + tile.start, size),
+            ]
+            near = split(jnp.concatenate([here[0], far_ref[there]], 1))
+            away = split(jnp.concatenate([here[1], next_far_ref[there]], 1))
             out_ref[:, done : done + size] = (product(near, top, NN) + product(away, bottom, NN)).T
             done += size
 
 
-def placed(place, turned, routes, own, neighbour, far, next_far, sizes):
+def placed(place, turned, routes, own, neighbour, far, next_far, spans, first=()):
     width = own.shape[1]
-    rows = sum(sizes)
+    rows = sum(span.stop - span.start for _, span in spans)
     return pl.pallas_call(
-        functools.partial(place_kernel, sizes),
-        in_specs=[SMEM] + [VMEM] * (4 + 2 * len(far)),
+        functools.partial(place_kernel, spans, len(neighbour)),
+        in_specs=[SMEM] + [VMEM] * (3 + len(neighbour) + 2 * len(far)) + [ANY] * len(first),
         out_specs=VMEM,
         out_shape=array(routes.shape[2], rows),
         compiler_params=params(16),
@@ -245,31 +262,36 @@
             flops=48 * rows * width * width, bytes_accessed=16 * rows * width, transcendentals=0
         ),
         name="placed",
-    )(place, turned, routes, own, neighbour, *far, *next_far)
-
-
-def spread_kernel(total, kept_ref, norm_ref, out_ref):
+    )(place, turned, routes, own, *neighbour, *far, *next_far, *first)
+
+
+def spread_kernel(total, *refs):
+    norm_ref, out_ref = refs[-2:]
     scale = jnp.sqrt(total / norm_ref[0:1, 0:1])
-    for tile in range(out_ref.shape[1]):
-        value = kept_ref[:, tile * LANES : (tile + 1) * LANES] * scale
-        out_ref[:, tile] = value.reshape(out_ref.shape[0], out_ref.shape[2], LANES)
-
-
-def spread(kept, norm, total, capacity):
-    shape = (kept.shape[0] // capacity, kept.shape[1] // LANES, capacity, LANES)
+    done = 0
+    for ref in refs[:-2]:
+        for tile in range(ref.shape[1] // LANES):
+            value = ref[:, tile * LANES : (tile + 1) * LANES] * scale
+            out_ref[:, done] = value.reshape(out_ref.shape[0], out_ref.shape[2], LANES)
+            done += 1
+
+
+def spread(values, norm, total, capacity):
+    count = sum(value.shape[1] for value in values) // LANES
     return pl.pallas_call(
         functools.partial(spread_kernel, total),
-        in_specs=[VMEM, VMEM],
+        in_specs=[VMEM] * (len(values) + 1),
         out_specs=VMEM,
-        out_shape=array(*shape),
+        out_shape=array(values[0].shape[0] // capacity, count, capacity, LANES),
         compiler_params=params(8),
         name="spread",
-    )(kept, norm)
+    )(*values, norm)
 
 
 def join_kernel(tiles_ref, out_ref):
-    for tile in range(tiles_ref.shape[1]):
-        out_ref[:, :, tile * LANES : (tile + 1) * LANES] = tiles_ref[:, tile]
+    for member, site in enumerate(member_order(tiles_ref.shape[0])):
+        for tile in range(tiles_ref.shape[1]):
+            out_ref[site, :, tile * LANES : (tile + 1) * LANES] = tiles_ref[member, tile]
 
 
 def join(tiles):
@@ -289,6 +311,17 @@
     return lax.ppermute(value, axis, pairs)
 
 
+def member_order(groups):
+    if groups % 32:
+        return list(range(groups))
+    return [
+        16 * high + 8 * low + z
+        for high in range(groups // 16)
+        for z in range(8)
+        for low in range(2)
+    ]
+
+
 def route_of(listed, side, groups):
     width = listed.shape[0]
     kept = width // 2
@@ -297,7 +330,12 @@
     same = owners[:, None] == owners[None, :]
     slot = jnp.sum((same & (order[None, :] < order[:, None])).astype(jnp.int32), axis=1)
     capacity = max(2, 2 * kept // groups)
-    target = (owners * 2 + side) * capacity + slot
+    order_of = member_order(groups)
+    rank = jnp.array([order_of.index(site) for site in range(groups)], jnp.int32)
+    ranks = jnp.sum(
+        jnp.where(owners[:, None] == jnp.arange(groups, dtype=jnp.int32), rank, 0), axis=1
+    )
+    target = (ranks * 2 + side) * capacity + slot
     places = jnp.arange(2 * groups * capacity, dtype=jnp.int32)
     columns = jnp.arange(width, dtype=jnp.int32)
     picked = (keep[:, None] == columns[None, :]).astype(BF16)
@@ -324,12 +362,16 @@
         lax.dynamic_slice_in_dim(source, start, size)
         for source, start, size in zip(sources, starts, sizes)
     ]
-    neighbour = from_partner(block, "bond", 1)
+    quarter = rows // 4
+    neighbour = [
+        from_partner(block[number * quarter : (number + 1) * quarter], "bond", 1)
+        for number in range(4)
+    ]
     far_a, far_b = [from_partner(piece, "bond", far) for piece in sent]
-    grams = gram_call(first_kernel, "first_gram", place, block, neighbour, far_a, listed)
+    grams = gram_call(first_kernel, "first_gram", place, block, far_a, listed, *neighbour)
     grams = gram_call(
         functools.partial(last_kernel, sizes[0]),
-        "last_gram", place, block, neighbour, far_b, grams,
+        "last_gram", place, block, far_b, grams, *neighbour,
     )
     far_grams = from_partner(grams, "bond", far)
     next_grams = [from_partner(value, "bond", 1) for value in (grams, far_grams)]
@@ -342,15 +384,27 @@
     )
 
     turned, squares = turn(place, grams, far_grams, *next_grams)
-    outgoing = placed(
-        place, turned, routes, block, neighbour, (far_a, far_b), (next_far_a, next_far_b), sizes
-    )
-    for distance in [1 << bit for bit in range(1, far.bit_length() - 1)]:
+    middle = sizes[0] * 2 // 3
+    outgoing = [
+        placed(
+            place, turned, routes, block, neighbour, (far_a,), (next_far_a,),
+            ((0, slice(0, middle)),),
+        )
+    ]
+    squares = squares + from_partner(squares, "bond", 2)
+    outgoing.append(
+        placed(
+            place, turned, routes, block, neighbour, (far_a, far_b), (next_far_a, next_far_b),
+            ((middle, slice(middle, sizes[0])), (sizes[0], slice(0, sizes[1]))), (squares,),
+        )
+    )
+    for distance in [1 << bit for bit in range(2, far.bit_length() - 1)]:
         squares = squares + from_partner(squares, "bond", distance)
     keep_count = keep_list.shape[1]
     capacity = max(2, 2 * keep_count // groups)
+    order = member_order(groups)
     members = [
-        [(first + far * side) * groups + site for site in range(groups) for side in range(2)]
+        [(first + far * side) * groups + site for site in order for side in range(2)]
         for first in range(far)
     ]
     arrived = lax.all_to_all(

time: 149 us -> 151 us (1.013)
  the two profiles are of different devices: /device:TPU:56 before, /device:TPU:70 now
where the time goes in v4:
time: 151 us
  blocking collectives  75.4 us (50%)
  starting transfers between devices  33.8 us (22%)
  Pallas kernels  21.9 us (15%)
  waiting for transfers between devices  12.1 us (8%)
  local copies, waits for them, and re-layouts  5.8 us (4%)
    all_to_all x1, blocking collectives, on_device(): lax.all_to_all(spread(outgoing, squares, float(rows * count * keep_count)...  75.4 us
    ppermute x13, starting transfers between devices, from_partner(): return lax.ppermute(value, axis, pairs)  33.8 us
    ppermute x13, waiting for transfers between devices, from_partner(): return lax.ppermute(value, axis, pairs)  12.1 us
    pallas_call x1, Pallas kernels, turn(): pl.pallas_call(turn_kernel, in_specs=[SMEM] + [VMEM] * len(values), out_s...  9.52 us
    pallas_call x2, Pallas kernels, placed(): pl.pallas_call(functools.partial(place_kernel, spans, len(neighbour)), in...  5.98 us
    pallas_call x2, Pallas kernels, gram_call(): pl.pallas_call(kernel, in_specs=[SMEM] + [VMEM] * len(values), out_specs=...  4.33 us
  transfers between devices with their start and end apart: 13, of which 6 were waited for; matrix products, arithmetic and copies ran while one was open for 3% of the time, Pallas kernels for 10%

profile of v4, /device:TPU:70, one launch (start us, length us, event | category | flops | bytes accessed | tf_op | source)
XLA Modules:
  0.0 150.5 jit_solution(5927886376795879567)
XLA Ops:
  0.0 2.1 %dynamic-slice_bitcast_fusion = f32[1536,128]{1,0:T(8,128)} fusion(f32[1,4096,128]{2,1,0:T(8,128)} %param.5, s32[]{:T(128)S(6)} %select_n.20), kind=kLoop, calls=%fused_computation.2 | loop fusion | bytes 1572868 | tf_op jit(solution)/shard_map/dynamic_slice | solution.py:362
  2.1 3.4 %collective-permute-start.1 = (f32[1536,128]{1,0:T(8,128)}, f32[1536,128]{1,0:T(8,128)}, u32[]{:S(2)}, u32[]{:S(2)}) collective-permute-start(f32[1536,128]{1,0:T(8,128)} %dynamic-slice_bitcast_fusion), channel_id=1, source_target_pairs={{0,256},{32,288},{64,320},{96,352},{128,384},{160,416},{192,448},{... | collective-permute-start | bytes 2359304 | tf_op jit(solution)/shard_map/ppermute | solution.py:311
  5.5 2.9 %slice_bitcast_fusion = (f32[1024,128]{1,0:T(8,128)}, f32[1024,128]{1,0:T(8,128)}, f32[1024,128]{1,0:T(8,128)}, f32[1024,128]{1,0:T(8,128)}) fusion(f32[1,4096,128]{2,1,0:T(8,128)} %param.5), kind=kLoop, calls=%fused_computation.3 | loop fusion | bytes 4194304 | tf_op jit(solution)/shard_map/slice | solution.py:367
  8.4 1.9 %collective-permute-start.5 = (f32[1024,128]{1,0:T(8,128)}, f32[1024,128]{1,0:T(8,128)S(1)}, u32[]{:S(2)}, u32[]{:S(2)}) collective-permute-start(f32[1024,128]{1,0:T(8,128)} %get-tuple-element.13), channel_id=1, source_target_pairs={{0,32},{32,0},{64,96},{96,64},{128,160},{160,128},{192,224},{224,1... | collective-permute-start | bytes 1572872 | tf_op jit(solution)/shard_map/ppermute | solution.py:311
  10.3 2.4 %collective-permute-start.3 = (f32[1024,128]{1,0:T(8,128)}, f32[1024,128]{1,0:T(8,128)S(1)}, u32[]{:S(2)}, u32[]{:S(2)}) collective-permute-start(f32[1024,128]{1,0:T(8,128)} %get-tuple-element.14), channel_id=1, source_target_pairs={{0,32},{32,0},{64,96},{96,64},{128,160},{160,128},{192,224},{224,1... | collective-permute-start | bytes 1572872 | tf_op jit(solution)/shard_map/ppermute | solution.py:311
  12.7 1.9 %collective-permute-start.2 = (f32[1024,128]{1,0:T(8,128)}, f32[1024,128]{1,0:T(8,128)}, u32[]{:S(2)}, u32[]{:S(2)}) collective-permute-start(f32[1024,128]{1,0:T(8,128)} %get-tuple-element.15), channel_id=1, source_target_pairs={{0,32},{32,0},{64,96},{96,64},{128,160},{160,128},{192,224},{224,1... | collective-permute-start | bytes 1572872 | tf_op jit(solution)/shard_map/ppermute | solution.py:311
  14.6 2.4 %collective-permute-start.4 = (f32[1024,128]{1,0:T(8,128)}, f32[1024,128]{1,0:T(8,128)}, u32[]{:S(2)}, u32[]{:S(2)}) collective-permute-start(f32[1024,128]{1,0:T(8,128)} %get-tuple-element.16), channel_id=1, source_target_pairs={{0,32},{32,0},{64,96},{96,64},{128,160},{160,128},{192,224},{224,1... | collective-permute-start | bytes 1572872 | tf_op jit(solution)/shard_map/ppermute | solution.py:311
  17.1 0.7 constant_dynamic-slice_fusion
  17.8 0.0 collective-permute-done.5.rest_3_
  17.8 4.0 %collective-permute-start = (f32[512,128]{1,0:T(8,128)}, f32[512,128]{1,0:T(8,128)S(1)}, u32[]{:S(2)}, u32[]{:S(2)}) collective-permute-start(f32[512,128]{1,0:T(8,128)} %constant_dynamic-slice_fusion), channel_id=1, source_target_pairs={{0,256},{32,288},{64,320},{96,352},{128,384},{160,416},{192,448},{... | collective-permute-start | bytes 786440 | tf_op jit(solution)/shard_map/ppermute | solution.py:311
  21.8 0.1 pad_add_fusion.place_ref
  21.9 0.0 copy-done.2
  21.9 0.1 fusion.6
  22.0 0.0 collective-permute-done.3.rest_1_
  22.0 0.0 collective-permute-done.2.rest_0_
  22.0 0.0 collective-permute-done.4.rest_2_
  22.0 4.2 %collective-permute-done.1.far_ref.rest_4_ = f32[1536,128]{1,0:T(8,128)} collective-permute-done((f32[1536,128]{1,0:T(8,128)}, f32[1536,128]{1,0:T(8,128)}, u32[]{:S(2)}, u32[]{:S(2)}) %collective-permute-start.1) | collective-permute-done | bytes 786464 | tf_op jit(solution)/shard_map/ppermute | solution.py:311
  26.2 2.8 %first_gram.1.before_ref = f32[520,128]{1,0:T(8,128)S(1)} custom-call(s32[2]{0:T(128)S(1)} %pad_add_fusion.place_ref, f32[4096,128]{1,0:T(8,128)S(1)} %bitcast.26, f32[1536,128]{1,0:T(8,128)} %collective-permute-done.1.far_ref.rest_4_, f32[8,128]{1,0:T(8,128)S(1)} %broadcast_in_dim.14.listed_ref, f32[1024,128]{1,0:T(8,128)} %collective-permute-done.2.rest_0_, ...), custom_call_target="tpu_custom_call" | custom-call | flops 1 | bytes 1 | tf_op jit(solution)/shard_map/first_gram/pallas_call | solution.py:116
  29.0 0.0 copy-start.1
  29.0 1.7 %collective-permute-done.far_ref.rest_5_ = f32[512,128]{1,0:T(8,128)S(1)} collective-permute-done((f32[512,128]{1,0:T(8,128)}, f32[512,128]{1,0:T(8,128)S(1)}, u32[]{:S(2)}, u32[]{:S(2)}) %collective-permute-start) | collective-permute-done | bytes 262176 | tf_op jit(solution)/shard_map/ppermute | solution.py:311
  30.7 1.5 %last_gram.1.mine_ref = f32[520,128]{1,0:T(8,128)S(1)} custom-call(s32[2]{0:T(128)S(1)} %pad_add_fusion.place_ref, f32[4096,128]{1,0:T(8,128)S(1)} %bitcast.27, f32[512,128]{1,0:T(8,128)S(1)} %collective-permute-done.far_ref.rest_5_, f32[520,128]{1,0:T(8,128)S(1)} %first_gram.1.before_ref, f32[1024,128]{1,0:T(8,128)} %collective-permute-done.2.rest_0_, ...), custom_call_target="tpu_custom_call" | custom-call | flops 1 | bytes 1 | tf_op jit(solution)/shard_map/last_gram/pallas_call | solution.py:116
  32.2 3.3 %collective-permute-start.6 = (f32[520,128]{1,0:T(8,128)S(1)}, f32[520,128]{1,0:T(8,128)S(1)}, u32[]{:S(2)}, u32[]{:S(2)}) collective-permute-start(f32[520,128]{1,0:T(8,128)S(1)} %last_gram.1.mine_ref), channel_id=1, source_target_pairs={{0,256},{32,288},{64,320},{96,352},{128,384},{160,416},{192,448},{... | collective-permute-start | bytes 798728 | tf_op jit(solution)/shard_map/ppermute | solution.py:311
  35.6 0.1 fusion.7
  35.6 0.2 convert_reduce_fusion.1
  35.8 1.9 %collective-permute-start.10 = (f32[512,128]{1,0:T(8,128)S(1)}, f32[512,128]{1,0:T(8,128)S(1)}, u32[]{:S(2)}, u32[]{:S(2)}) collective-permute-start(f32[512,128]{1,0:T(8,128)S(1)} %collective-permute-done.far_ref.rest_5_), channel_id=1, source_target_pairs={{0,32},{32,0},{64,96},{96,64},{128,160},{160,128},{192,224},{224,1... | collective-permute-start | bytes 786440 | tf_op jit(solution)/shard_map/ppermute | solution.py:311
  37.7 2.4 %collective-permute-start.7 = (f32[520,128]{1,0:T(8,128)S(1)}, f32[520,128]{1,0:T(8,128)S(1)}, u32[]{:S(2)}, u32[]{:S(2)}) collective-permute-start(f32[520,128]{1,0:T(8,128)S(1)} %last_gram.1.mine_ref), channel_id=1, source_target_pairs={{0,32},{32,0},{64,96},{96,64},{128,160},{160,128},{192,224},{224,1... | collective-permute-start | bytes 798728 | tf_op jit(solution)/shard_map/ppermute | solution.py:311
  40.1 1.9 %collective-permute-start.9 = (f32[1536,128]{1,0:T(8,128)}, f32[1536,128]{1,0:T(8,128)S(1)}, u32[]{:S(2)}, u32[]{:S(2)}) collective-permute-start(f32[1536,128]{1,0:T(8,128)} %collective-permute-done.1.far_ref.rest_4_), channel_id=1, source_target_pairs={{0,32},{32,0},{64,96},{96,64},{128,160},{160,128},{192,224},{224,1... | collective-permute-start | bytes 2359304 | tf_op jit(solution)/shard_map/ppermute | solution.py:311
  42.1 0.9 collective-permute-done.6.far_ref
  43.0 0.1 slice_bitcast_fusion.5
  43.1 1.9 %collective-permute-start.8 = (f32[520,128]{1,0:T(8,128)S(1)}, f32[520,128]{1,0:T(8,128)S(1)}, u32[]{:S(2)}, u32[]{:S(2)}) collective-permute-start(f32[520,128]{1,0:T(8,128)S(1)} %collective-permute-done.6.far_ref), channel_id=1, source_target_pairs={{0,32},{32,0},{64,96},{96,64},{128,160},{160,128},{192,224},{224,1... | collective-permute-start | bytes 798728 | tf_op jit(solution)/shard_map/ppermute | solution.py:311
  45.0 0.2 convert_reduce_fusion
  45.2 0.1 select_reduce_fusion.1
  45.3 0.3 convolution_bitcast_fusion
  45.6 0.0 collective-permute-done.7.next_ref
  45.6 0.9 collective-permute-done.8.next_far_ref
  46.5 9.5 %turn.1 = (f32[2,512,128]{2,1,0:T(8,128)S(1)}, f32[8,128]{1,0:T(8,128)S(1)}) custom-call(s32[2]{0:T(128)S(1)} %pad_add_fusion.place_ref, f32[520,128]{1,0:T(8,128)S(1)} %last_gram.1.mine_ref, f32[520,128]{1,0:T(8,128)S(1)} %collective-permute-done.6.far_ref, f32[520,128]{1,0:T(8,128)S(1)} %collective-permute-done.7.next_ref, ...), custom_call_target="tpu_custom_call" | custom-call | tf_op jit(solution)/shard_map/turn/pallas_call | solution.py:217
  56.0 3.5 %collective-permute-start.11 = (f32[8,128]{1,0:T(8,128)S(1)}, f32[8,128]{1,0:T(8,128)S(1)}, u32[]{:S(2)}, u32[]{:S(2)}) collective-permute-start(f32[8,128]{1,0:T(8,128)S(1)} %get-tuple-element.8), channel_id=1, source_target_pairs={{0,64},{32,96},{64,0},{96,32},{128,192},{160,224},{192,128},{224,1... | collective-permute-start | bytes 12296 | tf_op jit(solution)/shard_map/ppermute | solution.py:311
  59.5 0.3 convolution_bitcast_fusion.1
  59.8 1.7 %collective-permute-done.11 = f32[8,128]{1,0:T(8,128)S(1)} collective-permute-done((f32[8,128]{1,0:T(8,128)S(1)}, f32[8,128]{1,0:T(8,128)S(1)}, u32[]{:S(2)}, u32[]{:S(2)}) %collective-permute-start.11) | collective-permute-done | bytes 4128 | tf_op jit(solution)/shard_map/ppermute | solution.py:311
  61.5 2.8 %collective-permute-start.12 = (f32[8,128]{1,0:T(8,128)S(1)}, f32[8,128]{1,0:T(8,128)S(1)}, u32[]{:S(2)}, u32[]{:S(2)}) collective-permute-start(f32[8,128]{1,0:T(8,128)S(1)} %add.61.rest_8_), channel_id=1, source_target_pairs={{0,128},{32,160},{64,192},{96,224},{128,0},{160,32},{192,64},{224,... | collective-permute-start | bytes 12296 | tf_op jit(solution)/shard_map/ppermute | solution.py:311
  64.4 2.7 %collective-permute-done.12 = f32[8,128]{1,0:T(8,128)S(1)} collective-permute-done((f32[8,128]{1,0:T(8,128)S(1)}, f32[8,128]{1,0:T(8,128)S(1)}, u32[]{:S(2)}, u32[]{:S(2)}) %collective-permute-start.12) | collective-permute-done | bytes 4128 | tf_op jit(solution)/shard_map/ppermute | solution.py:311
  67.0 0.0 collective-permute-done.9.rest_5_.rest_6_
  67.0 3.0 %placed.2.refs_0_ = f32[256,1024]{1,0:T(8,128)S(1)} custom-call(s32[2]{0:T(128)S(1)} %pad_add_fusion.place_ref, f32[2,512,128]{2,1,0:T(8,128)S(1)} %get-tuple-element.7.turned_ref, f32[2,128,256]{2,1,0:T(8,128)S(1)} %pad_maximum_fusion.route_ref, f32[4096,128]{1,0:T(8,128)S(1)} %bitcast.28, f32[1024,128]{1,0:T(8,128)} %collective-permute-done.2.rest_0_, ...), custom_call_target="tpu_custom_call" | custom-call | flops 805306368 | bytes 2097152 | tf_op jit(solution)/shard_map/placed/pallas_call | solution.py:255
  70.0 0.0 collective-permute-done.10.rest_7_
  70.0 3.0 %placed.3.refs_1_ = f32[256,1024]{1,0:T(8,128)S(1)} custom-call(s32[2]{0:T(128)S(1)} %pad_add_fusion.place_ref, f32[2,512,128]{2,1,0:T(8,128)S(1)} %get-tuple-element.7.turned_ref, f32[2,128,256]{2,1,0:T(8,128)S(1)} %pad_maximum_fusion.route_ref, f32[4096,128]{1,0:T(8,128)S(1)} %bitcast.29, f32[1024,128]{1,0:T(8,128)} %collective-permute-done.2.rest_0_, ...), custom_call_target="tpu_custom_call" | custom-call | flops 805306368 | bytes 2097152 | tf_op jit(solution)/shard_map/placed/pallas_call | solution.py:255
  73.0 0.6 spread.1
  73.6 75.4 %all_to_all.5 = f32[64,16,4,128]{3,2,1,0:T(4,128)S(1)} all-to-all(f32[64,16,4,128]{3,2,1,0:T(4,128)S(1)} %spread.1), channel_id=1, replica_groups={{0,256,8,264,1,257,9,265,2,258,10,266,3,259,11,267,4,260,12,268,5,261,1..., dimensions={0} | all-to-all | bytes 4194304 | tf_op jit(solution)/shard_map/all_to_all | solution.py:410
  149.0 1.5 join.1
  (12 shorter events, 0.1 us)
Async XLA Ops:
  2.1 15.0 %copy-start = (f32[1,4096,128]{2,1,0:T(8,128)S(1)}, f32[1,4096,128]{2,1,0:T(8,128)}, u32[]{:S(2)}) copy-start(f32[1,4096,128]{2,1,0:T(8,128)} %param.5) | copy-start | bytes 6291460
  2.1 19.8 %copy-start.2 = (s32[1,64,1]{1,2,0:T(1,128)S(1)}, s32[1,64,1]{1,2,0:T(1,128)}, u32[]{:S(2)}) copy-start(s32[1,64,1]{1,2,0:T(1,128)} %param.7) | copy-start | bytes 772
  2.1 19.8 %copy-start.3 = (s32[1,64]{1,0:T(1,128)S(1)}, s32[1,64]{1,0:T(1,128)}, u32[]{:S(2)}) copy-start(s32[1,64]{1,0:T(1,128)} %param.6) | copy-start | bytes 772
  2.1 24.1 %collective-permute-start.1 = (f32[1536,128]{1,0:T(8,128)}, f32[1536,128]{1,0:T(8,128)}, u32[]{:S(2)}, u32[]{:S(2)}) collective-permute-start(f32[1536,128]{1,0:T(8,128)} %dynamic-slice_bitcast_fusion), channel_id=1, source_target_pairs={{0,256},{32,288},{64,320},{96,352},{128,384},{160,416},{192,448},{... | collective-permute-start | bytes 2359304 | tf_op jit(solution)/shard_map/ppermute | solution.py:311
  8.4 9.4 %collective-permute-start.5 = (f32[1024,128]{1,0:T(8,128)}, f32[1024,128]{1,0:T(8,128)S(1)}, u32[]{:S(2)}, u32[]{:S(2)}) collective-permute-start(f32[1024,128]{1,0:T(8,128)} %get-tuple-element.13), channel_id=1, source_target_pairs={{0,32},{32,0},{64,96},{96,64},{128,160},{160,128},{192,224},{224,1... | collective-permute-start | bytes 1572872 | tf_op jit(solution)/shard_map/ppermute | solution.py:311
  10.3 11.7 %collective-permute-start.3 = (f32[1024,128]{1,0:T(8,128)}, f32[1024,128]{1,0:T(8,128)S(1)}, u32[]{:S(2)}, u32[]{:S(2)}) collective-permute-start(f32[1024,128]{1,0:T(8,128)} %get-tuple-element.14), channel_id=1, source_target_pairs={{0,32},{32,0},{64,96},{96,64},{128,160},{160,128},{192,224},{224,1... | collective-permute-start | bytes 1572872 | tf_op jit(solution)/shard_map/ppermute | solution.py:311
  12.7 9.3 %collective-permute-start.2 = (f32[1024,128]{1,0:T(8,128)}, f32[1024,128]{1,0:T(8,128)}, u32[]{:S(2)}, u32[]{:S(2)}) collective-permute-start(f32[1024,128]{1,0:T(8,128)} %get-tuple-element.15), channel_id=1, source_target_pairs={{0,32},{32,0},{64,96},{96,64},{128,160},{160,128},{192,224},{224,1... | collective-permute-start | bytes 1572872 | tf_op jit(solution)/shard_map/ppermute | solution.py:311
  14.6 7.3 %collective-permute-start.4 = (f32[1024,128]{1,0:T(8,128)}, f32[1024,128]{1,0:T(8,128)}, u32[]{:S(2)}, u32[]{:S(2)}) collective-permute-start(f32[1024,128]{1,0:T(8,128)} %get-tuple-element.16), channel_id=1, source_target_pairs={{0,32},{32,0},{64,96},{96,64},{128,160},{160,128},{192,224},{224,1... | collective-permute-start | bytes 1572872 | tf_op jit(solution)/shard_map/ppermute | solution.py:311
  17.8 12.9 %collective-permute-start = (f32[512,128]{1,0:T(8,128)}, f32[512,128]{1,0:T(8,128)S(1)}, u32[]{:S(2)}, u32[]{:S(2)}) collective-permute-start(f32[512,128]{1,0:T(8,128)} %constant_dynamic-slice_fusion), channel_id=1, source_target_pairs={{0,256},{32,288},{64,320},{96,352},{128,384},{160,416},{192,448},{... | collective-permute-start | bytes 786440 | tf_op jit(solution)/shard_map/ppermute | solution.py:311
  29.0 16.2 %copy-start.1 = (s32[32]{0:T(128)S(1)}, s32[32]{0:T(128)}, u32[]{:S(2)}) copy-start(s32[32]{0:T(128)} %constant.39.clone) | copy-start | bytes 388
  32.2 10.8 %collective-permute-start.6 = (f32[520,128]{1,0:T(8,128)S(1)}, f32[520,128]{1,0:T(8,128)S(1)}, u32[]{:S(2)}, u32[]{:S(2)}) collective-permute-start(f32[520,128]{1,0:T(8,128)S(1)} %last_gram.1.mine_ref), channel_id=1, source_target_pairs={{0,256},{32,288},{64,320},{96,352},{128,384},{160,416},{192,448},{... | collective-permute-start | bytes 798728 | tf_op jit(solution)/shard_map/ppermute | solution.py:311
  35.8 34.2 %collective-permute-start.10 = (f32[512,128]{1,0:T(8,128)S(1)}, f32[512,128]{1,0:T(8,128)S(1)}, u32[]{:S(2)}, u32[]{:S(2)}) collective-permute-start(f32[512,128]{1,0:T(8,128)S(1)} %collective-permute-done.far_ref.rest_5_), channel_id=1, source_target_pairs={{0,32},{32,0},{64,96},{96,64},{128,160},{160,128},{192,224},{224,1... | collective-permute-start | bytes 786440 | tf_op jit(solution)/shard_map/ppermute | solution.py:311
  37.7 7.8 %collective-permute-start.7 = (f32[520,128]{1,0:T(8,128)S(1)}, f32[520,128]{1,0:T(8,128)S(1)}, u32[]{:S(2)}, u32[]{:S(2)}) collective-permute-start(f32[520,128]{1,0:T(8,128)S(1)} %last_gram.1.mine_ref), channel_id=1, source_target_pairs={{0,32},{32,0},{64,96},{96,64},{128,160},{160,128},{192,224},{224,1... | collective-permute-start | bytes 798728 | tf_op jit(solution)/shard_map/ppermute | solution.py:311
  40.1 26.9 %collective-permute-start.9 = (f32[1536,128]{1,0:T(8,128)}, f32[1536,128]{1,0:T(8,128)S(1)}, u32[]{:S(2)}, u32[]{:S(2)}) collective-permute-start(f32[1536,128]{1,0:T(8,128)} %collective-permute-done.1.far_ref.rest_4_), channel_id=1, source_target_pairs={{0,32},{32,0},{64,96},{96,64},{128,160},{160,128},{192,224},{224,1... | collective-permute-start | bytes 2359304 | tf_op jit(solution)/shard_map/ppermute | solution.py:311
  43.1 3.4 %collective-permute-start.8 = (f32[520,128]{1,0:T(8,128)S(1)}, f32[520,128]{1,0:T(8,128)S(1)}, u32[]{:S(2)}, u32[]{:S(2)}) collective-permute-start(f32[520,128]{1,0:T(8,128)S(1)} %collective-permute-done.6.far_ref), channel_id=1, source_target_pairs={{0,32},{32,0},{64,96},{96,64},{128,160},{160,128},{192,224},{224,1... | collective-permute-start | bytes 798728 | tf_op jit(solution)/shard_map/ppermute | solution.py:311
  56.0 5.5 %collective-permute-start.11 = (f32[8,128]{1,0:T(8,128)S(1)}, f32[8,128]{1,0:T(8,128)S(1)}, u32[]{:S(2)}, u32[]{:S(2)}) collective-permute-start(f32[8,128]{1,0:T(8,128)S(1)} %get-tuple-element.8), channel_id=1, source_target_pairs={{0,64},{32,96},{64,0},{96,32},{128,192},{160,224},{192,128},{224,1... | collective-permute-start | bytes 12296 | tf_op jit(solution)/shard_map/ppermute | solution.py:311
  61.5 5.5 %collective-permute-start.12 = (f32[8,128]{1,0:T(8,128)S(1)}, f32[8,128]{1,0:T(8,128)S(1)}, u32[]{:S(2)}, u32[]{:S(2)}) collective-permute-start(f32[8,128]{1,0:T(8,128)S(1)} %add.61.rest_8_), channel_id=1, source_target_pairs={{0,128},{32,160},{64,192},{96,224},{128,0},{160,32},{192,64},{224,... | collective-permute-start | bytes 12296 | tf_op jit(solution)/shard_map/ppermute | solution.py:311

commit v5 on v4

--- a/solution.py
+++ b/solution.py
@@ -384,21 +384,11 @@
     )
 
     turned, squares = turn(place, grams, far_grams, *next_grams)
-    middle = sizes[0] * 2 // 3
-    outgoing = [
-        placed(
-            place, turned, routes, block, neighbour, (far_a,), (next_far_a,),
-            ((0, slice(0, middle)),),
-        )
-    ]
-    squares = squares + from_partner(squares, "bond", 2)
-    outgoing.append(
-        placed(
-            place, turned, routes, block, neighbour, (far_a, far_b), (next_far_a, next_far_b),
-            ((middle, slice(middle, sizes[0])), (sizes[0], slice(0, sizes[1]))), (squares,),
-        )
-    )
-    for distance in [1 << bit for bit in range(2, far.bit_length() - 1)]:
+    outgoing = placed(
+        place, turned, routes, block, neighbour, (far_a, far_b), (next_far_a, next_far_b),
+        ((0, slice(0, sizes[0])), (sizes[0], slice(0, sizes[1]))),
+    )
+    for distance in [1 << bit for bit in range(1, far.bit_length() - 1)]:
         squares = squares + from_partner(squares, "bond", distance)
     keep_count = keep_list.shape[1]
     capacity = max(2, 2 * keep_count // groups)
@@ -408,7 +398,7 @@
         for first in range(far)
     ]
     arrived = lax.all_to_all(
-        spread(outgoing, squares, float(rows * count * keep_count), capacity),
+        spread([outgoing], squares, float(rows * count * keep_count), capacity),
         ("bond", "site"),
         split_axis=0,
         concat_axis=0,

time: 151 us -> 149 us (0.987)
  Pallas kernels: 21.9 us -> 19.7 us
    pallas_call x2 -> x1, Pallas kernels: 5.98 us -> 3.82 us  [placed(): pl.pallas_call(functools.partial(place_kernel, spans, len(neighbour)), in...]
  transfers between devices with their start and end apart: 13 -> 13, of which waited for: 6 -> 6; matrix products, arithmetic and copies ran while one was open for 3% -> 3% of each run, Pallas kernels for 10% -> 8%
where the time goes in v5:
time: 149 us; the launch traced here: 148 us
  blocking collectives  75.4 us (51%)
  starting transfers between devices  33.8 us (23%)
  Pallas kernels  19.7 us (13%)
  waiting for transfers between devices  12.1 us (8%)
  local copies, waits for them, and re-layouts  5.8 us (4%)
    all_to_all x1, blocking collectives, on_device(): lax.all_to_all(spread([outgoing], squares, float(rows * count * keep_coun...  75.4 us
    ppermute x13, starting transfers between devices, from_partner(): return lax.ppermute(value, axis, pairs)  33.8 us
    ppermute x13, waiting for transfers between devices, from_partner(): return lax.ppermute(value, axis, pairs)  12.1 us
    pallas_call x1, Pallas kernels, turn(): pl.pallas_call(turn_kernel, in_specs=[SMEM] + [VMEM] * len(values), out_s...  9.52 us
    pallas_call x2, Pallas kernels, gram_call(): pl.pallas_call(kernel, in_specs=[SMEM] + [VMEM] * len(values), out_specs=...  4.33 us
    pallas_call x1, Pallas kernels, placed(): pl.pallas_call(functools.partial(place_kernel, spans, len(neighbour)), in...  3.82 us
  transfers between devices with their start and end apart: 13, of which 6 were waited for; matrix products, arithmetic and copies ran while one was open for 3% of the time, Pallas kernels for 8%

profile of v5, /device:TPU:70, one launch (start us, length us, event | category | flops | bytes accessed | tf_op | source)
XLA Modules:
  0.0 148.3 jit_solution(13933181362110276941)
XLA Ops:
  0.0 2.1 %dynamic-slice_bitcast_fusion = f32[1536,128]{1,0:T(8,128)} fusion(f32[1,4096,128]{2,1,0:T(8,128)} %param.5, s32[]{:T(128)S(6)} %select_n.20), kind=kLoop, calls=%fused_computation.2 | loop fusion | bytes 1572868 | tf_op jit(solution)/shard_map/dynamic_slice | solution.py:362
  2.1 3.4 %collective-permute-start.1 = (f32[1536,128]{1,0:T(8,128)}, f32[1536,128]{1,0:T(8,128)}, u32[]{:S(2)}, u32[]{:S(2)}) collective-permute-start(f32[1536,128]{1,0:T(8,128)} %dynamic-slice_bitcast_fusion), channel_id=1, source_target_pairs={{0,256},{32,288},{64,320},{96,352},{128,384},{160,416},{192,448},{... | collective-permute-start | bytes 2359304 | tf_op jit(solution)/shard_map/ppermute | solution.py:311
  5.5 2.9 %slice_bitcast_fusion = (f32[1024,128]{1,0:T(8,128)}, f32[1024,128]{1,0:T(8,128)}, f32[1024,128]{1,0:T(8,128)}, f32[1024,128]{1,0:T(8,128)}) fusion(f32[1,4096,128]{2,1,0:T(8,128)} %param.5), kind=kLoop, calls=%fused_computation.3 | loop fusion | bytes 4194304 | tf_op jit(solution)/shard_map/slice | solution.py:367
  8.4 1.9 %collective-permute-start.5 = (f32[1024,128]{1,0:T(8,128)}, f32[1024,128]{1,0:T(8,128)S(1)}, u32[]{:S(2)}, u32[]{:S(2)}) collective-permute-start(f32[1024,128]{1,0:T(8,128)} %get-tuple-element.13), channel_id=1, source_target_pairs={{0,32},{32,0},{64,96},{96,64},{128,160},{160,128},{192,224},{224,1... | collective-permute-start | bytes 1572872 | tf_op jit(solution)/shard_map/ppermute | solution.py:311
  10.3 2.4 %collective-permute-start.3 = (f32[1024,128]{1,0:T(8,128)}, f32[1024,128]{1,0:T(8,128)S(1)}, u32[]{:S(2)}, u32[]{:S(2)}) collective-permute-start(f32[1024,128]{1,0:T(8,128)} %get-tuple-element.14), channel_id=1, source_target_pairs={{0,32},{32,0},{64,96},{96,64},{128,160},{160,128},{192,224},{224,1... | collective-permute-start | bytes 1572872 | tf_op jit(solution)/shard_map/ppermute | solution.py:311
  12.7 1.9 %collective-permute-start.2 = (f32[1024,128]{1,0:T(8,128)}, f32[1024,128]{1,0:T(8,128)}, u32[]{:S(2)}, u32[]{:S(2)}) collective-permute-start(f32[1024,128]{1,0:T(8,128)} %get-tuple-element.15), channel_id=1, source_target_pairs={{0,32},{32,0},{64,96},{96,64},{128,160},{160,128},{192,224},{224,1... | collective-permute-start | bytes 1572872 | tf_op jit(solution)/shard_map/ppermute | solution.py:311
  14.6 2.4 %collective-permute-start.4 = (f32[1024,128]{1,0:T(8,128)}, f32[1024,128]{1,0:T(8,128)}, u32[]{:S(2)}, u32[]{:S(2)}) collective-permute-start(f32[1024,128]{1,0:T(8,128)} %get-tuple-element.16), channel_id=1, source_target_pairs={{0,32},{32,0},{64,96},{96,64},{128,160},{160,128},{192,224},{224,1... | collective-permute-start | bytes 1572872 | tf_op jit(solution)/shard_map/ppermute | solution.py:311
  17.1 0.0 copy-done
  17.1 0.7 constant_dynamic-slice_fusion
  17.8 0.0 collective-permute-done.5.rest_3_
  17.8 4.0 %collective-permute-start = (f32[512,128]{1,0:T(8,128)}, f32[512,128]{1,0:T(8,128)S(1)}, u32[]{:S(2)}, u32[]{:S(2)}) collective-permute-start(f32[512,128]{1,0:T(8,128)} %constant_dynamic-slice_fusion), channel_id=1, source_target_pairs={{0,256},{32,288},{64,320},{96,352},{128,384},{160,416},{192,448},{... | collective-permute-start | bytes 786440 | tf_op jit(solution)/shard_map/ppermute | solution.py:311
  21.8 0.1 pad_add_fusion.place_ref
  21.9 0.0 copy-done.2
  21.9 0.1 fusion.6
  22.0 0.0 collective-permute-done.3.rest_1_
  22.0 0.0 collective-permute-done.2.rest_0_
  22.0 0.0 collective-permute-done.4.rest_2_
  22.0 4.2 %collective-permute-done.1.far_ref.rest_4_ = f32[1536,128]{1,0:T(8,128)} collective-permute-done((f32[1536,128]{1,0:T(8,128)}, f32[1536,128]{1,0:T(8,128)}, u32[]{:S(2)}, u32[]{:S(2)}) %collective-permute-start.1) | collective-permute-done | bytes 786464 | tf_op jit(solution)/shard_map/ppermute | solution.py:311
  26.2 2.8 %first_gram.1.before_ref = f32[520,128]{1,0:T(8,128)S(1)} custom-call(s32[2]{0:T(128)S(1)} %pad_add_fusion.place_ref, f32[4096,128]{1,0:T(8,128)S(1)} %bitcast.26, f32[1536,128]{1,0:T(8,128)} %collective-permute-done.1.far_ref.rest_4_, f32[8,128]{1,0:T(8,128)S(1)} %broadcast_in_dim.14.listed_ref, f32[1024,128]{1,0:T(8,128)} %collective-permute-done.2.rest_0_, ...), custom_call_target="tpu_custom_call" | custom-call | flops 1 | bytes 1 | tf_op jit(solution)/shard_map/first_gram/pallas_call | solution.py:116
  29.0 0.0 copy-start.1
  29.0 1.7 %collective-permute-done.far_ref.rest_5_ = f32[512,128]{1,0:T(8,128)S(1)} collective-permute-done((f32[512,128]{1,0:T(8,128)}, f32[512,128]{1,0:T(8,128)S(1)}, u32[]{:S(2)}, u32[]{:S(2)}) %collective-permute-start) | collective-permute-done | bytes 262176 | tf_op jit(solution)/shard_map/ppermute | solution.py:311
  30.7 1.5 %last_gram.1.mine_ref = f32[520,128]{1,0:T(8,128)S(1)} custom-call(s32[2]{0:T(128)S(1)} %pad_add_fusion.place_ref, f32[4096,128]{1,0:T(8,128)S(1)} %bitcast.27, f32[512,128]{1,0:T(8,128)S(1)} %collective-permute-done.far_ref.rest_5_, f32[520,128]{1,0:T(8,128)S(1)} %first_gram.1.before_ref, f32[1024,128]{1,0:T(8,128)} %collective-permute-done.2.rest_0_, ...), custom_call_target="tpu_custom_call" | custom-call | flops 1 | bytes 1 | tf_op jit(solution)/shard_map/last_gram/pallas_call | solution.py:116
  32.2 3.3 %collective-permute-start.6 = (f32[520,128]{1,0:T(8,128)S(1)}, f32[520,128]{1,0:T(8,128)S(1)}, u32[]{:S(2)}, u32[]{:S(2)}) collective-permute-start(f32[520,128]{1,0:T(8,128)S(1)} %last_gram.1.mine_ref), channel_id=1, source_target_pairs={{0,256},{32,288},{64,320},{96,352},{128,384},{160,416},{192,448},{... | collective-permute-start | bytes 798728 | tf_op jit(solution)/shard_map/ppermute | solution.py:311
  35.6 0.1 fusion.7
  35.6 0.2 convert_reduce_fusion.1
  35.8 1.9 %collective-permute-start.10 = (f32[512,128]{1,0:T(8,128)S(1)}, f32[512,128]{1,0:T(8,128)S(1)}, u32[]{:S(2)}, u32[]{:S(2)}) collective-permute-start(f32[512,128]{1,0:T(8,128)S(1)} %collective-permute-done.far_ref.rest_5_), channel_id=1, source_target_pairs={{0,32},{32,0},{64,96},{96,64},{128,160},{160,128},{192,224},{224,1... | collective-permute-start | bytes 786440 | tf_op jit(solution)/shard_map/ppermute | solution.py:311
  37.7 2.4 %collective-permute-start.7 = (f32[520,128]{1,0:T(8,128)S(1)}, f32[520,128]{1,0:T(8,128)S(1)}, u32[]{:S(2)}, u32[]{:S(2)}) collective-permute-start(f32[520,128]{1,0:T(8,128)S(1)} %last_gram.1.mine_ref), channel_id=1, source_target_pairs={{0,32},{32,0},{64,96},{96,64},{128,160},{160,128},{192,224},{224,1... | collective-permute-start | bytes 798728 | tf_op jit(solution)/shard_map/ppermute | solution.py:311
  40.1 1.9 %collective-permute-start.9 = (f32[1536,128]{1,0:T(8,128)}, f32[1536,128]{1,0:T(8,128)S(1)}, u32[]{:S(2)}, u32[]{:S(2)}) collective-permute-start(f32[1536,128]{1,0:T(8,128)} %collective-permute-done.1.far_ref.rest_4_), channel_id=1, source_target_pairs={{0,32},{32,0},{64,96},{96,64},{128,160},{160,128},{192,224},{224,1... | collective-permute-start | bytes 2359304 | tf_op jit(solution)/shard_map/ppermute | solution.py:311
  42.1 0.9 collective-permute-done.6.far_ref
  43.0 0.1 slice_bitcast_fusion.5
  43.1 1.9 %collective-permute-start.8 = (f32[520,128]{1,0:T(8,128)S(1)}, f32[520,128]{1,0:T(8,128)S(1)}, u32[]{:S(2)}, u32[]{:S(2)}) collective-permute-start(f32[520,128]{1,0:T(8,128)S(1)} %collective-permute-done.6.far_ref), channel_id=1, source_target_pairs={{0,32},{32,0},{64,96},{96,64},{128,160},{160,128},{192,224},{224,1... | collective-permute-start | bytes 798728 | tf_op jit(solution)/shard_map/ppermute | solution.py:311
  45.0 0.2 convert_reduce_fusion
  45.2 0.1 select_reduce_fusion.1
  45.3 0.3 convolution_bitcast_fusion
  45.6 0.0 collective-permute-done.7.next_ref
  45.6 0.9 collective-permute-done.8.next_far_ref
  46.5 9.5 %turn.1 = (f32[2,512,128]{2,1,0:T(8,128)S(1)}, f32[8,128]{1,0:T(8,128)S(1)}) custom-call(s32[2]{0:T(128)S(1)} %pad_add_fusion.place_ref, f32[520,128]{1,0:T(8,128)S(1)} %last_gram.1.mine_ref, f32[520,128]{1,0:T(8,128)S(1)} %collective-permute-done.6.far_ref, f32[520,128]{1,0:T(8,128)S(1)} %collective-permute-done.7.next_ref, ...), custom_call_target="tpu_custom_call" | custom-call | tf_op jit(solution)/shard_map/turn/pallas_call | solution.py:217
  56.0 3.5 %collective-permute-start.11 = (f32[8,128]{1,0:T(8,128)S(1)}, f32[8,128]{1,0:T(8,128)S(1)}, u32[]{:S(2)}, u32[]{:S(2)}) collective-permute-start(f32[8,128]{1,0:T(8,128)S(1)} %get-tuple-element.8), channel_id=1, source_target_pairs={{0,64},{32,96},{64,0},{96,32},{128,192},{160,224},{192,128},{224,1... | collective-permute-start | bytes 12296 | tf_op jit(solution)/shard_map/ppermute | solution.py:311
  59.5 0.3 convolution_bitcast_fusion.1
  59.8 1.7 %collective-permute-done.11 = f32[8,128]{1,0:T(8,128)S(1)} collective-permute-done((f32[8,128]{1,0:T(8,128)S(1)}, f32[8,128]{1,0:T(8,128)S(1)}, u32[]{:S(2)}, u32[]{:S(2)}) %collective-permute-start.11) | collective-permute-done | bytes 4128 | tf_op jit(solution)/shard_map/ppermute | solution.py:311
  61.5 2.8 %collective-permute-start.12 = (f32[8,128]{1,0:T(8,128)S(1)}, f32[8,128]{1,0:T(8,128)S(1)}, u32[]{:S(2)}, u32[]{:S(2)}) collective-permute-start(f32[8,128]{1,0:T(8,128)S(1)} %add.61), channel_id=1, source_target_pairs={{0,128},{32,160},{64,192},{96,224},{128,0},{160,32},{192,64},{224,... | collective-permute-start | bytes 12296 | tf_op jit(solution)/shard_map/ppermute | solution.py:311
  64.4 2.7 %collective-permute-done.12 = f32[8,128]{1,0:T(8,128)S(1)} collective-permute-done((f32[8,128]{1,0:T(8,128)S(1)}, f32[8,128]{1,0:T(8,128)S(1)}, u32[]{:S(2)}, u32[]{:S(2)}) %collective-permute-start.12) | collective-permute-done | bytes 4128 | tf_op jit(solution)/shard_map/ppermute | solution.py:311
  67.0 0.0 collective-permute-done.10.rest_7_
  67.0 0.0 collective-permute-done.9.rest_6_
  67.0 3.8 %placed.1.refs_0_ = f32[256,2048]{1,0:T(8,128)S(1)} custom-call(s32[2]{0:T(128)S(1)} %pad_add_fusion.place_ref, f32[2,512,128]{2,1,0:T(8,128)S(1)} %get-tuple-element.7.turned_ref, f32[2,128,256]{2,1,0:T(8,128)S(1)} %pad_maximum_fusion.route_ref, f32[4096,128]{1,0:T(8,128)S(1)} %bitcast.28, f32[1024,128]{1,0:T(8,128)} %collective-permute-done.2.rest_0_, ...), custom_call_target="tpu_custom_call" | custom-call | flops 1610612736 | bytes 4194304 | tf_op jit(solution)/shard_map/placed/pallas_call | solution.py:255
  70.9 0.6 spread.1
  71.5 75.4 %all_to_all.5 = f32[64,16,4,128]{3,2,1,0:T(4,128)S(1)} all-to-all(f32[64,16,4,128]{3,2,1,0:T(4,128)S(1)} %spread.1), channel_id=1, replica_groups={{0,256,8,264,1,257,9,265,2,258,10,266,3,259,11,267,4,260,12,268,5,261,1..., dimensions={0} | all-to-all | bytes 4194304 | tf_op jit(solution)/shard_map/all_to_all | solution.py:400
  146.9 1.5 join.1
  (11 shorter events, 0.1 us)
Async XLA Ops:
  2.1 15.0 %copy-start = (f32[1,4096,128]{2,1,0:T(8,128)S(1)}, f32[1,4096,128]{2,1,0:T(8,128)}, u32[]{:S(2)}) copy-start(f32[1,4096,128]{2,1,0:T(8,128)} %param.5) | copy-start | bytes 6291460
  2.1 19.8 %copy-start.2 = (s32[1,64,1]{1,2,0:T(1,128)S(1)}, s32[1,64,1]{1,2,0:T(1,128)}, u32[]{:S(2)}) copy-start(s32[1,64,1]{1,2,0:T(1,128)} %param.7) | copy-start | bytes 772
  2.1 19.8 %copy-start.3 = (s32[1,64]{1,0:T(1,128)S(1)}, s32[1,64]{1,0:T(1,128)}, u32[]{:S(2)}) copy-start(s32[1,64]{1,0:T(1,128)} %param.6) | copy-start | bytes 772
  2.1 24.1 %collective-permute-start.1 = (f32[1536,128]{1,0:T(8,128)}, f32[1536,128]{1,0:T(8,128)}, u32[]{:S(2)}, u32[]{:S(2)}) collective-permute-start(f32[1536,128]{1,0:T(8,128)} %dynamic-slice_bitcast_fusion), channel_id=1, source_target_pairs={{0,256},{32,288},{64,320},{96,352},{128,384},{160,416},{192,448},{... | collective-permute-start | bytes 2359304 | tf_op jit(solution)/shard_map/ppermute | solution.py:311
  8.4 9.4 %collective-permute-start.5 = (f32[1024,128]{1,0:T(8,128)}, f32[1024,128]{1,0:T(8,128)S(1)}, u32[]{:S(2)}, u32[]{:S(2)}) collective-permute-start(f32[1024,128]{1,0:T(8,128)} %get-tuple-element.13), channel_id=1, source_target_pairs={{0,32},{32,0},{64,96},{96,64},{128,160},{160,128},{192,224},{224,1... | collective-permute-start | bytes 1572872 | tf_op jit(solution)/shard_map/ppermute | solution.py:311
  10.3 11.7 %collective-permute-start.3 = (f32[1024,128]{1,0:T(8,128)}, f32[1024,128]{1,0:T(8,128)S(1)}, u32[]{:S(2)}, u32[]{:S(2)}) collective-permute-start(f32[1024,128]{1,0:T(8,128)} %get-tuple-element.14), channel_id=1, source_target_pairs={{0,32},{32,0},{64,96},{96,64},{128,160},{160,128},{192,224},{224,1... | collective-permute-start | bytes 1572872 | tf_op jit(solution)/shard_map/ppermute | solution.py:311
  12.7 9.3 %collective-permute-start.2 = (f32[1024,128]{1,0:T(8,128)}, f32[1024,128]{1,0:T(8,128)}, u32[]{:S(2)}, u32[]{:S(2)}) collective-permute-start(f32[1024,128]{1,0:T(8,128)} %get-tuple-element.15), channel_id=1, source_target_pairs={{0,32},{32,0},{64,96},{96,64},{128,160},{160,128},{192,224},{224,1... | collective-permute-start | bytes 1572872 | tf_op jit(solution)/shard_map/ppermute | solution.py:311
  14.6 7.3 %collective-permute-start.4 = (f32[1024,128]{1,0:T(8,128)}, f32[1024,128]{1,0:T(8,128)}, u32[]{:S(2)}, u32[]{:S(2)}) collective-permute-start(f32[1024,128]{1,0:T(8,128)} %get-tuple-element.16), channel_id=1, source_target_pairs={{0,32},{32,0},{64,96},{96,64},{128,160},{160,128},{192,224},{224,1... | collective-permute-start | bytes 1572872 | tf_op jit(solution)/shard_map/ppermute | solution.py:311
  17.8 12.9 %collective-permute-start = (f32[512,128]{1,0:T(8,128)}, f32[512,128]{1,0:T(8,128)S(1)}, u32[]{:S(2)}, u32[]{:S(2)}) collective-permute-start(f32[512,128]{1,0:T(8,128)} %constant_dynamic-slice_fusion), channel_id=1, source_target_pairs={{0,256},{32,288},{64,320},{96,352},{128,384},{160,416},{192,448},{... | collective-permute-start | bytes 786440 | tf_op jit(solution)/shard_map/ppermute | solution.py:311
  29.0 16.2 %copy-start.1 = (s32[32]{0:T(128)S(1)}, s32[32]{0:T(128)}, u32[]{:S(2)}) copy-start(s32[32]{0:T(128)} %constant.39.clone) | copy-start | bytes 388
  32.2 10.8 %collective-permute-start.6 = (f32[520,128]{1,0:T(8,128)S(1)}, f32[520,128]{1,0:T(8,128)S(1)}, u32[]{:S(2)}, u32[]{:S(2)}) collective-permute-start(f32[520,128]{1,0:T(8,128)S(1)} %last_gram.1.mine_ref), channel_id=1, source_target_pairs={{0,256},{32,288},{64,320},{96,352},{128,384},{160,416},{192,448},{... | collective-permute-start | bytes 798728 | tf_op jit(solution)/shard_map/ppermute | solution.py:311
  35.8 31.2 %collective-permute-start.10 = (f32[512,128]{1,0:T(8,128)S(1)}, f32[512,128]{1,0:T(8,128)S(1)}, u32[]{:S(2)}, u32[]{:S(2)}) collective-permute-start(f32[512,128]{1,0:T(8,128)S(1)} %collective-permute-done.far_ref.rest_5_), channel_id=1, source_target_pairs={{0,32},{32,0},{64,96},{96,64},{128,160},{160,128},{192,224},{224,1... | collective-permute-start | bytes 786440 | tf_op jit(solution)/shard_map/ppermute | solution.py:311
  37.7 7.8 %collective-permute-start.7 = (f32[520,128]{1,0:T(8,128)S(1)}, f32[520,128]{1,0:T(8,128)S(1)}, u32[]{:S(2)}, u32[]{:S(2)}) collective-permute-start(f32[520,128]{1,0:T(8,128)S(1)} %last_gram.1.mine_ref), channel_id=1, source_target_pairs={{0,32},{32,0},{64,96},{96,64},{128,160},{160,128},{192,224},{224,1... | collective-permute-start | bytes 798728 | tf_op jit(solution)/shard_map/ppermute | solution.py:311
  40.1 26.9 %collective-permute-start.9 = (f32[1536,128]{1,0:T(8,128)}, f32[1536,128]{1,0:T(8,128)S(1)}, u32[]{:S(2)}, u32[]{:S(2)}) collective-permute-start(f32[1536,128]{1,0:T(8,128)} %collective-permute-done.1.far_ref.rest_4_), channel_id=1, source_target_pairs={{0,32},{32,0},{64,96},{96,64},{128,160},{160,128},{192,224},{224,1... | collective-permute-start | bytes 2359304 | tf_op jit(solution)/shard_map/ppermute | solution.py:311
  43.1 3.4 %collective-permute-start.8 = (f32[520,128]{1,0:T(8,128)S(1)}, f32[520,128]{1,0:T(8,128)S(1)}, u32[]{:S(2)}, u32[]{:S(2)}) collective-permute-start(f32[520,128]{1,0:T(8,128)S(1)} %collective-permute-done.6.far_ref), channel_id=1, source_target_pairs={{0,32},{32,0},{64,96},{96,64},{128,160},{160,128},{192,224},{224,1... | collective-permute-start | bytes 798728 | tf_op jit(solution)/shard_map/ppermute | solution.py:311
  56.0 5.5 %collective-permute-start.11 = (f32[8,128]{1,0:T(8,128)S(1)}, f32[8,128]{1,0:T(8,128)S(1)}, u32[]{:S(2)}, u32[]{:S(2)}) collective-permute-start(f32[8,128]{1,0:T(8,128)S(1)} %get-tuple-element.8), channel_id=1, source_target_pairs={{0,64},{32,96},{64,0},{96,32},{128,192},{160,224},{192,128},{224,1... | collective-permute-start | bytes 12296 | tf_op jit(solution)/shard_map/ppermute | solution.py:311
  61.5 5.5 %collective-permute-start.12 = (f32[8,128]{1,0:T(8,128)S(1)}, f32[8,128]{1,0:T(8,128)S(1)}, u32[]{:S(2)}, u32[]{:S(2)}) collective-permute-start(f32[8,128]{1,0:T(8,128)S(1)} %add.61), channel_id=1, source_target_pairs={{0,128},{32,160},{64,192},{96,224},{128,0},{160,32},{192,64},{224,... | collective-permute-start | bytes 12296 | tf_op jit(solution)/shard_map/ppermute | solution.py:311

commit v6 on v5

--- a/solution.py
+++ b/solution.py
@@ -163,7 +163,7 @@
     return jnp.sum((numbers == column.astype(F32)).astype(F32), axis=0, keepdims=True)
 
 
-def turn_kernel(place_ref, mine_ref, far_ref, next_ref, next_far_ref, turned_ref, norm_ref):
+def turn_kernel(place_ref, mine_ref, far_ref, next_ref, next_far_ref, first_ref, second_ref, norm_ref):
     width = mine_ref.shape[1]
     sign_far = jnp.where(place_ref[0] == 0, 1.0, -1.0)
     sign_next = jnp.where(place_ref[1] == 0, 1.0, -1.0)
@@ -196,44 +196,93 @@
     ]
     seconds = rotations(grams, sign_next)
 
+    first_ref[0], first_ref[1] = turn_01, turn_23
     total = jnp.zeros((1, 1), F32)
-    for number, (gram, second, which) in enumerate(zip(grams, seconds, (lo, hi))):
-        parts = split(second)
-        moved = product(split(gram), parts, NN) * second
+    for number, (gram, second) in enumerate(zip(grams, seconds)):
+        second_ref[number] = second[:, :width]
+        moved = product(split(gram), split(second), NN) * second
         kept = jnp.concatenate([kept_rows[number], kept_rows[number + 2]], 1)
         total += jnp.sum(jnp.sum(moved, axis=0, keepdims=True) * kept, axis=1, keepdims=True)
-        turned_ref[number] = jnp.concatenate(
+    norm_ref[...] = jnp.broadcast_to(total, norm_ref.shape)
+
+
+def turn(place, *values):
+    width = values[0].shape[1]
+    return pl.pallas_call(
+        turn_kernel,
+        in_specs=[SMEM] + [VMEM] * len(values),
+        out_specs=[VMEM] * 3,
+        out_shape=[
+            array(2, 2 * width, 2 * width),
+            array(2, 2 * width, width),
+            array(8, width),
+        ],
+        compiler_params=params(24),
+        name="turn",
+    )(place, *values)
+
+
+def route_kernel(first_ref, second_ref, route_ref, high_ref, low_ref):
+    width = second_ref.shape[2]
+    firsts = [split(first_ref[number]) for number in range(2)]
+    totals = [0.0, 0.0]
+    for number in range(2):
+        second = split(second_ref[number])
+        which = slice(number * width, (number + 1) * width)
+        turned = jnp.concatenate(
             [
-                product([p[:, which] for p in s_01], [p[lo, lo] for p in parts], NN),
-                product([p[:, which] for p in s_23], [p[hi, lo] for p in parts], NN),
+                product(
+                    [piece[:, which] for piece in first],
+                    [piece[side * width : (side + 1) * width] for piece in second],
+                    NN,
+                )
+                for side, first in enumerate(firsts)
             ],
             0,
         )
-    norm_ref[...] = jnp.broadcast_to(total, norm_ref.shape)
-
-
-def turn(place, *values):
-    width = values[0].shape[1]
-    return pl.pallas_call(
-        turn_kernel,
-        in_specs=[SMEM] + [VMEM] * len(values),
-        out_specs=[VMEM, VMEM],
-        out_shape=[array(2, 4 * width, width), array(8, width)],
-        compiler_params=params(24),
-        name="turn",
-    )(place, *values)
-
-
-def place_kernel(spans, count, place_ref, turned_ref, route_ref, block_ref, *rest):
+        route = route_ref[number].astype(BF16)
+        totals = [total + dot(piece, route, NN) for total, piece in zip(totals, split(turned))]
+    high_ref[...] = totals[0].astype(BF16)
+    low_ref[...] = totals[1].astype(BF16)
+
+
+def routed(first, second, routes):
+    shape = jax.ShapeDtypeStruct((2 * first.shape[1], routes.shape[2]), BF16)
+    return pl.pallas_call(
+        route_kernel,
+        in_specs=[VMEM] * 3,
+        out_specs=[VMEM] * 2,
+        out_shape=[shape, shape],
+        compiler_params=params(12),
+        cost_estimate=BRIEF,
+        name="routed",
+    )(first, second, routes)
+
+
+def sum_kernel(left_ref, right_ref, *rest):
+    rest[-1][...] = left_ref[...] + right_ref[...]
+
+
+def sum_after(left, right, *first):
+    return pl.pallas_call(
+        sum_kernel,
+        in_specs=[VMEM, VMEM] + [ANY] * len(first),
+        out_specs=VMEM,
+        out_shape=array(*left.shape),
+        compiler_params=params(8),
+        cost_estimate=BRIEF,
+        name="sum_after",
+    )(left, right, *first)
+
+
+def place_kernel(spans, count, place_ref, high_ref, low_ref, block_ref, *rest):
     next_refs, rest = rest[:count], rest[count:]
     far_refs, next_far_refs, out_ref = rest[: len(spans)], rest[len(spans) : 2 * len(spans)], rest[-1]
     width = block_ref.shape[1]
-    moved = []
-    for piece in zip(*[split(turned_ref[number]) for number in range(2)]):
-        total = sum(dot(piece[number], route_ref[number].astype(BF16), NN) for number in range(2))
-        moved.append(total.astype(BF16))
-    top = [piece[: 2 * width] for piece in moved]
-    bottom = [piece[2 * width :] for piece in moved]
+    top, bottom = [
+        [ref[side * 2 * width : (side + 1) * 2 * width] for ref in (high_ref, low_ref)]
+        for side in range(2)
+    ]
     done = 0
     for far_ref, next_far_ref, (start, span) in zip(far_refs, next_far_refs, spans):
         for tile in tiles(span.stop - span.start):
@@ -249,43 +298,43 @@
             done += size
 
 
-def placed(place, turned, routes, own, neighbour, far, next_far, spans, first=()):
+def placed(place, parts, own, neighbour, far, next_far, spans):
     width = own.shape[1]
     rows = sum(span.stop - span.start for _, span in spans)
     return pl.pallas_call(
         functools.partial(place_kernel, spans, len(neighbour)),
-        in_specs=[SMEM] + [VMEM] * (3 + len(neighbour) + 2 * len(far)) + [ANY] * len(first),
+        in_specs=[SMEM] + [VMEM] * (3 + len(neighbour) + 2 * len(far)),
         out_specs=VMEM,
-        out_shape=array(routes.shape[2], rows),
+        out_shape=array(parts[0].shape[1], rows),
         compiler_params=params(16),
         cost_estimate=pl.CostEstimate(
             flops=48 * rows * width * width, bytes_accessed=16 * rows * width, transcendentals=0
         ),
         name="placed",
-    )(place, turned, routes, own, *neighbour, *far, *next_far, *first)
+    )(place, *parts, own, *neighbour, *far, *next_far)
 
 
 def spread_kernel(total, *refs):
-    norm_ref, out_ref = refs[-2:]
-    scale = jnp.sqrt(total / norm_ref[0:1, 0:1])
+    norm_ref, other_ref, out_ref = refs[-3:]
+    scale = jnp.sqrt(total / (norm_ref[0:1, 0:1] + other_ref[0:1, 0:1]))
     done = 0
-    for ref in refs[:-2]:
+    for ref in refs[:-3]:
         for tile in range(ref.shape[1] // LANES):
             value = ref[:, tile * LANES : (tile + 1) * LANES] * scale
             out_ref[:, done] = value.reshape(out_ref.shape[0], out_ref.shape[2], LANES)
             done += 1
 
 
-def spread(values, norm, total, capacity):
+def spread(values, norms, total, capacity):
     count = sum(value.shape[1] for value in values) // LANES
     return pl.pallas_call(
         functools.partial(spread_kernel, total),
-        in_specs=[VMEM] * (len(values) + 1),
+        in_specs=[VMEM] * (len(values) + 2),
         out_specs=VMEM,
         out_shape=array(values[0].shape[0] // capacity, count, capacity, LANES),
         compiler_params=params(8),
         name="spread",
-    )(*values, norm)
+    )(*values, *norms)
 
 
 def join_kernel(tiles_ref, out_ref):
@@ -383,13 +432,16 @@
         ]
     )
 
-    turned, squares = turn(place, grams, far_grams, *next_grams)
+    first, second, squares = turn(place, grams, far_grams, *next_grams)
+    parts = routed(first, second, routes)
+    squares = sum_after(
+        squares, from_partner(squares, "bond", 2), parts[0], next_far_a, next_far_b
+    )
     outgoing = placed(
-        place, turned, routes, block, neighbour, (far_a, far_b), (next_far_a, next_far_b),
+        place, parts, block, neighbour, (far_a, far_b), (next_far_a, next_far_b),
         ((0, slice(0, sizes[0])), (sizes[0], slice(0, sizes[1]))),
     )
-    for distance in [1 << bit for bit in range(1, far.bit_length() - 1)]:
-        squares = squares + from_partner(squares, "bond", distance)
+    norms = (squares, from_partner(squares, "bond", 4))
     keep_count = keep_list.shape[1]
     capacity = max(2, 2 * keep_count // groups)
     order = member_order(groups)
@@ -398,7 +450,7 @@
         for first in range(far)
     ]
     arrived = lax.all_to_all(
-        spread([outgoing], squares, float(rows * count * keep_count), capacity),
+        spread([outgoing], norms, float(rows * count * keep_count), capacity),
         ("bond", "site"),
         split_axis=0,
         concat_axis=0,

time: 149 us -> 145 us (0.973)
  the two profiles are of different devices: /device:TPU:70 before, /device:TPU:16 now
where the time goes in v6:
time: 145 us
  blocking collectives  73.7 us (51%)
  starting transfers between devices  35.9 us (25%)
  Pallas kernels  20.1 us (14%)
  waiting for transfers between devices  7.94 us (5%)
  local copies, waits for them, and re-layouts  5.79 us (4%)
    all_to_all x1, blocking collectives, on_device(): lax.all_to_all(spread([outgoing], norms, float(rows * count * keep_count)...  73.7 us
    ppermute x13, starting transfers between devices, from_partner(): return lax.ppermute(value, axis, pairs)  35.9 us
    pallas_call x1, Pallas kernels, turn(): pl.pallas_call(turn_kernel, in_specs=[SMEM] + [VMEM] * len(values), out_s...  9.46 us
    ppermute x13, waiting for transfers between devices, from_partner(): return lax.ppermute(value, axis, pairs)  7.94 us
    pallas_call x2, Pallas kernels, gram_call(): pl.pallas_call(kernel, in_specs=[SMEM] + [VMEM] * len(values), out_specs=...  4.33 us
    pallas_call x1, Pallas kernels, placed(): pl.pallas_call(functools.partial(place_kernel, spans, len(neighbour)), in...  3.51 us
  transfers between devices with their start and end apart: 13, of which 4 were waited for; matrix products, arithmetic and copies ran while one was open for 3% of the time, Pallas kernels for 11%

profile of v6, /device:TPU:16, one launch (start us, length us, event | category | flops | bytes accessed | tf_op | source)
XLA Modules:
  0.0 144.8 jit_solution(9263256478996181848)
XLA Ops:
  0.0 2.1 %dynamic-slice_bitcast_fusion = f32[1536,128]{1,0:T(8,128)} fusion(f32[1,4096,128]{2,1,0:T(8,128)} %param.5, s32[]{:T(128)S(6)} %select_n.20), kind=kLoop, calls=%fused_computation.2 | loop fusion | bytes 1572868 | tf_op jit(solution)/shard_map/dynamic_slice | solution.py:411
  2.1 5.1 %collective-permute-start.1 = (f32[1536,128]{1,0:T(8,128)}, f32[1536,128]{1,0:T(8,128)}, u32[]{:S(2)}, u32[]{:S(2)}) collective-permute-start(f32[1536,128]{1,0:T(8,128)} %dynamic-slice_bitcast_fusion), channel_id=1, source_target_pairs={{0,256},{32,288},{64,320},{96,352},{128,384},{160,416},{192,448},{... | collective-permute-start | bytes 2359304 | tf_op jit(solution)/shard_map/ppermute | solution.py:360
  7.1 2.9 %slice_bitcast_fusion = (f32[1024,128]{1,0:T(8,128)}, f32[1024,128]{1,0:T(8,128)}, f32[1024,128]{1,0:T(8,128)}, f32[1024,128]{1,0:T(8,128)}) fusion(f32[1,4096,128]{2,1,0:T(8,128)} %param.5), kind=kLoop, calls=%fused_computation.3 | loop fusion | bytes 4194304 | tf_op jit(solution)/shard_map/slice | solution.py:416
  10.0 1.9 %collective-permute-start.5 = (f32[1024,128]{1,0:T(8,128)}, f32[1024,128]{1,0:T(8,128)S(1)}, u32[]{:S(2)}, u32[]{:S(2)}) collective-permute-start(f32[1024,128]{1,0:T(8,128)} %get-tuple-element.19), channel_id=1, source_target_pairs={{0,32},{32,0},{64,96},{96,64},{128,160},{160,128},{192,224},{224,1... | collective-permute-start | bytes 1572872 | tf_op jit(solution)/shard_map/ppermute | solution.py:360
  11.9 2.4 %collective-permute-start.3 = (f32[1024,128]{1,0:T(8,128)}, f32[1024,128]{1,0:T(8,128)S(1)}, u32[]{:S(2)}, u32[]{:S(2)}) collective-permute-start(f32[1024,128]{1,0:T(8,128)} %get-tuple-element.20), channel_id=1, source_target_pairs={{0,32},{32,0},{64,96},{96,64},{128,160},{160,128},{192,224},{224,1... | collective-permute-start | bytes 1572872 | tf_op jit(solution)/shard_map/ppermute | solution.py:360
  14.3 1.9 %collective-permute-start.2 = (f32[1024,128]{1,0:T(8,128)}, f32[1024,128]{1,0:T(8,128)}, u32[]{:S(2)}, u32[]{:S(2)}) collective-permute-start(f32[1024,128]{1,0:T(8,128)} %get-tuple-element.21), channel_id=1, source_target_pairs={{0,32},{32,0},{64,96},{96,64},{128,160},{160,128},{192,224},{224,1... | collective-permute-start | bytes 1572872 | tf_op jit(solution)/shard_map/ppermute | solution.py:360
  16.2 2.4 %collective-permute-start.4 = (f32[1024,128]{1,0:T(8,128)}, f32[1024,128]{1,0:T(8,128)}, u32[]{:S(2)}, u32[]{:S(2)}) collective-permute-start(f32[1024,128]{1,0:T(8,128)} %get-tuple-element.22), channel_id=1, source_target_pairs={{0,32},{32,0},{64,96},{96,64},{128,160},{160,128},{192,224},{224,1... | collective-permute-start | bytes 1572872 | tf_op jit(solution)/shard_map/ppermute | solution.py:360
  18.7 0.7 constant_dynamic-slice_fusion
  19.4 0.0 collective-permute-done.5.rest_3_
  19.4 2.4 %collective-permute-start = (f32[512,128]{1,0:T(8,128)}, f32[512,128]{1,0:T(8,128)S(1)}, u32[]{:S(2)}, u32[]{:S(2)}) collective-permute-start(f32[512,128]{1,0:T(8,128)} %constant_dynamic-slice_fusion), channel_id=1, source_target_pairs={{0,256},{32,288},{64,320},{96,352},{128,384},{160,416},{192,448},{... | collective-permute-start | bytes 786440 | tf_op jit(solution)/shard_map/ppermute | solution.py:360
  21.8 0.1 pad_add_fusion.place_ref
  21.9 0.0 copy-done.2
  21.9 0.1 fusion.6
  22.0 0.0 collective-permute-done.3.rest_1_
  22.0 0.0 collective-permute-done.2.rest_0_
  22.0 0.0 collective-permute-done.4.rest_2_
  22.0 3.4 %collective-permute-done.1.far_ref.rest_4_ = f32[1536,128]{1,0:T(8,128)} collective-permute-done((f32[1536,128]{1,0:T(8,128)}, f32[1536,128]{1,0:T(8,128)}, u32[]{:S(2)}, u32[]{:S(2)}) %collective-permute-start.1) | collective-permute-done | bytes 786464 | tf_op jit(solution)/shard_map/ppermute | solution.py:360
  25.4 2.8 %first_gram.1.before_ref = f32[520,128]{1,0:T(8,128)S(1)} custom-call(s32[2]{0:T(128)S(1)} %pad_add_fusion.place_ref, f32[4096,128]{1,0:T(8,128)S(1)} %bitcast.26, f32[1536,128]{1,0:T(8,128)} %collective-permute-done.1.far_ref.rest_4_, f32[8,128]{1,0:T(8,128)S(1)} %broadcast_in_dim.14.listed_ref, f32[1024,128]{1,0:T(8,128)} %collective-permute-done.2.rest_0_, ...), custom_call_target="tpu_custom_call" | custom-call | flops 1 | bytes 1 | tf_op jit(solution)/shard_map/first_gram/pallas_call | solution.py:116
  28.2 0.0 copy-start.1
  28.2 3.0 %collective-permute-done.far_ref.rest_5_ = f32[512,128]{1,0:T(8,128)S(1)} collective-permute-done((f32[512,128]{1,0:T(8,128)}, f32[512,128]{1,0:T(8,128)S(1)}, u32[]{:S(2)}, u32[]{:S(2)}) %collective-permute-start) | collective-permute-done | bytes 262176 | tf_op jit(solution)/shard_map/ppermute | solution.py:360
  31.2 1.5 %last_gram.1.mine_ref = f32[520,128]{1,0:T(8,128)S(1)} custom-call(s32[2]{0:T(128)S(1)} %pad_add_fusion.place_ref, f32[4096,128]{1,0:T(8,128)S(1)} %bitcast.27, f32[512,128]{1,0:T(8,128)S(1)} %collective-permute-done.far_ref.rest_5_, f32[520,128]{1,0:T(8,128)S(1)} %first_gram.1.before_ref, f32[1024,128]{1,0:T(8,128)} %collective-permute-done.2.rest_0_, ...), custom_call_target="tpu_custom_call" | custom-call | flops 1 | bytes 1 | tf_op jit(solution)/shard_map/last_gram/pallas_call | solution.py:116
  32.7 4.4 %collective-permute-start.6 = (f32[520,128]{1,0:T(8,128)S(1)}, f32[520,128]{1,0:T(8,128)S(1)}, u32[]{:S(2)}, u32[]{:S(2)}) collective-permute-start(f32[520,128]{1,0:T(8,128)S(1)} %last_gram.1.mine_ref), channel_id=1, source_target_pairs={{0,256},{32,288},{64,320},{96,352},{128,384},{160,416},{192,448},{... | collective-permute-start | bytes 798728 | tf_op jit(solution)/shard_map/ppermute | solution.py:360
  37.2 0.1 fusion.7
  37.2 0.2 convert_reduce_fusion.1
  37.4 1.9 %collective-permute-start.10 = (f32[512,128]{1,0:T(8,128)S(1)}, f32[512,128]{1,0:T(8,128)S(1)}, u32[]{:S(2)}, u32[]{:S(2)}) collective-permute-start(f32[512,128]{1,0:T(8,128)S(1)} %collective-permute-done.far_ref.rest_5_), channel_id=1, source_target_pairs={{0,32},{32,0},{64,96},{96,64},{128,160},{160,128},{192,224},{224,1... | collective-permute-start | bytes 786440 | tf_op jit(solution)/shard_map/ppermute | solution.py:360
  39.4 2.4 %collective-permute-start.7 = (f32[520,128]{1,0:T(8,128)S(1)}, f32[520,128]{1,0:T(8,128)S(1)}, u32[]{:S(2)}, u32[]{:S(2)}) collective-permute-start(f32[520,128]{1,0:T(8,128)S(1)} %last_gram.1.mine_ref), channel_id=1, source_target_pairs={{0,32},{32,0},{64,96},{96,64},{128,160},{160,128},{192,224},{224,1... | collective-permute-start | bytes 798728 | tf_op jit(solution)/shard_map/ppermute | solution.py:360
  41.8 1.9 %collective-permute-start.9 = (f32[1536,128]{1,0:T(8,128)}, f32[1536,128]{1,0:T(8,128)S(1)}, u32[]{:S(2)}, u32[]{:S(2)}) collective-permute-start(f32[1536,128]{1,0:T(8,128)} %collective-permute-done.1.far_ref.rest_4_), channel_id=1, source_target_pairs={{0,32},{32,0},{64,96},{96,64},{128,160},{160,128},{192,224},{224,1... | collective-permute-start | bytes 2359304 | tf_op jit(solution)/shard_map/ppermute | solution.py:360
  43.7 0.0 collective-permute-done.6.far_ref
  43.7 0.1 slice_bitcast_fusion.5
  43.8 2.4 %collective-permute-start.8 = (f32[520,128]{1,0:T(8,128)S(1)}, f32[520,128]{1,0:T(8,128)S(1)}, u32[]{:S(2)}, u32[]{:S(2)}) collective-permute-start(f32[520,128]{1,0:T(8,128)S(1)} %collective-permute-done.6.far_ref), channel_id=1, source_target_pairs={{0,32},{32,0},{64,96},{96,64},{128,160},{160,128},{192,224},{224,1... | collective-permute-start | bytes 798728 | tf_op jit(solution)/shard_map/ppermute | solution.py:360
  46.2 0.2 convert_reduce_fusion
  46.4 0.1 select_reduce_fusion.1
  46.5 0.3 convolution_bitcast_fusion
  46.8 0.3 convolution_bitcast_fusion.1
  47.1 0.0 collective-permute-done.7.next_ref
  47.1 0.3 collective-permute-done.8.next_far_ref
  47.3 9.5 %turn.1 = (f32[2,256,256]{2,1,0:T(8,128)S(1)}, f32[2,256,128]{2,1,0:T(8,128)S(1)}, f32[8,128]{1,0:T(8,128)S(1)}) custom-call(s32[2]{0:T(128)S(1)} %pad_add_fusion.place_ref, f32[520,128]{1,0:T(8,128)S(1)} %last_gram.1.mine_ref, f32[520,128]{1,0:T(8,128)S(1)} %collective-permute-done.6.far_ref, f32[520,128]{1,0:T(8,128)S(1)} %collective-permute-done.7.next_ref, ...), custom_call_target="tpu_custom_call" | custom-call | tf_op jit(solution)/shard_map/turn/pallas_call | solution.py:211
  56.8 3.5 %collective-permute-start.11 = (f32[8,128]{1,0:T(8,128)S(1)}, f32[8,128]{1,0:T(8,128)S(1)}, u32[]{:S(2)}, u32[]{:S(2)}) collective-permute-start(f32[8,128]{1,0:T(8,128)S(1)} %get-tuple-element.14.left_ref), channel_id=1, source_target_pairs={{0,64},{32,96},{64,0},{96,32},{128,192},{160,224},{192,128},{224,1... | collective-permute-start | bytes 12296 | tf_op jit(solution)/shard_map/ppermute | solution.py:360
  60.3 0.7 routed.1
  61.1 0.0 collective-permute-done.10.rest_7_.rest_2_
  61.1 1.2 collective-permute-done.11.right_ref
  62.3 0.0 collective-permute-done.9.rest_6_.rest_1_
  62.3 3.2 %collective-permute-start.12 = (f32[8,128]{1,0:T(8,128)S(1)}, f32[8,128]{1,0:T(8,128)S(1)}, u32[]{:S(2)}, u32[]{:S(2)}) collective-permute-start(f32[8,128]{1,0:T(8,128)S(1)} %sum_after.1.refs_1_), channel_id=1, source_target_pairs={{0,128},{32,160},{64,192},{96,224},{128,0},{160,32},{192,64},{224,... | collective-permute-start | bytes 12296 | tf_op jit(solution)/shard_map/ppermute | solution.py:360
  65.5 3.5 %placed.1.refs_0_ = f32[256,2048]{1,0:T(8,128)S(1)} custom-call(s32[2]{0:T(128)S(1)} %pad_add_fusion.place_ref, bf16[512,256]{1,0:T(8,128)(2,1)S(1)} %get-tuple-element.12.high_ref.rest_0_, bf16[512,256]{1,0:T(8,128)(2,1)S(1)} %get-tuple-element.13.low_ref, f32[4096,128]{1,0:T(8,128)S(1)} %bitcast.28, f32[1024,128]{1,0:T(8,128)} %collective-permute-done.2.rest_0_, ...), custom_call_target="tpu_custom_call" | custom-call | flops 1610612736 | bytes 4194304 | tf_op jit(solution)/shard_map/placed/pallas_call | solution.py:304
  69.1 0.0 collective-permute-done.12.refs_2_
  69.1 0.6 spread.1
  69.7 73.7 %all_to_all.5 = f32[64,16,4,128]{3,2,1,0:T(4,128)S(1)} all-to-all(f32[64,16,4,128]{3,2,1,0:T(4,128)S(1)} %spread.1), channel_id=1, replica_groups={{0,256,8,264,1,257,9,265,2,258,10,266,3,259,11,267,4,260,12,268,5,261,1..., dimensions={0} | all-to-all | bytes 4194304 | tf_op jit(solution)/shard_map/all_to_all | solution.py:452
  143.3 1.5 %join.1 = f32[32,4,4096]{2,1,0:T(4,128)} custom-call(f32[32,32,4,128]{3,2,1,0:T(4,128)S(1)} %bitcast.29), custom_call_target="tpu_custom_call" | custom-call | tf_op jit(solution)/shard_map/join/pallas_call | solution.py:348
  (11 shorter events, 0.1 us)
Async XLA Ops:
  2.1 16.6 %copy-start = (f32[1,4096,128]{2,1,0:T(8,128)S(1)}, f32[1,4096,128]{2,1,0:T(8,128)}, u32[]{:S(2)}) copy-start(f32[1,4096,128]{2,1,0:T(8,128)} %param.5) | copy-start | bytes 6291460
  2.1 19.8 %copy-start.2 = (s32[1,64,1]{1,2,0:T(1,128)S(1)}, s32[1,64,1]{1,2,0:T(1,128)}, u32[]{:S(2)}) copy-start(s32[1,64,1]{1,2,0:T(1,128)} %param.7) | copy-start | bytes 772
  2.1 19.8 %copy-start.3 = (s32[1,64]{1,0:T(1,128)S(1)}, s32[1,64]{1,0:T(1,128)}, u32[]{:S(2)}) copy-start(s32[1,64]{1,0:T(1,128)} %param.6) | copy-start | bytes 772
  2.1 23.3 %collective-permute-start.1 = (f32[1536,128]{1,0:T(8,128)}, f32[1536,128]{1,0:T(8,128)}, u32[]{:S(2)}, u32[]{:S(2)}) collective-permute-start(f32[1536,128]{1,0:T(8,128)} %dynamic-slice_bitcast_fusion), channel_id=1, source_target_pairs={{0,256},{32,288},{64,320},{96,352},{128,384},{160,416},{192,448},{... | collective-permute-start | bytes 2359304 | tf_op jit(solution)/shard_map/ppermute | solution.py:360
  10.0 9.4 %collective-permute-start.5 = (f32[1024,128]{1,0:T(8,128)}, f32[1024,128]{1,0:T(8,128)S(1)}, u32[]{:S(2)}, u32[]{:S(2)}) collective-permute-start(f32[1024,128]{1,0:T(8,128)} %get-tuple-element.19), channel_id=1, source_target_pairs={{0,32},{32,0},{64,96},{96,64},{128,160},{160,128},{192,224},{224,1... | collective-permute-start | bytes 1572872 | tf_op jit(solution)/shard_map/ppermute | solution.py:360
  11.9 10.1 %collective-permute-start.3 = (f32[1024,128]{1,0:T(8,128)}, f32[1024,128]{1,0:T(8,128)S(1)}, u32[]{:S(2)}, u32[]{:S(2)}) collective-permute-start(f32[1024,128]{1,0:T(8,128)} %get-tuple-element.20), channel_id=1, source_target_pairs={{0,32},{32,0},{64,96},{96,64},{128,160},{160,128},{192,224},{224,1... | collective-permute-start | bytes 1572872 | tf_op jit(solution)/shard_map/ppermute | solution.py:360
  14.3 7.7 %collective-permute-start.2 = (f32[1024,128]{1,0:T(8,128)}, f32[1024,128]{1,0:T(8,128)}, u32[]{:S(2)}, u32[]{:S(2)}) collective-permute-start(f32[1024,128]{1,0:T(8,128)} %get-tuple-element.21), channel_id=1, source_target_pairs={{0,32},{32,0},{64,96},{96,64},{128,160},{160,128},{192,224},{224,1... | collective-permute-start | bytes 1572872 | tf_op jit(solution)/shard_map/ppermute | solution.py:360
  16.2 5.7 %collective-permute-start.4 = (f32[1024,128]{1,0:T(8,128)}, f32[1024,128]{1,0:T(8,128)}, u32[]{:S(2)}, u32[]{:S(2)}) collective-permute-start(f32[1024,128]{1,0:T(8,128)} %get-tuple-element.22), channel_id=1, source_target_pairs={{0,32},{32,0},{64,96},{96,64},{128,160},{160,128},{192,224},{224,1... | collective-permute-start | bytes 1572872 | tf_op jit(solution)/shard_map/ppermute | solution.py:360
  19.4 11.8 %collective-permute-start = (f32[512,128]{1,0:T(8,128)}, f32[512,128]{1,0:T(8,128)S(1)}, u32[]{:S(2)}, u32[]{:S(2)}) collective-permute-start(f32[512,128]{1,0:T(8,128)} %constant_dynamic-slice_fusion), channel_id=1, source_target_pairs={{0,256},{32,288},{64,320},{96,352},{128,384},{160,416},{192,448},{... | collective-permute-start | bytes 786440 | tf_op jit(solution)/shard_map/ppermute | solution.py:360
  28.2 18.2 %copy-start.1 = (s32[32]{0:T(128)S(1)}, s32[32]{0:T(128)}, u32[]{:S(2)}) copy-start(s32[32]{0:T(128)} %constant.39.clone) | copy-start | bytes 388
  32.7 11.0 %collective-permute-start.6 = (f32[520,128]{1,0:T(8,128)S(1)}, f32[520,128]{1,0:T(8,128)S(1)}, u32[]{:S(2)}, u32[]{:S(2)}) collective-permute-start(f32[520,128]{1,0:T(8,128)S(1)} %last_gram.1.mine_ref), channel_id=1, source_target_pairs={{0,256},{32,288},{64,320},{96,352},{128,384},{160,416},{192,448},{... | collective-permute-start | bytes 798728 | tf_op jit(solution)/shard_map/ppermute | solution.py:360
  37.4 23.7 %collective-permute-start.10 = (f32[512,128]{1,0:T(8,128)S(1)}, f32[512,128]{1,0:T(8,128)S(1)}, u32[]{:S(2)}, u32[]{:S(2)}) collective-permute-start(f32[512,128]{1,0:T(8,128)S(1)} %collective-permute-done.far_ref.rest_5_), channel_id=1, source_target_pairs={{0,32},{32,0},{64,96},{96,64},{128,160},{160,128},{192,224},{224,1... | collective-permute-start | bytes 786440 | tf_op jit(solution)/shard_map/ppermute | solution.py:360
  39.4 7.7 %collective-permute-start.7 = (f32[520,128]{1,0:T(8,128)S(1)}, f32[520,128]{1,0:T(8,128)S(1)}, u32[]{:S(2)}, u32[]{:S(2)}) collective-permute-start(f32[520,128]{1,0:T(8,128)S(1)} %last_gram.1.mine_ref), channel_id=1, source_target_pairs={{0,32},{32,0},{64,96},{96,64},{128,160},{160,128},{192,224},{224,1... | collective-permute-start | bytes 798728 | tf_op jit(solution)/shard_map/ppermute | solution.py:360
  41.8 20.6 %collective-permute-start.9 = (f32[1536,128]{1,0:T(8,128)}, f32[1536,128]{1,0:T(8,128)S(1)}, u32[]{:S(2)}, u32[]{:S(2)}) collective-permute-start(f32[1536,128]{1,0:T(8,128)} %collective-permute-done.1.far_ref.rest_4_), channel_id=1, source_target_pairs={{0,32},{32,0},{64,96},{96,64},{128,160},{160,128},{192,224},{224,1... | collective-permute-start | bytes 2359304 | tf_op jit(solution)/shard_map/ppermute | solution.py:360
  43.8 3.5 %collective-permute-start.8 = (f32[520,128]{1,0:T(8,128)S(1)}, f32[520,128]{1,0:T(8,128)S(1)}, u32[]{:S(2)}, u32[]{:S(2)}) collective-permute-start(f32[520,128]{1,0:T(8,128)S(1)} %collective-permute-done.6.far_ref), channel_id=1, source_target_pairs={{0,32},{32,0},{64,96},{96,64},{128,160},{160,128},{192,224},{224,1... | collective-permute-start | bytes 798728 | tf_op jit(solution)/shard_map/ppermute | solution.py:360
  56.8 5.5 %collective-permute-start.11 = (f32[8,128]{1,0:T(8,128)S(1)}, f32[8,128]{1,0:T(8,128)S(1)}, u32[]{:S(2)}, u32[]{:S(2)}) collective-permute-start(f32[8,128]{1,0:T(8,128)S(1)} %get-tuple-element.14.left_ref), channel_id=1, source_target_pairs={{0,64},{32,96},{64,0},{96,32},{128,192},{160,224},{192,128},{224,1... | collective-permute-start | bytes 12296 | tf_op jit(solution)/shard_map/ppermute | solution.py:360
  62.3 6.7 %collective-permute-start.12 = (f32[8,128]{1,0:T(8,128)S(1)}, f32[8,128]{1,0:T(8,128)S(1)}, u32[]{:S(2)}, u32[]{:S(2)}) collective-permute-start(f32[8,128]{1,0:T(8,128)S(1)} %sum_after.1.refs_1_), channel_id=1, source_target_pairs={{0,128},{32,160},{64,192},{96,224},{128,0},{160,32},{192,64},{224,... | collective-permute-start | bytes 12296 | tf_op jit(solution)/shard_map/ppermute | solution.py:360

commit v7 on v6

--- a/solution.py
+++ b/solution.py
@@ -38,8 +38,11 @@
 
 
 def product(left, right, contract):
-    return dot(left[0], right[0], contract) + (
-        dot(left[0], right[1], contract) + dot(left[1], right[0], contract)
+    (along_left,), (along_right,) = contract
+    return dot(
+        jnp.concatenate([left[0], left[0], left[1]], along_left),
+        jnp.concatenate([right[0], right[1], right[0]], along_right),
+        contract,
     )
 
 
@@ -338,9 +341,8 @@
 
 
 def join_kernel(tiles_ref, out_ref):
-    for member, site in enumerate(member_order(tiles_ref.shape[0])):
-        for tile in range(tiles_ref.shape[1]):
-            out_ref[site, :, tile * LANES : (tile + 1) * LANES] = tiles_ref[member, tile]
+    for tile in range(tiles_ref.shape[1]):
+        out_ref[:, :, tile * LANES : (tile + 1) * LANES] = tiles_ref[:, tile]
 
 
 def join(tiles):
@@ -358,17 +360,6 @@
 def from_partner(value, axis, distance):
     pairs = [(source, source ^ distance) for source in range(lax.axis_size(axis))]
     return lax.ppermute(value, axis, pairs)
-
-
-def member_order(groups):
-    if groups % 32:
-        return list(range(groups))
-    return [
-        16 * high + 8 * low + z
-        for high in range(groups // 16)
-        for z in range(8)
-        for low in range(2)
-    ]
 
 
 def route_of(listed, side, groups):
@@ -379,12 +370,7 @@
     same = owners[:, None] == owners[None, :]
     slot = jnp.sum((same & (order[None, :] < order[:, None])).astype(jnp.int32), axis=1)
     capacity = max(2, 2 * kept // groups)
-    order_of = member_order(groups)
-    rank = jnp.array([order_of.index(site) for site in range(groups)], jnp.int32)
-    ranks = jnp.sum(
-        jnp.where(owners[:, None] == jnp.arange(groups, dtype=jnp.int32), rank, 0), axis=1
-    )
-    target = (ranks * 2 + side) * capacity + slot
+    target = (owners * 2 + side) * capacity + slot
     places = jnp.arange(2 * groups * capacity, dtype=jnp.int32)
     columns = jnp.arange(width, dtype=jnp.int32)
     picked = (keep[:, None] == columns[None, :]).astype(BF16)
@@ -444,9 +430,8 @@
     norms = (squares, from_partner(squares, "bond", 4))
     keep_count = keep_list.shape[1]
     capacity = max(2, 2 * keep_count // groups)
-    order = member_order(groups)
     members = [
-        [(first + far * side) * groups + site for site in order for side in range(2)]
+        [(first + far * side) * groups + site for site in range(groups) for side in range(2)]
         for first in range(far)
     ]
     arrived = lax.all_to_all(

time: 145 us -> 150 us (1.034)
  the two profiles are of different devices: /device:TPU:16 before, /device:TPU:56 now
where the time goes in v7:
time: 150 us
  blocking collectives  73.8 us (49%)
  starting transfers between devices  35.9 us (24%)
  Pallas kernels  20.1 us (13%)
  waiting for transfers between devices  13.4 us (9%)
  local copies, waits for them, and re-layouts  4.82 us (3%)
    all_to_all x1, blocking collectives, on_device(): lax.all_to_all(spread([outgoing], norms, float(rows * count * keep_count)...  73.8 us
    ppermute x13, starting transfers between devices, from_partner(): return lax.ppermute(value, axis, pairs)  35.9 us
    ppermute x13, waiting for transfers between devices, from_partner(): return lax.ppermute(value, axis, pairs)  13.4 us
    pallas_call x1, Pallas kernels, turn(): pl.pallas_call(turn_kernel, in_specs=[SMEM] + [VMEM] * len(values), out_s...  9.46 us
    pallas_call x2, Pallas kernels, gram_call(): pl.pallas_call(kernel, in_specs=[SMEM] + [VMEM] * len(values), out_specs=...  4.36 us
    pallas_call x1, Pallas kernels, placed(): pl.pallas_call(functools.partial(place_kernel, spans, len(neighbour)), in...  3.52 us
    slice x1, local copies, waits for them, and re-layouts, on_device(): block[number * quarter:(number + 1) * quarter]  3.01 us
  transfers between devices with their start and end apart: 13, of which 4 were waited for; matrix products, arithmetic and copies ran while one was open for 2% of the time, Pallas kernels for 11%

profile of v7, /device:TPU:56, one launch (start us, length us, event | category | flops | bytes accessed | tf_op | source)
XLA Modules:
  0.0 149.6 jit_solution(3162322154097362462)
XLA Ops:
  0.0 3.0 %slice_bitcast_fusion = (f32[1024,128]{1,0:T(8,128)}, f32[1024,128]{1,0:T(8,128)}, f32[1024,128]{1,0:T(8,128)}, f32[1024,128]{1,0:T(8,128)}) fusion(f32[1,4096,128]{2,1,0:T(8,128)} %param.3), kind=kLoop, calls=%fused_computation.3 | loop fusion | bytes 4194304 | tf_op jit(solution)/shard_map/slice | solution.py:402
  3.0 2.0 %collective-permute-start.5 = (f32[1024,128]{1,0:T(8,128)}, f32[1024,128]{1,0:T(8,128)S(1)}, u32[]{:S(2)}, u32[]{:S(2)}) collective-permute-start(f32[1024,128]{1,0:T(8,128)} %get-tuple-element.17), channel_id=1, source_target_pairs={{0,32},{32,0},{64,96},{96,64},{128,160},{160,128},{192,224},{224,1... | collective-permute-start | bytes 1572872 | tf_op jit(solution)/shard_map/ppermute | solution.py:362
  5.1 0.9 dynamic-slice_bitcast_fusion
  6.0 4.9 %collective-permute-start.1 = (f32[1536,128]{1,0:T(8,128)}, f32[1536,128]{1,0:T(8,128)}, u32[]{:S(2)}, u32[]{:S(2)}) collective-permute-start(f32[1536,128]{1,0:T(8,128)} %dynamic-slice_bitcast_fusion), channel_id=1, source_target_pairs={{0,256},{32,288},{64,320},{96,352},{128,384},{160,416},{192,448},{... | collective-permute-start | bytes 2359304 | tf_op jit(solution)/shard_map/ppermute | solution.py:362
  11.0 2.1 %collective-permute-start.3 = (f32[1024,128]{1,0:T(8,128)}, f32[1024,128]{1,0:T(8,128)S(1)}, u32[]{:S(2)}, u32[]{:S(2)}) collective-permute-start(f32[1024,128]{1,0:T(8,128)} %get-tuple-element.18), channel_id=1, source_target_pairs={{0,32},{32,0},{64,96},{96,64},{128,160},{160,128},{192,224},{224,1... | collective-permute-start | bytes 1572872 | tf_op jit(solution)/shard_map/ppermute | solution.py:362
  13.1 2.2 %collective-permute-start.2 = (f32[1024,128]{1,0:T(8,128)}, f32[1024,128]{1,0:T(8,128)}, u32[]{:S(2)}, u32[]{:S(2)}) collective-permute-start(f32[1024,128]{1,0:T(8,128)} %get-tuple-element.19), channel_id=1, source_target_pairs={{0,32},{32,0},{64,96},{96,64},{128,160},{160,128},{192,224},{224,1... | collective-permute-start | bytes 1572872 | tf_op jit(solution)/shard_map/ppermute | solution.py:362
  15.3 2.1 %collective-permute-start.4 = (f32[1024,128]{1,0:T(8,128)}, f32[1024,128]{1,0:T(8,128)}, u32[]{:S(2)}, u32[]{:S(2)}) collective-permute-start(f32[1024,128]{1,0:T(8,128)} %get-tuple-element.20), channel_id=1, source_target_pairs={{0,32},{32,0},{64,96},{96,64},{128,160},{160,128},{192,224},{224,1... | collective-permute-start | bytes 1572872 | tf_op jit(solution)/shard_map/ppermute | solution.py:362
  17.4 0.7 constant_dynamic-slice_fusion
  18.2 0.0 collective-permute-done.5.rest_3_
  18.2 2.4 %collective-permute-start = (f32[512,128]{1,0:T(8,128)}, f32[512,128]{1,0:T(8,128)S(1)}, u32[]{:S(2)}, u32[]{:S(2)}) collective-permute-start(f32[512,128]{1,0:T(8,128)} %constant_dynamic-slice_fusion), channel_id=1, source_target_pairs={{0,256},{32,288},{64,320},{96,352},{128,384},{160,416},{192,448},{... | collective-permute-start | bytes 786440 | tf_op jit(solution)/shard_map/ppermute | solution.py:362
  20.6 0.0 copy-done.1
  20.6 0.1 fusion.6
  20.7 0.1 unstack.19
  20.8 0.1 pad_add_fusion.place_ref
  20.8 0.2 convert_reduce_fusion.1
  21.0 0.0 collective-permute-done.3.rest_1_
  21.0 0.0 collective-permute-done.2.rest_0_
  21.0 0.0 collective-permute-done.4.rest_2_
  21.0 9.0 %collective-permute-done.1.far_ref.rest_4_ = f32[1536,128]{1,0:T(8,128)} collective-permute-done((f32[1536,128]{1,0:T(8,128)}, f32[1536,128]{1,0:T(8,128)}, u32[]{:S(2)}, u32[]{:S(2)}) %collective-permute-start.1) | collective-permute-done | bytes 786464 | tf_op jit(solution)/shard_map/ppermute | solution.py:362
  30.1 2.8 %first_gram.1.before_ref = f32[520,128]{1,0:T(8,128)S(1)} custom-call(s32[2]{0:T(128)S(1)} %pad_add_fusion.place_ref, f32[4096,128]{1,0:T(8,128)S(1)} %bitcast.28, f32[1536,128]{1,0:T(8,128)} %collective-permute-done.1.far_ref.rest_4_, f32[8,128]{1,0:T(8,128)S(1)} %broadcast_in_dim.2.listed_ref, f32[1024,128]{1,0:T(8,128)} %collective-permute-done.2.rest_0_, ...), custom_call_target="tpu_custom_call" | custom-call | flops 1 | bytes 1 | tf_op jit(solution)/shard_map/first_gram/pallas_call | solution.py:119
  32.9 2.3 %collective-permute-done.far_ref.rest_5_ = f32[512,128]{1,0:T(8,128)S(1)} collective-permute-done((f32[512,128]{1,0:T(8,128)}, f32[512,128]{1,0:T(8,128)S(1)}, u32[]{:S(2)}, u32[]{:S(2)}) %collective-permute-start) | collective-permute-done | bytes 262176 | tf_op jit(solution)/shard_map/ppermute | solution.py:362
  35.2 1.5 %last_gram.1.mine_ref = f32[520,128]{1,0:T(8,128)S(1)} custom-call(s32[2]{0:T(128)S(1)} %pad_add_fusion.place_ref, f32[4096,128]{1,0:T(8,128)S(1)} %bitcast.29, f32[512,128]{1,0:T(8,128)S(1)} %collective-permute-done.far_ref.rest_5_, f32[520,128]{1,0:T(8,128)S(1)} %first_gram.1.before_ref, f32[1024,128]{1,0:T(8,128)} %collective-permute-done.2.rest_0_, ...), custom_call_target="tpu_custom_call" | custom-call | flops 1 | bytes 1 | tf_op jit(solution)/shard_map/last_gram/pallas_call | solution.py:119
  36.7 4.9 %collective-permute-start.6 = (f32[520,128]{1,0:T(8,128)S(1)}, f32[520,128]{1,0:T(8,128)S(1)}, u32[]{:S(2)}, u32[]{:S(2)}) collective-permute-start(f32[520,128]{1,0:T(8,128)S(1)} %last_gram.1.mine_ref), channel_id=1, source_target_pairs={{0,256},{32,288},{64,320},{96,352},{128,384},{160,416},{192,448},{... | collective-permute-start | bytes 798728 | tf_op jit(solution)/shard_map/ppermute | solution.py:362
  41.7 0.1 fusion.7
  41.7 0.3 convolution_bitcast_fusion.1
  42.0 1.9 %collective-permute-start.10 = (f32[512,128]{1,0:T(8,128)S(1)}, f32[512,128]{1,0:T(8,128)S(1)}, u32[]{:S(2)}, u32[]{:S(2)}) collective-permute-start(f32[512,128]{1,0:T(8,128)S(1)} %collective-permute-done.far_ref.rest_5_), channel_id=1, source_target_pairs={{0,32},{32,0},{64,96},{96,64},{128,160},{160,128},{192,224},{224,1... | collective-permute-start | bytes 786440 | tf_op jit(solution)/shard_map/ppermute | solution.py:362
  44.0 2.4 %collective-permute-start.7 = (f32[520,128]{1,0:T(8,128)S(1)}, f32[520,128]{1,0:T(8,128)S(1)}, u32[]{:S(2)}, u32[]{:S(2)}) collective-permute-start(f32[520,128]{1,0:T(8,128)S(1)} %last_gram.1.mine_ref), channel_id=1, source_target_pairs={{0,32},{32,0},{64,96},{96,64},{128,160},{160,128},{192,224},{224,1... | collective-permute-start | bytes 798728 | tf_op jit(solution)/shard_map/ppermute | solution.py:362
  46.4 1.9 %collective-permute-start.9 = (f32[1536,128]{1,0:T(8,128)}, f32[1536,128]{1,0:T(8,128)S(1)}, u32[]{:S(2)}, u32[]{:S(2)}) collective-permute-start(f32[1536,128]{1,0:T(8,128)} %collective-permute-done.1.far_ref.rest_4_), channel_id=1, source_target_pairs={{0,32},{32,0},{64,96},{96,64},{128,160},{160,128},{192,224},{224,1... | collective-permute-start | bytes 2359304 | tf_op jit(solution)/shard_map/ppermute | solution.py:362
  48.3 0.0 collective-permute-done.6.far_ref
  48.3 2.4 %collective-permute-start.8 = (f32[520,128]{1,0:T(8,128)S(1)}, f32[520,128]{1,0:T(8,128)S(1)}, u32[]{:S(2)}, u32[]{:S(2)}) collective-permute-start(f32[520,128]{1,0:T(8,128)S(1)} %collective-permute-done.6.far_ref), channel_id=1, source_target_pairs={{0,32},{32,0},{64,96},{96,64},{128,160},{160,128},{192,224},{224,1... | collective-permute-start | bytes 798728 | tf_op jit(solution)/shard_map/ppermute | solution.py:362
  50.7 0.1 slice_bitcast_fusion.5
  50.8 0.2 convert_reduce_fusion
  51.0 0.1 multiply_add_fusion
  51.1 0.3 convolution_bitcast_fusion
  51.4 0.0 collective-permute-done.7.next_ref
  51.4 0.5 collective-permute-done.8.next_far_ref
  51.9 9.5 %turn.1 = (f32[2,256,256]{2,1,0:T(8,128)S(1)}, f32[2,256,128]{2,1,0:T(8,128)S(1)}, f32[8,128]{1,0:T(8,128)S(1)}) custom-call(s32[2]{0:T(128)S(1)} %pad_add_fusion.place_ref, f32[520,128]{1,0:T(8,128)S(1)} %last_gram.1.mine_ref, f32[520,128]{1,0:T(8,128)S(1)} %collective-permute-done.6.far_ref, f32[520,128]{1,0:T(8,128)S(1)} %collective-permute-done.7.next_ref, ...), custom_call_target="tpu_custom_call" | custom-call | tf_op jit(solution)/shard_map/turn/pallas_call | solution.py:214
  61.3 3.3 %collective-permute-start.11 = (f32[8,128]{1,0:T(8,128)S(1)}, f32[8,128]{1,0:T(8,128)S(1)}, u32[]{:S(2)}, u32[]{:S(2)}) collective-permute-start(f32[8,128]{1,0:T(8,128)S(1)} %get-tuple-element.14.left_ref), channel_id=1, source_target_pairs={{0,64},{32,96},{64,0},{96,32},{128,192},{160,224},{192,128},{224,1... | collective-permute-start | bytes 12296 | tf_op jit(solution)/shard_map/ppermute | solution.py:362
  64.7 0.7 routed.1
  65.4 0.0 collective-permute-done.10.rest_7_.rest_2_
  65.4 1.5 %collective-permute-done.11.right_ref = f32[8,128]{1,0:T(8,128)S(1)} collective-permute-done((f32[8,128]{1,0:T(8,128)S(1)}, f32[8,128]{1,0:T(8,128)S(1)}, u32[]{:S(2)}, u32[]{:S(2)}) %collective-permute-start.11) | collective-permute-done | bytes 4128 | tf_op jit(solution)/shard_map/ppermute | solution.py:362
  66.9 0.0 collective-permute-done.9.rest_6_.rest_1_
  66.9 3.2 %collective-permute-start.12 = (f32[8,128]{1,0:T(8,128)S(1)}, f32[8,128]{1,0:T(8,128)S(1)}, u32[]{:S(2)}, u32[]{:S(2)}) collective-permute-start(f32[8,128]{1,0:T(8,128)S(1)} %sum_after.1.refs_1_), channel_id=1, source_target_pairs={{0,128},{32,160},{64,192},{96,224},{128,0},{160,32},{192,64},{224,... | collective-permute-start | bytes 12296 | tf_op jit(solution)/shard_map/ppermute | solution.py:362
  70.1 3.5 %placed.1.refs_0_ = f32[256,2048]{1,0:T(8,128)S(1)} custom-call(s32[2]{0:T(128)S(1)} %pad_add_fusion.place_ref, bf16[512,256]{1,0:T(8,128)(2,1)S(1)} %get-tuple-element.12.high_ref.rest_0_, bf16[512,256]{1,0:T(8,128)(2,1)S(1)} %get-tuple-element.13.low_ref, f32[4096,128]{1,0:T(8,128)S(1)} %bitcast.30, f32[1024,128]{1,0:T(8,128)} %collective-permute-done.2.rest_0_, ...), custom_call_target="tpu_custom_call" | custom-call | flops 1610612736 | bytes 4194304 | tf_op jit(solution)/shard_map/placed/pallas_call | solution.py:307
  73.7 0.0 collective-permute-done.12.refs_2_
  73.7 0.6 spread.1
  74.3 73.8 %all_to_all.5 = f32[64,16,4,128]{3,2,1,0:T(4,128)S(1)} all-to-all(f32[64,16,4,128]{3,2,1,0:T(4,128)S(1)} %spread.1), channel_id=1, replica_groups={{0,256,1,257,2,258,3,259,4,260,5,261,6,262,7,263,8,264,9,265,10,266,11,..., dimensions={0} | all-to-all | bytes 4194304 | tf_op jit(solution)/shard_map/all_to_all | solution.py:437
  148.0 1.5 %join.1 = f32[32,4,4096]{2,1,0:T(4,128)} custom-call(f32[32,32,4,128]{3,2,1,0:T(4,128)S(1)} %bitcast.31), custom_call_target="tpu_custom_call" | custom-call | tf_op jit(solution)/shard_map/join/pallas_call | solution.py:350
  (9 shorter events, 0.0 us)
Async XLA Ops:
  0.0 5.1 %copy-start = (f32[1,4096,128]{2,1,0:T(8,128)S(1)}, f32[1,4096,128]{2,1,0:T(8,128)}, u32[]{:S(2)}) copy-start(f32[1,4096,128]{2,1,0:T(8,128)} %param.3) | copy-start | bytes 6291460
  3.0 17.6 %copy-start.1 = (s32[1,64,1]{1,2,0:T(1,128)S(1)}, s32[1,64,1]{1,2,0:T(1,128)}, u32[]{:S(2)}) copy-start(s32[1,64,1]{1,2,0:T(1,128)} %param.5) | copy-start | bytes 772
  3.0 17.6 %copy-start.2 = (s32[1,64]{1,0:T(1,128)S(1)}, s32[1,64]{1,0:T(1,128)}, u32[]{:S(2)}) copy-start(s32[1,64]{1,0:T(1,128)} %param.4) | copy-start | bytes 772
  3.0 15.2 %collective-permute-start.5 = (f32[1024,128]{1,0:T(8,128)}, f32[1024,128]{1,0:T(8,128)S(1)}, u32[]{:S(2)}, u32[]{:S(2)}) collective-permute-start(f32[1024,128]{1,0:T(8,128)} %get-tuple-element.17), channel_id=1, source_target_pairs={{0,32},{32,0},{64,96},{96,64},{128,160},{160,128},{192,224},{224,1... | collective-permute-start | bytes 1572872 | tf_op jit(solution)/shard_map/ppermute | solution.py:362
  6.0 24.0 %collective-permute-start.1 = (f32[1536,128]{1,0:T(8,128)}, f32[1536,128]{1,0:T(8,128)}, u32[]{:S(2)}, u32[]{:S(2)}) collective-permute-start(f32[1536,128]{1,0:T(8,128)} %dynamic-slice_bitcast_fusion), channel_id=1, source_target_pairs={{0,256},{32,288},{64,320},{96,352},{128,384},{160,416},{192,448},{... | collective-permute-start | bytes 2359304 | tf_op jit(solution)/shard_map/ppermute | solution.py:362
  11.0 10.0 %collective-permute-start.3 = (f32[1024,128]{1,0:T(8,128)}, f32[1024,128]{1,0:T(8,128)S(1)}, u32[]{:S(2)}, u32[]{:S(2)}) collective-permute-start(f32[1024,128]{1,0:T(8,128)} %get-tuple-element.18), channel_id=1, source_target_pairs={{0,32},{32,0},{64,96},{96,64},{128,160},{160,128},{192,224},{224,1... | collective-permute-start | bytes 1572872 | tf_op jit(solution)/shard_map/ppermute | solution.py:362
  13.1 7.9 %collective-permute-start.2 = (f32[1024,128]{1,0:T(8,128)}, f32[1024,128]{1,0:T(8,128)}, u32[]{:S(2)}, u32[]{:S(2)}) collective-permute-start(f32[1024,128]{1,0:T(8,128)} %get-tuple-element.19), channel_id=1, source_target_pairs={{0,32},{32,0},{64,96},{96,64},{128,160},{160,128},{192,224},{224,1... | collective-permute-start | bytes 1572872 | tf_op jit(solution)/shard_map/ppermute | solution.py:362
  15.3 5.7 %collective-permute-start.4 = (f32[1024,128]{1,0:T(8,128)}, f32[1024,128]{1,0:T(8,128)}, u32[]{:S(2)}, u32[]{:S(2)}) collective-permute-start(f32[1024,128]{1,0:T(8,128)} %get-tuple-element.20), channel_id=1, source_target_pairs={{0,32},{32,0},{64,96},{96,64},{128,160},{160,128},{192,224},{224,1... | collective-permute-start | bytes 1572872 | tf_op jit(solution)/shard_map/ppermute | solution.py:362
  18.2 17.0 %collective-permute-start = (f32[512,128]{1,0:T(8,128)}, f32[512,128]{1,0:T(8,128)S(1)}, u32[]{:S(2)}, u32[]{:S(2)}) collective-permute-start(f32[512,128]{1,0:T(8,128)} %constant_dynamic-slice_fusion), channel_id=1, source_target_pairs={{0,256},{32,288},{64,320},{96,352},{128,384},{160,416},{192,448},{... | collective-permute-start | bytes 786440 | tf_op jit(solution)/shard_map/ppermute | solution.py:362
  36.7 11.6 %collective-permute-start.6 = (f32[520,128]{1,0:T(8,128)S(1)}, f32[520,128]{1,0:T(8,128)S(1)}, u32[]{:S(2)}, u32[]{:S(2)}) collective-permute-start(f32[520,128]{1,0:T(8,128)S(1)} %last_gram.1.mine_ref), channel_id=1, source_target_pairs={{0,256},{32,288},{64,320},{96,352},{128,384},{160,416},{192,448},{... | collective-permute-start | bytes 798728 | tf_op jit(solution)/shard_map/ppermute | solution.py:362
  42.0 23.3 %collective-permute-start.10 = (f32[512,128]{1,0:T(8,128)S(1)}, f32[512,128]{1,0:T(8,128)S(1)}, u32[]{:S(2)}, u32[]{:S(2)}) collective-permute-start(f32[512,128]{1,0:T(8,128)S(1)} %collective-permute-done.far_ref.rest_5_), channel_id=1, source_target_pairs={{0,32},{32,0},{64,96},{96,64},{128,160},{160,128},{192,224},{224,1... | collective-permute-start | bytes 786440 | tf_op jit(solution)/shard_map/ppermute | solution.py:362
  44.0 7.4 %collective-permute-start.7 = (f32[520,128]{1,0:T(8,128)S(1)}, f32[520,128]{1,0:T(8,128)S(1)}, u32[]{:S(2)}, u32[]{:S(2)}) collective-permute-start(f32[520,128]{1,0:T(8,128)S(1)} %last_gram.1.mine_ref), channel_id=1, source_target_pairs={{0,32},{32,0},{64,96},{96,64},{128,160},{160,128},{192,224},{224,1... | collective-permute-start | bytes 798728 | tf_op jit(solution)/shard_map/ppermute | solution.py:362
  46.4 20.5 %collective-permute-start.9 = (f32[1536,128]{1,0:T(8,128)}, f32[1536,128]{1,0:T(8,128)S(1)}, u32[]{:S(2)}, u32[]{:S(2)}) collective-permute-start(f32[1536,128]{1,0:T(8,128)} %collective-permute-done.1.far_ref.rest_4_), channel_id=1, source_target_pairs={{0,32},{32,0},{64,96},{96,64},{128,160},{160,128},{192,224},{224,1... | collective-permute-start | bytes 2359304 | tf_op jit(solution)/shard_map/ppermute | solution.py:362
  48.3 3.6 %collective-permute-start.8 = (f32[520,128]{1,0:T(8,128)S(1)}, f32[520,128]{1,0:T(8,128)S(1)}, u32[]{:S(2)}, u32[]{:S(2)}) collective-permute-start(f32[520,128]{1,0:T(8,128)S(1)} %collective-permute-done.6.far_ref), channel_id=1, source_target_pairs={{0,32},{32,0},{64,96},{96,64},{128,160},{160,128},{192,224},{224,1... | collective-permute-start | bytes 798728 | tf_op jit(solution)/shard_map/ppermute | solution.py:362
  61.3 5.5 %collective-permute-start.11 = (f32[8,128]{1,0:T(8,128)S(1)}, f32[8,128]{1,0:T(8,128)S(1)}, u32[]{:S(2)}, u32[]{:S(2)}) collective-permute-start(f32[8,128]{1,0:T(8,128)S(1)} %get-tuple-element.14.left_ref), channel_id=1, source_target_pairs={{0,64},{32,96},{64,0},{96,32},{128,192},{160,224},{192,128},{224,1... | collective-permute-start | bytes 12296 | tf_op jit(solution)/shard_map/ppermute | solution.py:362
  66.9 6.8 %collective-permute-start.12 = (f32[8,128]{1,0:T(8,128)S(1)}, f32[8,128]{1,0:T(8,128)S(1)}, u32[]{:S(2)}, u32[]{:S(2)}) collective-permute-start(f32[8,128]{1,0:T(8,128)S(1)} %sum_after.1.refs_1_), channel_id=1, source_target_pairs={{0,128},{32,160},{64,192},{96,224},{128,0},{160,32},{192,64},{224,... | collective-permute-start | bytes 12296 | tf_op jit(solution)/shard_map/ppermute | solution.py:362
